TPU v7x, 32 devices: a whole 2x2x4 slice. The times are simulated.
32 devices in a mesh: fsdp: 4 (over x, core), ctx: 8 (over z, y).
Axes of the slice: x: 2, y: 2, z: 4, core: 2. Of those that a mesh axis runs over, the one named last changes fastest.
Arguments:
- layer_input: bfloat16 [8192, 1024], P(('fsdp', 'ctx')), may hold values from -6 to 6
- positions: int32 [8192], P(('fsdp', 'ctx')), may hold values from 0 to 3070, as said below
- value_expert_routes: int32 [8192, 4, 2], P(('fsdp', 'ctx')), may hold values from 0 to 4, all different within a row
- output_expert_routes: int32 [8192, 4, 2], P(('fsdp', 'ctx')), may hold values from 0 to 4, all different within a row
- first_layernorm_gain: bfloat16 [1024], P('ctx'), may hold values from 0.25 to 1.75
- first_layernorm_bias: bfloat16 [1024], P('ctx'), may hold values from -4 to 4
- query_weight: bfloat16 [1024, 448], P('ctx'), may hold values from -0.1875 to 0.1875
- key_weight: bfloat16 [1024, 448], P('ctx'), may hold values from -0.1875 to 0.1875
- relative_weight: bfloat16 [1024, 448], P('ctx'), may hold values from -0.25 to 0.25
- content_query_bias: bfloat16 [4, 112], replicated, may hold values from -4 to 4
- position_query_bias: bfloat16 [4, 112], replicated, may hold values from -4 to 4
- value_select_weight: bfloat16 [1024, 20], P('ctx'), may hold values from -0.125 to 0.125
- value_expert_weight: bfloat16 [1024, 2240], P('ctx'), may hold values from -0.1875 to 0.1875
- output_select_weight: bfloat16 [1024, 20], P('ctx'), may hold values from -0.125 to 0.125
- output_expert_weight: bfloat16 [2240, 1024], P('ctx'), as said below
- second_layernorm_gain: bfloat16 [1024], P('ctx'), may hold values from 0.25 to 1.75
- second_layernorm_bias: bfloat16 [1024], P('ctx'), may hold values from -4 to 4
- feedforward_in_weight1: bfloat16 [1024, 4096], P('ctx'), may hold values from -0.1875 to 0.1875
- feedforward_in_bias1: bfloat16 [4096], P('ctx'), may hold values from -4 to 4
- feedforward_out_weight2: bfloat16 [4096, 1024], P('ctx'), may hold values from -0.125 to 0.125
- feedforward_out_bias2: bfloat16 [1024], P('ctx'), may hold values from -4 to 4
- cotangent: bfloat16 [8192, 1024], P(('fsdp', 'ctx')), may hold values from -6 to 6
Outputs:
- output: bfloat16 [8192, 1024], P(('fsdp', 'ctx'))
- d_input: float32 [8192, 1024], P(('fsdp', 'ctx'))
- grad_ln1_gain: float32 [1024], P('ctx')
- grad_ln1_bias: float32 [1024], P('ctx')
- grad_w_query: float32 [1024, 448], P('ctx')
- grad_w_key: float32 [1024, 448], P('ctx')
- grad_w_rel: float32 [1024, 448], P('ctx')
- grad_u_bias: float32 [4, 112], replicated
- grad_v_bias: float32 [4, 112], replicated
- grad_w_vsel: float32 [1024, 20], P('ctx')
- grad_w_value: float32 [1024, 2240], P('ctx')
- grad_w_osel: float32 [1024, 20], P('ctx')
- grad_w_out: float32 [2240, 1024], P('ctx')
- grad_ln2_gain: float32 [1024], P('ctx')
- grad_ln2_bias: float32 [1024], P('ctx')
- grad_w_ffn1: float32 [1024, 4096], P('ctx')
- grad_b_ffn1: float32 [4096], P('ctx')
- grad_w_ffn2: float32 [4096, 1024], P('ctx')
- grad_b_ffn2: float32 [1024], P('ctx')
Inputs may be any that keep to these rules, and one draw needn't show every extreme that they name: Within each sequence of 2048 tokens the positions start at 0 and rise by 1 or 2 from one token to the next, by 2 at exactly (2047) // 2 of the steps, so that every sequence ends at the largest value. `value_expert_routes`: in each token and head the 2 experts differ. `output_expert_routes`: in each token and head the 2 experts differ. `output_expert_weight`: entries of mean zero.
All inputs are finite; a program needn't handle non-finite values.
Results may differ from a plain program's by a relative error of at most 0.025.
Values may be sent and summed in bfloat16 or wider, within the bound.
A program may use at most 256 MiB of HBM per device.

v0:
```python
import math

import jax
import jax.numpy as jnp
from jax import lax
from jax.sharding import PartitionSpec as P

norm_eps = 1e-05
masked_score = -1e30


def layer_norm(values_in, gain, shift):
    center = jnp.mean(values_in, axis=-1, keepdims=True)
    offsets = values_in - center
    spread = jnp.mean(offsets * offsets, axis=-1, keepdims=True)
    return offsets * lax.rsqrt(spread + norm_eps) * gain + shift


def frequencies(model_width):
    return 1.0 / 10000.0 ** (jnp.arange(0, model_width, 2, dtype=jnp.float32) / model_width)


def routing_mask(routes, experts_total):
    labels = jnp.arange(experts_total, dtype=jnp.int32)
    return jnp.sum((routes[..., None] == labels).astype(jnp.float32), axis=-2)


def gelu_tanh(values_in):
    return jax.nn.gelu(values_in, approximate=True)


def key_features_of(places, freq_table):
    angle_rows = places.astype(jnp.float32)[:, None] * freq_table[None, :]
    return jnp.concatenate([jnp.cos(angle_rows), jnp.sin(angle_rows)], axis=-1).astype(jnp.bfloat16)


def on_device(
    layer_input,
    positions,
    value_expert_routes,
    output_expert_routes,
    first_layernorm_gain,
    first_layernorm_bias,
    query_weight,
    key_weight,
    relative_weight,
    content_query_bias,
    position_query_bias,
    value_select_weight,
    value_expert_weight,
    output_select_weight,
    output_expert_weight,
    second_layernorm_gain,
    second_layernorm_bias,
    feedforward_in_weight1,
    feedforward_in_bias1,
    feedforward_out_weight2,
    feedforward_out_bias2,
    cotangent,
):
    full_weights = (
        lax.all_gather(first_layernorm_gain, "ctx", axis=0, tiled=True),
        lax.all_gather(first_layernorm_bias, "ctx", axis=0, tiled=True),
        lax.all_gather(query_weight, "ctx", axis=0, tiled=True),
        lax.all_gather(key_weight, "ctx", axis=0, tiled=True),
        lax.all_gather(relative_weight, "ctx", axis=0, tiled=True),
        lax.all_gather(value_select_weight, "ctx", axis=0, tiled=True),
        lax.all_gather(value_expert_weight, "ctx", axis=0, tiled=True),
        lax.all_gather(output_select_weight, "ctx", axis=0, tiled=True),
        lax.all_gather(output_expert_weight, "ctx", axis=0, tiled=True),
        lax.all_gather(second_layernorm_gain, "ctx", axis=0, tiled=True),
        lax.all_gather(second_layernorm_bias, "ctx", axis=0, tiled=True),
        lax.all_gather(feedforward_in_weight1, "ctx", axis=0, tiled=True),
        lax.all_gather(feedforward_in_bias1, "ctx", axis=0, tiled=True),
        lax.all_gather(feedforward_out_weight2, "ctx", axis=0, tiled=True),
        lax.all_gather(feedforward_out_bias2, "ctx", axis=0, tiled=True),
    )
    (
        first_norm_gain,
        first_norm_shift,
        query_matrix,
        key_matrix,
        relative_matrix,
        value_select_matrix,
        value_matrix,
        output_select_matrix,
        output_matrix,
        second_norm_gain,
        second_norm_shift,
        feedforward_in_matrix,
        feedforward_in_bias,
        feedforward_out_matrix,
        feedforward_out_bias,
    ) = full_weights
    tok_rows, model_width = layer_input.shape
    heads_total, head_size = content_query_bias.shape
    experts_total = value_select_matrix.shape[1] // heads_total
    joint_width = heads_total * head_size
    half_width = model_width // 2
    score_scale = 1.0 / math.sqrt(head_size)
    seq_rows = lax.axis_size("ctx") * tok_rows
    first_row = lax.axis_index("ctx") * tok_rows
    query_rows = first_row + jnp.arange(tok_rows, dtype=jnp.int32)
    last_row = first_row + tok_rows - 1
    single_float = jnp.float32
    bf16 = jnp.bfloat16
    hidden_f = layer_input.astype(single_float)
    normed_one, norm_one_back = jax.vjp(
        layer_norm,
        hidden_f,
        first_norm_gain.astype(single_float),
        first_norm_shift.astype(single_float),
    )
    normalized_reduced = normed_one.astype(bf16)
    query_full = jnp.dot(
        normalized_reduced, query_matrix, preferred_element_type=single_float
    ).reshape(tok_rows, heads_total, head_size)
    q_content = ((query_full + content_query_bias.astype(single_float)) * score_scale).astype(bf16)
    q_position = (query_full + position_query_bias.astype(single_float)).astype(bf16)
    rel_heads = relative_matrix.reshape(model_width, heads_total, head_size)
    rel_query = jnp.einsum(
        "thc,dhc->thd", q_position, rel_heads, preferred_element_type=single_float
    )
    freq_table = frequencies(model_width)
    angle_rows = positions.astype(single_float)[:, None] * freq_table[None, :]
    query_sin = jnp.sin(angle_rows)[:, None, :]
    query_cos = jnp.cos(angle_rows)[:, None, :]
    part_sin = rel_query[..., :half_width]
    part_cos = rel_query[..., half_width:]
    g_position = (
        jnp.concatenate(
            [
                part_sin * query_sin + part_cos * query_cos,
                part_cos * query_sin - part_sin * query_cos,
            ],
            axis=-1,
        )
        * score_scale
    ).astype(bf16)
    keys_low = jnp.dot(normalized_reduced, key_matrix, preferred_element_type=single_float).astype(
        bf16
    )
    value_select_sigmoid = jax.nn.sigmoid(
        jnp.dot(normalized_reduced, value_select_matrix, preferred_element_type=single_float)
    ).reshape(tok_rows, heads_total, experts_total)
    value_select_mask = routing_mask(value_expert_routes, experts_total)
    value_expert_gate = value_select_sigmoid * value_select_mask
    expert_vals = jnp.dot(
        normalized_reduced, value_matrix, preferred_element_type=single_float
    ).reshape(tok_rows, heads_total, experts_total, head_size)
    values_low = (
        jnp.sum(value_expert_gate[..., None] * expert_vals, axis=2)
        .reshape(tok_rows, joint_width)
        .astype(bf16)
    )
    all_places = lax.all_gather(positions, "ctx", axis=0, tiled=True)

    def block_scores(key_blk, place_blk, block_start):
        key_count = key_blk.shape[0]
        key_heads = key_blk.reshape(key_count, heads_total, head_size)
        features = key_features_of(place_blk, freq_table)
        scores = jnp.einsum(
            "thc,khc->htk", q_content, key_heads, preferred_element_type=single_float
        )
        scores = scores + jnp.einsum(
            "thd,kd->htk", g_position, features, preferred_element_type=single_float
        )
        allowed = (block_start + jnp.arange(key_count, dtype=jnp.int32))[None, :] <= query_rows[
            :, None
        ]
        return (jnp.where(allowed[None], scores, masked_score), allowed, key_heads, features)

    def over_blocks(carried, piece, step_fn):
        key_piece, val_piece = piece
        piece_rows = key_piece.shape[0]
        block_rows = math.gcd(piece_rows, 1024)

        def one_block(running, block_number):
            offset = block_number * block_rows
            key_blk = lax.dynamic_slice_in_dim(key_piece, offset, block_rows, 0)
            val_blk = lax.dynamic_slice_in_dim(val_piece, offset, block_rows, 0)
            place_blk = lax.dynamic_slice_in_dim(all_places, offset, block_rows, 0)
            running = lax.cond(
                offset <= last_row,
                lambda current: step_fn(current, key_blk, val_blk, place_blk, offset),
                lambda current: current,
                running,
            )
            return (running, None)

        carried, unused = lax.scan(
            one_block, carried, jnp.arange(piece_rows // block_rows, dtype=jnp.int32)
        )
        return carried

    def forward_step(running, key_blk, val_blk, place_blk, block_start):
        best_now, totals, accum = running
        scores, allowed, key_heads, features = block_scores(key_blk, place_blk, block_start)
        best_new = jnp.maximum(best_now, jnp.max(scores, axis=-1))
        rescale = jnp.exp(best_now - best_new)
        weights = jnp.where(allowed[None], jnp.exp(scores - best_new[..., None]), 0.0)
        totals = totals * rescale + jnp.sum(weights, axis=-1)
        val_heads = val_blk.reshape(key_blk.shape[0], heads_total, head_size)
        accum = accum * rescale.T[..., None] + jnp.einsum(
            "htk,khc->thc", weights.astype(bf16), val_heads, preferred_element_type=single_float
        )
        return (best_new, totals, accum)

    start_state = (
        jnp.full((heads_total, tok_rows), masked_score, single_float),
        jnp.zeros((heads_total, tok_rows), single_float),
        jnp.zeros((tok_rows, heads_total, head_size), single_float),
    )
    best_all, totals, accum = over_blocks(
        start_state,
        (
            lax.all_gather(keys_low, "ctx", axis=0, tiled=True),
            lax.all_gather(values_low, "ctx", axis=0, tiled=True),
        ),
        forward_step,
    )
    attn_o = accum / totals.T[..., None]
    log_sum = best_all + jnp.log(totals)
    osel_sig = jax.nn.sigmoid(
        jnp.dot(normalized_reduced, output_select_matrix, preferred_element_type=single_float)
    ).reshape(tok_rows, heads_total, experts_total)
    osel_mask = routing_mask(output_expert_routes, experts_total)
    out_gate = osel_sig * osel_mask
    mixed_low = (
        (out_gate[..., None] * attn_o[:, :, None, :])
        .reshape(tok_rows, heads_total * experts_total * head_size)
        .astype(bf16)
    )
    attn_out = jnp.dot(mixed_low, output_matrix, preferred_element_type=single_float)
    middle = hidden_f + attn_out
    normed_two, norm_two_back = jax.vjp(
        layer_norm,
        middle,
        second_norm_gain.astype(single_float),
        second_norm_shift.astype(single_float),
    )
    normed_two_low = normed_two.astype(bf16)
    pre_act = jnp.dot(
        normed_two_low, feedforward_in_matrix, preferred_element_type=single_float
    ) + feedforward_in_bias.astype(single_float)
    act_vals, gelu_back = jax.vjp(gelu_tanh, pre_act)
    act_low = act_vals.astype(bf16)
    ffn_result = jnp.dot(
        act_low, feedforward_out_matrix, preferred_element_type=single_float
    ) + feedforward_out_bias.astype(single_float)
    output = (middle + ffn_result).astype(bf16)
    grad_ffn_out = jnp.einsum("tf,td->fd", act_low, cotangent, preferred_element_type=single_float)
    grad_ffn_out_bias = jnp.sum(cotangent.astype(single_float), axis=0)
    d_act = jnp.einsum(
        "td,fd->tf", cotangent, feedforward_out_matrix, preferred_element_type=single_float
    )
    d_pre_low = gelu_back(d_act)[0].astype(bf16)
    grad_ffn_in = jnp.einsum(
        "td,tf->df", normed_two_low, d_pre_low, preferred_element_type=single_float
    )
    grad_ffn_in_bias = jnp.sum(d_pre_low.astype(single_float), axis=0)
    d_norm_two = jnp.einsum(
        "tf,df->td", d_pre_low, feedforward_in_matrix, preferred_element_type=single_float
    )
    d_mid_part, grad_gain_two, grad_shift_two = norm_two_back(d_norm_two)
    d_middle = cotangent.astype(single_float) + d_mid_part
    d_mid_low = d_middle.astype(bf16)
    grad_out = jnp.einsum("tk,td->kd", mixed_low, d_mid_low, preferred_element_type=single_float)
    d_mixed = jnp.einsum(
        "td,kd->tk", d_mid_low, output_matrix, preferred_element_type=single_float
    ).reshape(tok_rows, heads_total, experts_total, head_size)
    d_attn_low = jnp.sum(out_gate[..., None] * d_mixed, axis=2).astype(bf16)
    d_out_gate = jnp.sum(attn_o[:, :, None, :] * d_mixed, axis=-1)
    d_osel_low = (
        (d_out_gate * osel_mask * osel_sig * (1.0 - osel_sig))
        .reshape(tok_rows, heads_total * experts_total)
        .astype(bf16)
    )
    grad_osel = jnp.einsum(
        "ni,np->ip", normalized_reduced, d_osel_low, preferred_element_type=single_float
    )
    delta_rows = jnp.sum(d_attn_low.astype(single_float) * attn_o, axis=-1).T

    def block_grads(key_blk, val_blk, place_blk, block_start):
        key_count = key_blk.shape[0]
        scores, allowed, key_heads, features = block_scores(key_blk, place_blk, block_start)
        probs = jnp.where(allowed[None], jnp.exp(scores - log_sum[..., None]), 0.0)
        val_heads = val_blk.reshape(key_count, heads_total, head_size)
        d_probs = jnp.einsum(
            "thc,khc->htk", d_attn_low, val_heads, preferred_element_type=single_float
        )
        d_scores = (probs * (d_probs - delta_rows[..., None])).astype(bf16)
        return (probs, d_scores, key_heads, features)

    def key_side(probs, d_scores):
        key_count = probs.shape[-1]
        d_vals = jnp.einsum(
            "htk,thc->khc", probs.astype(bf16), d_attn_low, preferred_element_type=single_float
        )
        d_keys = jnp.einsum(
            "htk,thc->khc", d_scores, q_content, preferred_element_type=single_float
        )
        return jnp.concatenate(
            [d_keys.reshape(key_count, joint_width), d_vals.reshape(key_count, joint_width)],
            axis=-1,
        )

    def query_side(d_content, d_position, d_scores, key_heads, features):
        d_content = d_content + jnp.einsum(
            "htk,khc->thc", d_scores, key_heads, preferred_element_type=single_float
        )
        d_position = d_position + jnp.einsum(
            "htk,kd->thd", d_scores, features, preferred_element_type=single_float
        )
        return (d_content, d_position)

    query_state = (
        jnp.zeros((tok_rows, heads_total, head_size), single_float),
        jnp.zeros((tok_rows, heads_total, model_width), single_float),
    )

    def backward_step(running, key_blk, val_blk, place_blk, block_start):
        d_content, d_position, key_grads = running
        probs, d_scores, key_heads, features = block_grads(key_blk, val_blk, place_blk, block_start)
        d_content, d_position = query_side(d_content, d_position, d_scores, key_heads, features)
        block_grad = key_side(probs, d_scores)
        current = lax.dynamic_slice_in_dim(key_grads, block_start, key_blk.shape[0], 0)
        key_grads = lax.dynamic_update_slice_in_dim(key_grads, current + block_grad, block_start, 0)
        return (d_content, d_position, key_grads)

    back_state = (
        query_state[0],
        query_state[1],
        jnp.zeros((seq_rows, 2 * joint_width), single_float),
    )
    d_content, d_position, key_grads = over_blocks(
        back_state,
        (
            lax.all_gather(keys_low, "ctx", axis=0, tiled=True),
            lax.all_gather(values_low, "ctx", axis=0, tiled=True),
        ),
        backward_step,
    )
    own_grads = lax.psum_scatter(key_grads, "ctx", scatter_dimension=0, tiled=True)
    d_keys_own = own_grads[:, :joint_width]
    d_vals_own = own_grads[:, joint_width:].reshape(tok_rows, heads_total, head_size)
    grad_sin = d_position[..., :half_width]
    grad_cos = d_position[..., half_width:]
    d_rel_low = (
        jnp.concatenate(
            [
                grad_sin * query_sin - grad_cos * query_cos,
                grad_sin * query_cos + grad_cos * query_sin,
            ],
            axis=-1,
        )
        * score_scale
    ).astype(bf16)
    grad_rel = jnp.einsum(
        "thd,thc->dhc", d_rel_low, q_position, preferred_element_type=single_float
    ).reshape(model_width, joint_width)
    d_qpos = jnp.einsum("thd,dhc->thc", d_rel_low, rel_heads, preferred_element_type=single_float)
    d_scaled = d_content * score_scale
    grad_ubias = jnp.sum(d_scaled, axis=0)
    grad_vbias = jnp.sum(d_qpos, axis=0)
    d_query_low = (d_scaled + d_qpos).reshape(tok_rows, joint_width).astype(bf16)
    d_keys_low = d_keys_own.astype(bf16)
    d_expert_low = (
        (value_expert_gate[..., None] * d_vals_own[:, :, None, :])
        .reshape(tok_rows, heads_total * experts_total * head_size)
        .astype(bf16)
    )
    value_gate_grad = jnp.sum(expert_vals * d_vals_own[:, :, None, :], axis=-1)
    value_select_grad_low = (
        (value_gate_grad * value_select_mask * value_select_sigmoid * (1.0 - value_select_sigmoid))
        .reshape(tok_rows, heads_total * experts_total)
        .astype(bf16)
    )
    grad_query = jnp.einsum(
        "ni,np->ip", normalized_reduced, d_query_low, preferred_element_type=single_float
    )
    grad_key = jnp.einsum(
        "ni,np->ip", normalized_reduced, d_keys_low, preferred_element_type=single_float
    )
    grad_value = jnp.einsum(
        "ni,np->ip", normalized_reduced, d_expert_low, preferred_element_type=single_float
    )
    value_select_gradient = jnp.einsum(
        "ni,np->ip", normalized_reduced, value_select_grad_low, preferred_element_type=single_float
    )
    d_norm_one = jnp.einsum(
        "ai,zi->az", d_query_low, query_matrix, preferred_element_type=single_float
    )
    d_norm_one = d_norm_one + jnp.einsum(
        "ai,zi->az", d_keys_low, key_matrix, preferred_element_type=single_float
    )
    d_norm_one = d_norm_one + jnp.einsum(
        "ai,zi->az", d_expert_low, value_matrix, preferred_element_type=single_float
    )
    d_norm_one = d_norm_one + jnp.einsum(
        "ai,zi->az", value_select_grad_low, value_select_matrix, preferred_element_type=single_float
    )
    d_norm_one = d_norm_one + jnp.einsum(
        "ai,zi->az", d_osel_low, output_select_matrix, preferred_element_type=single_float
    )
    d_in_part, grad_gain_one, grad_shift_one = norm_one_back(d_norm_one)
    d_input = d_middle + d_in_part
    seq_owned = (
        lax.psum_scatter(grad_gain_one, "ctx", scatter_dimension=0, tiled=True),
        lax.psum_scatter(grad_shift_one, "ctx", scatter_dimension=0, tiled=True),
        lax.psum_scatter(grad_query, "ctx", scatter_dimension=0, tiled=True),
        lax.psum_scatter(grad_key, "ctx", scatter_dimension=0, tiled=True),
        lax.psum_scatter(grad_rel, "ctx", scatter_dimension=0, tiled=True),
        lax.psum_scatter(value_select_gradient, "ctx", scatter_dimension=0, tiled=True),
        lax.psum_scatter(grad_value, "ctx", scatter_dimension=0, tiled=True),
        lax.psum_scatter(grad_osel, "ctx", scatter_dimension=0, tiled=True),
        lax.psum_scatter(grad_out, "ctx", scatter_dimension=0, tiled=True),
        lax.psum_scatter(grad_gain_two, "ctx", scatter_dimension=0, tiled=True),
        lax.psum_scatter(grad_shift_two, "ctx", scatter_dimension=0, tiled=True),
        lax.psum_scatter(grad_ffn_in, "ctx", scatter_dimension=0, tiled=True),
        lax.psum_scatter(grad_ffn_in_bias, "ctx", scatter_dimension=0, tiled=True),
        lax.psum_scatter(grad_ffn_out, "ctx", scatter_dimension=0, tiled=True),
        lax.psum_scatter(grad_ffn_out_bias, "ctx", scatter_dimension=0, tiled=True),
    )
    owned = (
        lax.psum(seq_owned[0].astype(jnp.bfloat16), "fsdp").astype(jnp.float32),
        lax.psum(seq_owned[1].astype(jnp.bfloat16), "fsdp").astype(jnp.float32),
        lax.psum(seq_owned[2].astype(jnp.bfloat16), "fsdp").astype(jnp.float32),
        lax.psum(seq_owned[3].astype(jnp.bfloat16), "fsdp").astype(jnp.float32),
        lax.psum(seq_owned[4].astype(jnp.bfloat16), "fsdp").astype(jnp.float32),
        lax.psum(seq_owned[5].astype(jnp.bfloat16), "fsdp").astype(jnp.float32),
        lax.psum(seq_owned[6].astype(jnp.bfloat16), "fsdp").astype(jnp.float32),
        lax.psum(seq_owned[7].astype(jnp.bfloat16), "fsdp").astype(jnp.float32),
        lax.psum(seq_owned[8].astype(jnp.bfloat16), "fsdp").astype(jnp.float32),
        lax.psum(seq_owned[9].astype(jnp.bfloat16), "fsdp").astype(jnp.float32),
        lax.psum(seq_owned[10].astype(jnp.bfloat16), "fsdp").astype(jnp.float32),
        lax.psum(seq_owned[11].astype(jnp.bfloat16), "fsdp").astype(jnp.float32),
        lax.psum(seq_owned[12].astype(jnp.bfloat16), "fsdp").astype(jnp.float32),
        lax.psum(seq_owned[13].astype(jnp.bfloat16), "fsdp").astype(jnp.float32),
        lax.psum(seq_owned[14].astype(jnp.bfloat16), "fsdp").astype(jnp.float32),
    )
    bias_sums = lax.psum((grad_ubias, grad_vbias), ("fsdp", "ctx"))
    return (
        output,
        d_input,
        owned[0],
        owned[1],
        owned[2],
        owned[3],
        owned[4],
        bias_sums[0],
        bias_sums[1],
        owned[5],
        owned[6],
        owned[7],
        owned[8],
        owned[9],
        owned[10],
        owned[11],
        owned[12],
        owned[13],
        owned[14],
    )


def solution(mesh):
    in_specs = (
        P(("fsdp", "ctx"), None),
        P(("fsdp", "ctx")),
        P(("fsdp", "ctx"), None, None),
        P(("fsdp", "ctx"), None, None),
        P("ctx"),
        P("ctx"),
        P("ctx", None),
        P("ctx", None),
        P("ctx", None),
        P(),
        P(),
        P("ctx", None),
        P("ctx", None),
        P("ctx", None),
        P("ctx", None),
        P("ctx"),
        P("ctx"),
        P("ctx", None),
        P("ctx"),
        P("ctx", None),
        P("ctx"),
        P(("fsdp", "ctx"), None),
    )
    out_specs = (
        P(("fsdp", "ctx"), None),
        P(("fsdp", "ctx"), None),
        P("ctx"),
        P("ctx"),
        P("ctx", None),
        P("ctx", None),
        P("ctx", None),
        P(),
        P(),
        P("ctx", None),
        P("ctx", None),
        P("ctx", None),
        P("ctx", None),
        P("ctx"),
        P("ctx"),
        P("ctx", None),
        P("ctx"),
        P("ctx", None),
        P("ctx"),
    )
    return jax.shard_map(
        on_device, mesh=mesh, in_specs=in_specs, out_specs=out_specs, check_vma=False
    )
```

profile of v0, /device:TPU:15, one launch (start us, length us, event | category | flops | bytes accessed | tf_op | source)
XLA Modules:
  0.0 2129.0 jit_solution(9459317577461123192)
XLA Ops:
  40.7 39.9 %all_gather.59 = bf16[1024,448]{0,1:T(8,128)(2,1)S(1)} all-gather(bf16[128,448]{0,1:T(8,128)(2,1)} %param.37), channel_id=1, replica_groups=mesh['fsdp'=4,'ctx'=8] {'ctx'}, dimensions={0}, use_global_device_ids=true | all-gather | bytes 1032192 | tf_op jit(solution)/shard_map/all_gather | solution.py:65
  82.9 24.4 %all_gather.64 = bf16[1024,20]{0,1:T(8,128)(2,1)S(1)} all-gather(bf16[128,20]{0,1:T(8,128)(2,1)S(1)} %copy-done.83), channel_id=1, replica_groups=mesh['fsdp'=4,'ctx'=8] {'ctx'}, dimensions={0}, use_global_device_ids=true | all-gather | bytes 46080 | tf_op jit(solution)/shard_map/all_gather | solution.py:67
  143.6 19.7 all-gather.5
  163.3 21.8 %all_gather.58 = bf16[1024,20]{0,1:T(8,128)(2,1)S(1)} all-gather(bf16[128,20]{0,1:T(8,128)(2,1)S(1)} %copy-done.84), channel_id=1, replica_groups=mesh['fsdp'=4,'ctx'=8] {'ctx'}, dimensions={0}, use_global_device_ids=true | all-gather | bytes 46080 | tf_op jit(solution)/shard_map/all_gather | solution.py:69
  204.3 30.5 %all_gather.61 = bf16[1024,448]{0,1:T(8,128)(2,1)S(1)} all-gather(bf16[128,448]{0,1:T(8,128)(2,1)S(1)} %copy-done.62), channel_id=1, replica_groups=mesh['fsdp'=4,'ctx'=8] {'ctx'}, dimensions={0}, use_global_device_ids=true | all-gather | bytes 1032192 | tf_op jit(solution)/shard_map/all_gather | solution.py:64
  235.3 44.4 %all_gather.63 = bf16[1024,448]{0,1:T(8,128)(2,1)S(1)} all-gather(bf16[128,448]{0,1:T(8,128)(2,1)S(1)} %copy-done.63), channel_id=1, replica_groups=mesh['fsdp'=4,'ctx'=8] {'ctx'}, dimensions={0}, use_global_device_ids=true | all-gather | bytes 1032192 | tf_op jit(solution)/shard_map/all_gather | solution.py:66
  282.3 18.8 while.30
  309.1 118.6 %all-gather.24.cloned.1.call-done = bf16[4096,1024]{1,0:T(8,128)(2,1)} async-done(((bf16[512,1024]{1,0:T(8,128)(2,1)}), bf16[4096,1024]{1,0:T(8,128)(2,1)}) %all-gather.24.cloned.1.call-update) | async-done | bytes 8388624 | tf_op jit(solution)/shard_map/all_gather | solution.py:75
  435.5 117.4 %all-gather.22.cloned.1.call-done = bf16[1024,4096]{1,0:T(8,128)(2,1)} async-done(((bf16[128,4096]{1,0:T(8,128)(2,1)}), bf16[1024,4096]{1,0:T(8,128)(2,1)}) %all-gather.22.cloned.1.call-update) | async-done | bytes 8388624 | tf_op jit(solution)/shard_map/all_gather | solution.py:73
  578.9 46.5 %while.31 = (s32[]{:T(128)}, f32[256,4,112]{0,2,1:T(8,128)S(1)}, f32[256,4,1024]{0,2,1:T(8,128)}, f32[2048,896]{0,1:T(8,128)}, s32[2]{0:T(128)S(1)}, /*index=5*/...) while((s32[]{:T(128)}, f32[256,4,112]{0,2,1:T(8,128)S(1)}, ...), condition=%wide.region_20.21_spmd.clone, body=%wide.region_17.0_spmd.clone.sunk | while | flops 5490985984 | bytes 140943952 | solution.py:191
  580.3 43.8 %conditional.7 = ((f32[256,4,112]{0,2,1:T(8,128)S(1)}, f32[256,4,1024]{0,2,1:T(8,128)}, f32[2048,896]{0,1:T(8,128)})) conditional(s32[]{:T(128)} %convert_element_type.417, (f32[256,4,112]{0,2,1:T(8,128)S(1)}, f32[256,4,1024]{0,2,1:T(8,128)}, f32[2048,896]{0,1:T(8,128)}) %tuple.123, (s32[]{:T(128)}, s32[]{:T(128)}, ...), branch_computations={%region_18.18_spmd, %region_19.19_spmd.clone} | conditional | flops 5490985984 | bytes 140940512 | solution.py:183
  606.1 18.0 dynamic_update_slice.6
  647.6 154.1 %reduce-scatter.11.cloned.1.call-done = f32[256,896]{0,1:T(8,128)} async-done(((f32[2048,896]{0,1:T(8,128)}), f32[256,896]{0,1:T(8,128)}) %reduce-scatter.11.cloned.1.call-update) | async-done | bytes 917520 | tf_op jit(solution)/shard_map/reduce_scatter | solution.py:344
  853.9 48.1 %all-reduce.6 = (f32[4,112]{1,0:T(4,128)}, f32[4,112]{1,0:T(4,128)}) all-reduce(f32[4,112]{1,0:T(4,128)S(1)} %copy-done.88, f32[4,112]{1,0:T(4,128)S(1)} %get-tuple-element.733), channel_id=1, replica_groups=mesh['fsdp'=4,'ctx'=8] {'fsdp','ctx'}, use_global_device_ids=true, to_apply=%region_39.40 | all-reduce | flops 896 | bytes 7168 | tf_op jit(solution)/shard_map/psum | solution.py:442
  912.5 19.0 reduce-scatter.17.cloned.1.call-done
  933.2 68.2 %reduce-scatter.13.cloned.1.call-done = f32[128,448]{0,1:T(8,128)} async-done(((f32[1024,448]{0,1:T(8,128)}), f32[128,448]{0,1:T(8,128)}) %reduce-scatter.13.cloned.1.call-update) | async-done | bytes 229392 | tf_op jit(solution)/shard_map/reduce_scatter | solution.py:411
  1008.6 62.1 %reduce-scatter.15.cloned.1.call-done = f32[128,448]{0,1:T(8,128)} async-done(((f32[1024,448]{0,1:T(8,128)}), f32[128,448]{0,1:T(8,128)}) %reduce-scatter.15.cloned.1.call-update) | async-done | bytes 229392 | tf_op jit(solution)/shard_map/reduce_scatter | solution.py:412
  1072.2 161.2 %reduce-scatter.25.cloned.1.call-done = f32[280,1024]{1,0:T(8,128)} async-done(((f32[2240,1024]{1,0:T(8,128)}), f32[280,1024]{1,0:T(8,128)}) %reduce-scatter.25.cloned.1.call-update) | async-done | bytes 1146896 | tf_op jit(solution)/shard_map/reduce_scatter | solution.py:417
  1235.7 160.7 %reduce-scatter.21.cloned.1.call-done = f32[128,2240]{0,1:T(8,128)} async-done(((f32[1024,2240]{0,1:T(8,128)}), f32[128,2240]{0,1:T(8,128)}) %reduce-scatter.21.cloned.1.call-update) | async-done | bytes 1146896 | tf_op jit(solution)/shard_map/reduce_scatter | solution.py:415
  1398.5 283.4 %reduce-scatter.29.cloned.1.call-done = f32[512,1024]{1,0:T(8,128)} async-done(((f32[4096,1024]{1,0:T(8,128)}), f32[512,1024]{1,0:T(8,128)}) %reduce-scatter.29.cloned.1.call-update) | async-done | bytes 2097168 | tf_op jit(solution)/shard_map/reduce_scatter | solution.py:422
  1684.6 282.7 %reduce-scatter.27.cloned.1.call-done = f32[128,4096]{1,0:T(8,128)} async-done(((f32[1024,4096]{1,0:T(8,128)}), f32[128,4096]{1,0:T(8,128)}) %reduce-scatter.27.cloned.1.call-update) | async-done | bytes 2097168 | tf_op jit(solution)/shard_map/reduce_scatter | solution.py:420
  1975.0 25.2 %all-reduce.7 = (bf16[1024]{0:T(1024)(128)(2,1)S(1)}, bf16[1024]{0:T(1024)(128)(2,1)S(1)}, bf16[1024]{0:T(1024)(128)(2,1)S(1)}, bf16[1024]{0:T(1024)(128)(2,1)S(...) all-reduce(f32[1024]{0:T(1024)S(1)} %get-tuple-element.625, ...), channel_id=3, replica_groups=mesh['fsdp'=4,'ctx'=8] {'ctx'}, use_global_device_ids=true, to_apply=%region_27.28.clone | all-reduce | flops 9216 | bytes 55296
  2000.7 26.5 %reduce-scatter.19.cloned.1.call-done = f32[128,20]{0,1:T(8,128)} async-done(((f32[1024,20]{0,1:T(8,128)}), f32[128,20]{0,1:T(8,128)}) %reduce-scatter.19.cloned.1.call-update) | async-done | bytes 10256 | tf_op jit(solution)/shard_map/reduce_scatter | solution.py:414
  2043.2 66.4 %all-reduce.12.cloned.1.call-done = (bf16[128,448]{0,1:T(8,128)(2,1)}, bf16[128,448]{0,1:T(8,128)(2,1)}, bf16[128,448]{0,1:T(8,128)(2,1)}, bf16[128,2240]{0,1:T(...) async-done(((bf16[128,448]{0,1:T(8,128)(2,1)}, bf16[128,448]{0,1:T(8,128)(2,1)}, bf16[128,448]{0,1:T(8,128)(2,1)}, ...) | async-done | bytes 3588112 | tf_op jit(solution)/shard_map/psum | solution.py:428
  (418 shorter events, 332.3 us)
Async XLA Ops:
  7.2 102.2 %all-gather.16.cloned.1.call-start = ((), (), s32[]{:S(2)}) async-start(), calls=%async_computation.11 | async-start | bytes 5160960 | tf_op jit(solution)/shard_map/all_gather | solution.py:68
  7.9 274.3 %all-gather.14.cloned.1.call-start = ((), (), s32[]{:S(2)}) async-start(), calls=%async_computation.10 | async-start | bytes 2064384 | tf_op jit(solution)/shard_map/all_gather | solution.py:217
  82.8 199.4 %all-gather.18.cloned.1.call-start = ((), (), s32[]{:S(2)}) async-start(), calls=%async_computation.12 | async-start | bytes 2064384 | tf_op jit(solution)/shard_map/all_gather | solution.py:218
  115.5 189.4 %all-gather.20.cloned.1.call-start = ((), (), s32[]{:S(2)}) async-start(), calls=%async_computation.13 | async-start | bytes 5160960 | tf_op jit(solution)/shard_map/all_gather | solution.py:70
  116.0 311.7 %all-gather.24.cloned.1.call-start = ((), (), s32[]{:S(2)}) async-start(), calls=%async_computation.15 | async-start | bytes 9437184 | tf_op jit(solution)/shard_map/all_gather | solution.py:75
  116.6 436.2 %all-gather.22.cloned.1.call-start = ((), (), s32[]{:S(2)}) async-start(), calls=%async_computation.14 | async-start | bytes 9437184 | tf_op jit(solution)/shard_map/all_gather | solution.py:73
  117.2 684.5 %reduce-scatter.11.cloned.1.call-start = ((), (), s32[]{:S(2)}) async-start(), calls=%async_computation.16 | async-start | bytes 8257536 | tf_op jit(solution)/shard_map/reduce_scatter | solution.py:344
  130.4 438.6 %copy-start.49 = (f32[8,1,128]{2,1,0:T(1,128)}, f32[8,1,128]{2,1,0:T(1,128)S(1)}, u32[]{:S(2)}) copy-start(f32[8,1,128]{2,1,0:T(1,128)S(1)} %convert_element_type.316) | copy-start | bytes 12292
  143.6 409.3 %copy-start.55 = (f32[8,1,128]{2,1,0:T(1,128)}, f32[8,1,128]{2,1,0:T(1,128)S(1)}, u32[]{:S(2)}) copy-start(f32[8,1,128]{2,1,0:T(1,128)S(1)} %convert_element_type.317) | copy-start | bytes 12292
  308.8 260.2 %copy-start.7 = (f32[256,1024]{1,0:T(8,128)}, f32[256,1024]{1,0:T(8,128)S(1)}, u32[]{:S(2)}) copy-start(f32[256,1024]{1,0:T(8,128)S(1)} %get-tuple-element.741) | copy-start | bytes 3145732
  308.8 260.2 %copy-start.68 = (f32[256]{0:T(256)}, f32[256]{0:T(256)S(1)}, u32[]{:S(2)}) copy-start(f32[256]{0:T(256)S(1)} %broadcast_multiply_fusion) | copy-start | bytes 3076
  309.1 259.9 %copy-start.70 = (f32[256]{0:T(256)}, f32[256]{0:T(256)S(1)}, u32[]{:S(2)}) copy-start(f32[256]{0:T(256)S(1)} %fusion.78) | copy-start | bytes 3076
  625.4 286.4 %reduce-scatter.23.cloned.1.call-start = ((), (), s32[]{:S(2)}) async-start(), calls=%async_computation.22 | async-start | bytes 110592 | tf_op jit(solution)/shard_map/reduce_scatter | solution.py:416
  637.7 293.8 %reduce-scatter.17.cloned.1.call-start = ((), (), s32[]{:S(2)}) async-start(), calls=%async_computation.19 | async-start | bytes 2064384 | tf_op jit(solution)/shard_map/reduce_scatter | solution.py:413
  642.1 359.2 %reduce-scatter.13.cloned.1.call-start = ((), (), s32[]{:S(2)}) async-start(), calls=%async_computation.17 | async-start | bytes 2064384 | tf_op jit(solution)/shard_map/reduce_scatter | solution.py:411
  647.6 423.1 %reduce-scatter.15.cloned.1.call-start = ((), (), s32[]{:S(2)}) async-start(), calls=%async_computation.18 | async-start | bytes 2064384 | tf_op jit(solution)/shard_map/reduce_scatter | solution.py:412
  804.4 429.1 %reduce-scatter.25.cloned.1.call-start = ((), (), s32[]{:S(2)}) async-start(), calls=%async_computation.23 | async-start | bytes 10321920 | tf_op jit(solution)/shard_map/reduce_scatter | solution.py:417
  809.4 586.9 %reduce-scatter.21.cloned.1.call-start = ((), (), s32[]{:S(2)}) async-start(), calls=%async_computation.21 | async-start | bytes 10321920 | tf_op jit(solution)/shard_map/reduce_scatter | solution.py:415
  818.0 863.8 %reduce-scatter.29.cloned.1.call-start = ((), (), s32[]{:S(2)}) async-start(), calls=%async_computation.25 | async-start | bytes 18874368 | tf_op jit(solution)/shard_map/reduce_scatter | solution.py:422
  829.9 1137.4 %reduce-scatter.27.cloned.1.call-start = ((), (), s32[]{:S(2)}) async-start(), calls=%async_computation.24 | async-start | bytes 18874368 | tf_op jit(solution)/shard_map/reduce_scatter | solution.py:420
  841.0 1186.3 %reduce-scatter.19.cloned.1.call-start = ((), (), s32[]{:S(2)}) async-start(), calls=%async_computation.20 | async-start | bytes 110592 | tf_op jit(solution)/shard_map/reduce_scatter | solution.py:414
  1003.8 1105.8 %all-reduce.12.cloned.1.call-start = ((), (), s32[]{:S(2)}) async-start(), calls=%async_computation.26 | async-start | bytes 7176192 | tf_op jit(solution)/shard_map/psum | solution.py:428
  1398.5 571.5 %copy-start.16 = (bf16[1024,448]{0,1:T(8,128)(2,1)S(1)}, bf16[1024,448]{0,1:T(8,128)(2,1)}, u32[]{:S(2)}) copy-start(bf16[1024,448]{0,1:T(8,128)(2,1)} %copy-done.15) | copy-start | bytes 2752516
  1398.5 571.5 %copy-start.29 = (f32[256,1024]{1,0:T(8,128)S(1)}, f32[256,1024]{1,0:T(8,128)}, u32[]{:S(2)}) copy-start(f32[256,1024]{1,0:T(8,128)} %fusion.99) | copy-start | bytes 3145732
  (95 other events, 2463.0 us)
Sparse Core Ops, SparseCore 0:
  10.1 93.7 all-gather.15
  106.5 46.1 all-gather.13
  155.3 46.5 all-gather.17
  204.0 100.8 all-gather.19
  306.9 120.7 all-gather.23
  429.7 123.1 all-gather.21
  625.5 176.1 reduce-scatter.10
  805.5 55.9 reduce-scatter.22
  864.9 66.5 reduce-scatter.16
  935.9 65.4 reduce-scatter.12
  1005.4 65.2 reduce-scatter.14
  1074.6 158.8 reduce-scatter.24
  1237.2 159.1 reduce-scatter.20
  1400.5 281.3 reduce-scatter.28
  1685.5 281.7 reduce-scatter.26
  1970.7 56.4 reduce-scatter.18
  2032.0 77.6 all-reduce.11
where the time goes:
time: 2140 us; the launch traced here: 2130 us
  waiting for transfers between devices  1530 us (71%)
  blocking collectives  346 us (16%)
  matrix products  111 us (5%)
  other arithmetic  71.4 us (3%)
  local copies, waits for them, and re-layouts  54.4 us (3%)
    reduce_scatter x1, waiting for transfers between devices, on_device(): lax.psum_scatter(grad_ffn_out, 'ctx', scatter_dimension=0, tiled=True)  283 us
    reduce_scatter x1, waiting for transfers between devices, on_device(): lax.psum_scatter(grad_ffn_in, 'ctx', scatter_dimension=0, tiled=True)  283 us
    reduce_scatter x1, waiting for transfers between devices, on_device(): lax.psum_scatter(grad_out, 'ctx', scatter_dimension=0, tiled=True)  161 us
    reduce_scatter x1, waiting for transfers between devices, on_device(): lax.psum_scatter(grad_value, 'ctx', scatter_dimension=0, tiled=True)  161 us
    reduce_scatter x1, waiting for transfers between devices, on_device(): lax.psum_scatter(key_grads, 'ctx', scatter_dimension=0, tiled=True)  154 us
    all_gather x1, waiting for transfers between devices, on_device(): lax.all_gather(feedforward_out_weight2, 'ctx', axis=0, tiled=True)  119 us
    all_gather x1, waiting for transfers between devices, on_device(): lax.all_gather(feedforward_in_weight1, 'ctx', axis=0, tiled=True)  117 us
    reduce_scatter x1, waiting for transfers between devices, on_device(): lax.psum_scatter(grad_query, 'ctx', scatter_dimension=0, tiled=True)  68.2 us
  transfers between devices with their start and end apart: 17, of which 13 were waited for; matrix products, arithmetic and copies ran while one was open for 7% of the time, Pallas kernels for 0%

commit v1 on v0

v1 whole, which is shorter than its diff:
```python
import functools
import math

import jax
import jax.numpy as jnp
import numpy as np
from jax import lax
from jax.experimental import pallas as pl
from jax.experimental.pallas import tpu as pltpu
from jax.sharding import PartitionSpec as P

MESH = pl.DeviceIdType.MESH
F32 = jnp.float32
BF16 = jnp.bfloat16
LN_EPS = 1e-05
MASKED = -1e30
LANES = 128
SPOT_A, SPOT_B = 63, 127
VMEM = pl.BlockSpec(memory_space=pltpu.VMEM)
ANY = pl.BlockSpec(memory_space=pl.ANY)
DMA = pltpu.SemaphoreType.DMA


def turn_coefficients():
    nodes = (np.cos(np.pi * (np.arange(400) + 0.5) / 400) + 1) / 8
    root = np.sqrt(nodes)
    powers = nodes[:, None] ** np.arange(7)[None, :]
    sine = np.linalg.lstsq(powers, np.sin(2 * np.pi * root) / root, rcond=None)[0]
    cosine = np.linalg.lstsq(powers, np.cos(2 * np.pi * root), rcond=None)[0]
    return [float(v) for v in sine], [float(v) for v in cosine]


SIN_TURN, COS_TURN = turn_coefficients()


def horner(coefs, v):
    total = coefs[-1]
    for coef in coefs[-2::-1]:
        total = total * v + coef
    return total


def turn_table(model_width):
    freq = 10000.0 ** (-np.arange(0, model_width, 2, dtype=np.float64) / model_width) / (2 * np.pi)
    mantissa, exponent = np.frexp(freq)
    coarse = np.ldexp(np.floor(mantissa * 256) / 256, exponent)
    table = np.zeros((8, model_width // 2), np.float32)
    table[0] = coarse
    table[1] = freq - coarse
    return table


def sin_cos(places, table_ref):
    coarse = places * table_ref[0:1, :]
    part = (coarse - jnp.round(coarse)) + places * table_ref[1:2, :]
    part = part - jnp.round(part)
    square = part * part
    return horner(SIN_TURN, square) * part, horner(COS_TURN, square)


def mm(left, right):
    return lax.dot_general(left, right, (((1,), (0,)), ((), ())), preferred_element_type=F32)


def mm_t(left, right):
    return lax.dot_general(left, right, (((1,), (1,)), ((), ())), preferred_element_type=F32)


def mm_left_t(left, right):
    return lax.dot_general(left, right, (((0,), (0,)), ((), ())), preferred_element_type=F32)


def copy_to(src, dst, send, recv, f, c):
    return pltpu.make_async_remote_copy(
        src_ref=src, dst_ref=dst, send_sem=send, recv_sem=recv, device_id=(f, c), device_id_type=MESH
    )


def greet(f, c, fsdp, n):
    barrier = pltpu.get_barrier_semaphore()

    def one(k, _):
        pl.semaphore_signal(barrier, inc=1, device_id=(f, lax.rem(c + k, n)), device_id_type=MESH)
        return 0

    lax.fori_loop(1, n, one, 0)
    for k in range(1, fsdp):
        pl.semaphore_signal(barrier, inc=1, device_id=(f ^ k, c), device_id_type=MESH)
    pl.semaphore_wait(barrier, n - 1 + fsdp - 1)


class LineGather:
    def __init__(self, f, c, n, own, at, recv, right, left, pair, lone=False):
        self.f, self.c, self.n, self.size = f, c, n, n // 2
        self.place, self.bit = c // 2, lax.rem(c, 2)
        self.own, self.at = own, at
        self.recv, self.right, self.left, self.pair = recv, right, left, pair
        self.lone = lone

    def valid(self, o):
        ok = jnp.logical_and(o >= 0, o < self.size)
        if self.lone:
            span = self.size // 4
            ok = jnp.logical_and(ok, jnp.logical_and(o >= self.f * span, o < (self.f + 1) * span))
        return ok

    def slot(self, block):
        return block - self.f * (self.n // 4) if self.lone else block

    def copy(self, src, block, sems, c):
        slot = self.slot(block)
        return copy_to(src, self.at(slot), sems.at[slot], self.recv.at[slot], self.f, c)

    def spread(self, src, block, go_right, go_left):
        @pl.when(go_right)
        def _():
            self.copy(src, block, self.right, self.c + 2).start()

        @pl.when(go_left)
        def _():
            self.copy(src, block, self.left, self.c - 2).start()

        self.copy(src, block, self.pair, self.c + 1 - 2 * self.bit).start()

    def begin(self, local):
        @pl.when(self.valid(self.place))
        def _():
            self.spread(self.own, self.c, self.place < self.size - 1, self.place > 0)
            local()

    def arrived(self, block):
        slot = self.slot(block)
        self.copy(self.at(slot), block, self.pair, self.c).wait_recv()

    def step(self, t):
        for sign in (-1, 1):
            o = self.place + sign * t
            block = 2 * o + self.bit

            @pl.when(self.valid(o))
            def _():
                self.arrived(block)
                self.spread(
                    self.at(self.slot(block)),
                    block,
                    jnp.logical_and(sign < 0, self.place < self.size - 1),
                    jnp.logical_and(sign > 0, self.place > 0),
                )

    def steps(self):
        lax.fori_loop(1, self.size, lambda t, u: (self.step(t), u)[1], 0)

    def finish(self):
        def one(o, _):
            @pl.when(self.valid(o))
            def _():
                self.arrived(2 * o + 1 - self.bit)
                block = 2 * o + self.bit
                source = self.at(self.slot(block))
                self.copy(source, block, self.pair, self.c).wait_send()

                @pl.when(jnp.logical_and(o <= self.place, self.place < self.size - 1))
                def _():
                    self.copy(source, block, self.right, self.c).wait_send()

                @pl.when(jnp.logical_and(o >= self.place, self.place > 0))
                def _():
                    self.copy(source, block, self.left, self.c).wait_send()

            return 0

        lax.fori_loop(0, self.size, one, 0)


class QuadGather:
    def __init__(self, f, c, out, send, recv):
        self.f, self.c, self.out, self.send, self.recv = f, c, out, send, recv

    def copy(self, slot, k, to, src=None):
        src = self.out.at[slot] if src is None else src
        return copy_to(src, self.out.at[slot], self.send.at[k], self.recv.at[slot], to, self.c)

    def begin(self, src=None):
        self.copy(self.f, 1, self.f ^ 2, src).start()
        self.copy(self.f, 0, self.f ^ 1, src).start()

    def got(self, slot):
        self.copy(slot, 0, self.f).wait_recv()

    def relay(self):
        self.got(self.f ^ 2)
        self.copy(self.f ^ 2, 2, self.f ^ 1).start()

    def sent(self):
        for k in range(3):
            self.copy(self.f, k, self.f).wait_send()


def spread_vector(rows, width):
    count = rows.shape[0]
    total = count * width
    lane = lax.broadcasted_iota(jnp.int32, (LANES, total), 0)
    column = lax.broadcasted_iota(jnp.int32, (LANES, total), 1)
    onehot = jnp.where(lane == lax.rem(column, width), 1.0, 0.0).astype(BF16)
    wide = mm(rows.astype(BF16), onehot)
    row = lax.broadcasted_iota(jnp.int32, (count, total), 0)
    column = lax.broadcasted_iota(jnp.int32, (count, total), 1)
    return jnp.sum(jnp.where(column // width == row, wide, 0.0), axis=0, keepdims=True)


def block_of(j, i, groups):
    return i * groups + jnp.where(lax.rem(i, 2) == 0, j, groups - 1 - j)


def holder_of(block, groups):
    row, within = block // groups, lax.rem(block, groups)
    return jnp.where(lax.rem(row, 2) == 0, within, groups - 1 - within), row


def key_places(kv):
    return kv[:, SPOT_A : SPOT_A + 1].astype(F32) * 128.0 + kv[:, SPOT_B : SPOT_B + 1].astype(F32)


def attend_kernel(
    n,
    x_ref, aux_ref, cot_ref, p1_ref, small_ref, wout_ref, bias_ref, table_ref,
    tok_ref, p1g_ref, smallg_ref, woutg_ref, cotg_ref, ev_ref, gates_ref, o_ref,
    qcat_ref, qpos_ref, kv_ref, lse_ref, of_ref,
    qs_ref, kvs_ref, qr_ref, os_ref, kcat_ref, m_ref, l_ref,
    sm_s, sm_r, p_r, p_a, p_b, p_c, w_r, w_a, w_b, w_c,
    t_s, t_r, c_s, c_r, q_s, q_r, kv_s, kv_r, o_s, o_r, loc,
):
    f, c = lax.axis_index("fsdp"), lax.axis_index("ctx")
    groups = n // 4
    seq, turn = c // groups, lax.rem(c, groups)
    tokens, width = x_ref.shape
    scale = 1.0 / math.sqrt(112)
    greet(f, c, 4, n)

    def small_send(k, _):
        to = lax.rem(c + k, n)
        copy_to(small_ref, smallg_ref.at[c], sm_s.at[to], sm_r.at[c], f, to).start()
        return 0

    lax.fori_loop(1, n, small_send, 0)
    smallg_ref[c] = small_ref[...]
    gather_p = LineGather(f, c, n, p1_ref, lambda k: p1g_ref.at[k], p_r, p_a, p_b, p_c)

    def own_p():
        p1g_ref[c] = p1_ref[...]

    gather_p.begin(own_p)
    wout_copy = pltpu.make_async_copy(wout_ref, woutg_ref.at[c - f * groups], loc.at[0])
    gather_w = LineGather(f, c, n, wout_ref, lambda k: woutg_ref.at[k], w_r, w_a, w_b, w_c, lone=True)
    cot_copy = pltpu.make_async_copy(cot_ref, cotg_ref.at[f], loc.at[1])
    cot_copy.start()

    hidden = x_ref[...].astype(F32)
    offsets = hidden - jnp.mean(hidden, axis=1, keepdims=True)
    spread = jnp.mean(offsets * offsets, axis=1, keepdims=True)
    xhat = offsets * lax.rsqrt(spread + LN_EPS)

    def small_wait(k, _):
        to = lax.rem(c + k, n)
        copy_to(small_ref, smallg_ref.at[to], sm_s.at[to], sm_r.at[to], f, to).wait()
        return 0

    lax.fori_loop(1, n, small_wait, 0)
    gain = spread_vector(smallg_ref[:, 0, :], width // n)
    shift = spread_vector(smallg_ref[:, 1, :], width // n)
    tok_ref[f, :, 0:width] = (xhat * gain + shift).astype(BF16)
    tok_ref[f, :, width:] = aux_ref[...]
    tok_gather = QuadGather(f, c, tok_ref, t_s, t_r)
    tok_gather.begin()
    gather_p.steps()
    tok_gather.relay()
    gather_w.begin(wout_copy.start)
    gather_p.finish()
    tok_gather.got(f ^ 1)
    tok_gather.got(f ^ 3)
    tok_gather.sent()
    cot_gather = QuadGather(f, c, cotg_ref, c_s, c_r)
    cot_gather.begin(cot_ref)

    lane = lax.broadcasted_iota(jnp.int32, (tokens, LANES), 1)
    source = lax.broadcasted_iota(jnp.int32, (LANES, LANES), 0)
    target = lax.broadcasted_iota(jnp.int32, (LANES, LANES), 1)
    wanted = f * 16 + lax.rem(target, 8) + jnp.where(target < 16, 8, 0)
    pick = jnp.where(
        jnp.logical_and(source == wanted, jnp.logical_and(target < 32, lax.rem(target, 8) < 5)), 1.0, 0.0
    ).astype(BF16)
    own_turn, own_slot = holder_of(c, groups)

    def project(t, _):
        s = lax.rem(seq + 1 + t, 4)
        normed = tok_ref[s, :, 0:width]
        aux = tok_ref[s, :, width:]
        weights = p1g_ref[...].reshape(width, p1g_ref.shape[2])
        qk = mm(normed, weights[:, 0:256])
        experts = mm(normed, weights[:, 256:896])
        ev_ref[s] = experts.astype(BF16)
        logits = jnp.zeros((tokens, LANES), F32)
        for e in range(5):
            for spot, first in ((SPOT_B, 0), (SPOT_A, 16)):
                column = experts[:, e * LANES + spot : e * LANES + spot + 1]
                logits = jnp.where(
                    jnp.logical_or(lane == first + e, lane == first + 8 + e), column, logits
                )
        sig = jax.nn.sigmoid(logits)
        gates = mm(aux, pick) * jnp.where(lax.rem(lane, 16) >= 8, sig * (1.0 - sig), sig)
        gates_ref[s] = gates
        values = jnp.zeros((tokens, LANES), F32)
        for e in range(5):
            values = values + gates[:, 16 + e : 17 + e] * experts[:, e * LANES : (e + 1) * LANES]
        spots = jnp.logical_or(lane == SPOT_A, lane == SPOT_B)
        values = jnp.where(spots, 0.0, values)
        keys = jnp.where(lane == SPOT_A, aux[:, 64:65].astype(F32), qk[:, 128:256])
        keys = jnp.where(lane == SPOT_B, aux[:, 65:66].astype(F32), keys)
        qs_ref[s] = qk[:, 0:128].astype(BF16)
        kvs_ref[s, :, 0:128] = keys.astype(BF16)
        kvs_ref[s, :, 128:256] = values.astype(BF16)
        to = s * groups + own_turn

        @pl.when(to != c)
        def _():
            copy_to(qs_ref.at[s], qr_ref.at[own_slot], q_s.at[s], q_r.at[own_slot], f, to).start()

        @pl.when(to == c)
        def _():
            qr_ref[own_slot] = qs_ref[s]

        def kv_send(k, _):
            to = s * groups + k

            @pl.when(to != c)
            def _():
                copy_to(kvs_ref.at[s], kv_ref.at[c], kv_s.at[to], kv_r.at[c], f, to).start()

            @pl.when(to == c)
            def _():
                kv_ref[c] = kvs_ref[s]

            return 0

        lax.fori_loop(0, groups, kv_send, 0)
        return 0

    lax.fori_loop(0, 4, project, 0)

    def kv_wait(block):
        @pl.when(block != c)
        def _():
            copy_to(kvs_ref.at[0], kv_ref.at[block], kv_s.at[block], kv_r.at[block], f, c).wait_recv()

    def prepare(i, _):
        block = block_of(turn, i, groups)

        @pl.when(block != c)
        def _():
            copy_to(qs_ref.at[0], qr_ref.at[i], q_s.at[0], q_r.at[i], f, c).wait_recv()

        kv_wait(block)
        query = qr_ref[i].astype(F32)
        q_position = (query + bias_ref[pl.ds(4 + f, 1), :]).astype(BF16)
        qpos_ref[i] = q_position
        qcat_ref[i, :, width:] = ((query + bias_ref[pl.ds(f, 1), :]) * scale).astype(BF16)
        rel = p1g_ref[:, :, 896:].reshape(width, LANES)
        rel_query = mm_t(q_position, rel)
        sine, cosine = sin_cos(key_places(kv_ref[block]), table_ref)
        first, second = rel_query[:, : width // 2], rel_query[:, width // 2 :]
        qcat_ref[i, :, 0 : width // 2] = ((first * sine + second * cosine) * scale).astype(BF16)
        qcat_ref[i, :, width // 2 : width] = ((second * sine - first * cosine) * scale).astype(BF16)
        m_ref[i] = jnp.full((tokens, 1), MASKED, F32)
        l_ref[i] = jnp.zeros((tokens, 1), F32)
        of_ref[i] = jnp.zeros((tokens, LANES), F32)
        return 0

    lax.fori_loop(0, 4, prepare, 0)
    row_in = lax.broadcasted_iota(jnp.int32, (tokens, tokens), 0)
    col_in = lax.broadcasted_iota(jnp.int32, (tokens, tokens), 1)

    def key_block(kb, _):
        own = [block_of(turn, i, groups) for i in range(4)]
        first = sum((b < kb).astype(jnp.int32) for b in own)
        ready = sum((b == kb).astype(jnp.int32) for b in own)

        @pl.when(ready == 0)
        def _():
            kv_wait(kb)

        sine, cosine = sin_cos(key_places(kv_ref[kb]), table_ref)
        kcat_ref[:, 0 : width // 2] = cosine.astype(BF16)
        kcat_ref[:, width // 2 : width] = sine.astype(BF16)
        kcat_ref[:, width:] = kv_ref[kb, :, 0:128]

        def query_block(i, _):
            gap = (block_of(turn, i, groups) - kb) * tokens
            scores = mm_t(qcat_ref[i], kcat_ref[...])
            scores = jnp.where(col_in <= row_in + gap, scores, MASKED)
            before = m_ref[i]
            best = jnp.maximum(before, jnp.max(scores, axis=1, keepdims=True))
            shrink = jnp.exp(before - best)
            probs = jnp.exp(scores - best)
            m_ref[i] = best
            l_ref[i] = l_ref[i] * shrink + jnp.sum(probs, axis=1, keepdims=True)
            of_ref[i] = of_ref[i] * shrink + mm(probs.astype(BF16), kv_ref[kb, :, 128:256])
            return 0

        lax.fori_loop(first, 4, query_block, 0)
        return 0

    lax.fori_loop(0, n, key_block, 0)

    def give(i, _):
        block = block_of(turn, i, groups)
        total = l_ref[i]
        result = of_ref[i] / total
        of_ref[i] = result
        lse_ref[i] = m_ref[i] + jnp.log(total)
        os_ref[i] = result.astype(BF16)

        @pl.when(block != c)
        def _():
            copy_to(os_ref.at[i], o_ref.at[seq], o_s.at[i], o_r.at[seq], f, block).start()

        @pl.when(block == c)
        def _():
            o_ref[seq] = os_ref[i]

        return 0

    lax.fori_loop(0, 4, give, 0)
    gather_w.steps()
    cot_gather.relay()
    cot_gather.got(f ^ 1)
    cot_gather.got(f ^ 3)
    cot_gather.sent()
    gather_w.finish()

    @pl.when(gather_w.valid(c // 2))
    def _():
        wout_copy.wait()

    cot_copy.wait()

    def drain(s, _):
        to = s * groups + own_turn

        @pl.when(to != c)
        def _():
            copy_to(qs_ref.at[s], qr_ref.at[own_slot], q_s.at[s], q_r.at[0], f, to).wait_send()
            copy_to(os_ref.at[0], o_ref.at[s], o_s.at[0], o_r.at[s], f, to).wait_recv()

        @pl.when(block_of(turn, s, groups) != c)
        def _():
            copy_to(os_ref.at[s], o_ref.at[s], o_s.at[s], o_r.at[0], f, to).wait_send()

        return 0

    lax.fori_loop(0, 4, drain, 0)

    def kv_drain(to, _):
        @pl.when(to != c)
        def _():
            copy_to(kvs_ref.at[0], kv_ref.at[0], kv_s.at[to], kv_r.at[0], f, c).wait_send()

        return 0

    lax.fori_loop(0, n, kv_drain, 0)


def sds(shape, dtype):
    return jax.ShapeDtypeStruct(shape, dtype)


def attend(n, x, aux, cot, p1, small, wout, bias, table):
    t, d = x.shape
    rows = p1.shape[0]
    out_rows = wout.shape[0]
    g = n // 4
    return pl.pallas_call(
        functools.partial(attend_kernel, n),
        out_shape=[
            sds((4, t, d + LANES), BF16), sds((n, rows, d), BF16), sds((n, 16, LANES), F32),
            sds((g, out_rows, d), BF16), sds((4, t, d), BF16), sds((4, t, 640), BF16),
            sds((4, t, LANES), F32), sds((4, t, LANES), BF16), sds((4, t, d + LANES), BF16),
            sds((4, t, LANES), BF16), sds((n, t, 256), BF16), sds((4, t, 1), F32), sds((4, t, LANES), F32),
        ],
        in_specs=[VMEM, VMEM, ANY, VMEM, VMEM, ANY, VMEM, VMEM],
        out_specs=[VMEM, VMEM, VMEM, ANY, ANY] + [VMEM] * 8,
        scratch_shapes=[
            pltpu.VMEM((4, t, LANES), BF16), pltpu.VMEM((4, t, 256), BF16), pltpu.VMEM((4, t, LANES), BF16),
            pltpu.VMEM((4, t, LANES), BF16), pltpu.VMEM((t, d + LANES), BF16),
            pltpu.VMEM((4, t, 1), F32), pltpu.VMEM((4, t, 1), F32),
            DMA((n,)), DMA((n,)), DMA((n,)), DMA((n,)), DMA((n,)), DMA((n,)),
            DMA((g,)), DMA((g,)), DMA((g,)), DMA((g,)),
            DMA((3,)), DMA((4,)), DMA((3,)), DMA((4,)), DMA((4,)), DMA((4,)),
            DMA((n,)), DMA((n,)), DMA((4,)), DMA((4,)), DMA((2,)),
        ],
        compiler_params=pltpu.CompilerParams(
            collective_id=0, has_side_effects=True, vmem_limit_bytes=56 << 20
        ),
        name="attend",
    )(x, aux, cot, p1, small, wout, bias, table)


class QuadSum:
    def __init__(self, f, c, core_out, core_in, x_out, x_in, keep, send, recv):
        self.f, self.c = f, c
        self.core_out, self.core_in, self.x_out, self.x_in = core_out, core_in, x_out, x_in
        self.keep, self.send, self.recv = keep, send, recv

    def core(self, k):
        return copy_to(
            self.core_out.at[k], self.core_in.at[k], self.send.at[k], self.recv.at[k], self.f ^ 1, self.c
        )

    def across(self):
        return copy_to(self.x_out, self.x_in, self.send.at[2], self.recv.at[2], self.f ^ 2, self.c)

    def put(self, k, value):
        if k in (1, 3):
            self.core_out[k // 2] = value.astype(BF16)
            self.core(k // 2).start()
        else:
            self.keep[k // 2] = value

    def cross(self):
        self.core(1).wait_recv()
        self.x_out[...] = (self.keep[1] + self.core_in[1].astype(F32)).astype(BF16)
        self.across().start()

    def total(self):
        self.core(0).wait_recv()
        self.across().wait_recv()
        return self.keep[0] + self.core_in[0].astype(F32) + self.x_in[...].astype(F32)

    def sent(self):
        self.core(0).wait_send()
        self.core(1).wait_send()
        self.across().wait_send()


def quad_sum_scratch(t, d):
    return [
        pltpu.VMEM((2, t, d), BF16), pltpu.VMEM((2, t, d), BF16), pltpu.VMEM((t, d), BF16),
        pltpu.VMEM((t, d), BF16), pltpu.VMEM((2, t, d), F32), DMA((3,)), DMA((3,)),
    ]


def layer_stats(v):
    offsets = v - jnp.mean(v, axis=1, keepdims=True)
    scale = lax.rsqrt(jnp.mean(offsets * offsets, axis=1, keepdims=True) + LN_EPS)
    return offsets * scale, scale


def layer_back(grad, gain, xhat, scale):
    inner = grad * gain
    return scale * (
        inner - jnp.mean(inner, axis=1, keepdims=True) - xhat * jnp.mean(inner * xhat, axis=1, keepdims=True)
    )


def gelu_pair(v):
    k = math.sqrt(2.0 / math.pi)
    square = v * v
    t = jnp.tanh(k * v * (1.0 + 0.044715 * square))
    half = 0.5 * (1.0 + t)
    return v * half, half + 0.5 * v * (1.0 - t * t) * (k * (1.0 + 3 * 0.044715 * square))


def bias_quarter(small_ref, f, n, quarter):
    span = n // 4
    shard = quarter // span
    piece = min(LANES, shard)
    lane = lax.broadcasted_iota(jnp.int32, (LANES, quarter), 0)
    column = lax.broadcasted_iota(jnp.int32, (LANES, quarter), 1)
    onehot = jnp.where(lane == lax.rem(column, piece), 1.0, 0.0).astype(BF16)
    row = lax.broadcasted_iota(jnp.int32, (span, quarter), 0)
    column = lax.broadcasted_iota(jnp.int32, (span, quarter), 1)
    total = jnp.zeros((1, quarter), F32)
    for k in range(shard // piece):
        rows = small_ref[pl.ds(f * span, span), 5 + k, :]
        wide = mm(rows.astype(BF16), onehot)
        keep = jnp.logical_and(column // shard == row, lax.rem(column, shard) // piece == k)
        total = total + jnp.sum(jnp.where(keep, wide, 0.0), axis=0, keepdims=True)
    return total


def feed_kernel(
    n,
    x_ref, cot_ref, gates_ref, o_ref, wout_ref, small_ref, w1_ref, w2_ref,
    out_ref, dmid_ref, gwout_ref, gw1_ref, gw2_ref, da_ref, gsel_ref, vec_ref,
    w1g, w2g, n2_ref, act_ref, slope_ref, dpre_ref, mixed_ref, dml_ref, mid_ref,
    a0, a1, a2, a3, a4, a5, a6, b0, b1, b2, b3, b4, b5, b6, e0, e1, e2, e3, e4, e5, e6,
    w1_r, w1_a, w1_b, w1_c, w2_r, w2_a, w2_b, w2_c, n_s, n_r, d_s, d_r, loc,
):
    f, c = lax.axis_index("fsdp"), lax.axis_index("ctx")
    tokens, width = x_ref.shape
    quarter = w1g.shape[1]
    greet(f, c, 4, n)
    rows1, rows2 = w1_ref.shape[0], w2_ref.shape[0]
    own1 = w1_ref.at[:, pl.ds(pl.multiple_of(f * quarter, LANES), quarter)]
    at1 = lambda k: w1g.at[pl.ds(pl.multiple_of(k * rows1, rows1), rows1), :]
    at2 = lambda k: w2g.at[pl.ds(pl.multiple_of(k * rows2, rows2), rows2), :]
    gather1 = LineGather(f, c, n, own1, at1, w1_r, w1_a, w1_b, w1_c)
    gather2 = LineGather(f, c, n, w2_ref, at2, w2_r, w2_a, w2_b, w2_c, lone=True)
    local1 = pltpu.make_async_copy(own1, at1(c), loc.at[0])
    local2 = pltpu.make_async_copy(w2_ref, at2(c - f * (n // 4)), loc.at[1])
    gather1.begin(local1.start)
    gather2.begin(local2.start)
    attn_sum = QuadSum(f, c, a0, a1, a2, a3, a4, a5, a6)
    back_sum = QuadSum(f, c, b0, b1, b2, b3, b4, b5, b6)
    out_sum = QuadSum(f, c, e0, e1, e2, e3, e4, e5, e6)

    for k in (3, 2, 1, 0):
        r = f ^ k
        for e in range(5):
            mixed_ref[r, :, e * LANES : (e + 1) * LANES] = (
                gates_ref[r, :, e : e + 1] * o_ref[r].astype(F32)
            ).astype(BF16)
        attn_sum.put(k, mm(mixed_ref[r], wout_ref[...]))
        if k == 2:
            attn_sum.cross()
    gather1.step(1)
    middle = x_ref[...].astype(F32) + attn_sum.total()
    mid_ref[...] = middle
    xhat, scale = layer_stats(middle)
    gain = spread_vector(small_ref[:, 2, :], width // n)
    shift = spread_vector(small_ref[:, 3, :], width // n)
    n2_ref[f] = (xhat * gain + shift).astype(BF16)
    n2_gather = QuadGather(f, c, n2_ref, n_s, n_r)
    n2_gather.begin()
    lax.fori_loop(2, n // 2, lambda t, u: (gather1.step(t), u)[1], 0)
    gather1.finish()
    local1.wait()
    gather2.step(1)
    first_bias = bias_quarter(small_ref, f, n, quarter)

    def enter(k):
        r = f ^ k
        act, slope = gelu_pair(mm(n2_ref[r], w1g[...]) + first_bias)
        act_ref[r] = act.astype(BF16)
        slope_ref[r] = slope

    enter(0)
    n2_gather.got(f ^ 1)
    enter(1)
    n2_gather.relay()
    enter(2)
    n2_gather.got(f ^ 3)
    enter(3)
    lax.fori_loop(2, n // 2, lambda t, u: (gather2.step(t), u)[1], 0)
    gather2.finish()

    @pl.when(gather2.valid(c // 2))
    def _():
        local2.wait()

    for k in (3, 2, 1, 0):
        r = f ^ k
        d_act = mm_t(cot_ref[r], w2g[...])
        dpre_ref[r] = (d_act * slope_ref[r]).astype(BF16)
        back_sum.put(k, mm_t(dpre_ref[r], w1g[...]))
        if k == 2:
            back_sum.cross()
    for k in (3, 2, 1, 0):
        out_sum.put(k, mm(act_ref[f ^ k], w2g[...]))
    tile = 256
    all_tokens = 4 * tokens

    def weight_tile(left_ref, right_ref, result_ref):
        def one(i, _):
            spot = pl.multiple_of(i * tile, tile)
            left = left_ref[:, :, pl.ds(spot, tile)].reshape(all_tokens, tile)
            right = right_ref[...].reshape(all_tokens, right_ref.shape[2])
            result_ref[pl.ds(spot, tile), :] = mm_left_t(left, right).astype(BF16)
            return 0

        lax.fori_loop(0, left_ref.shape[2] // tile, one, 0)

    weight_tile(act_ref, cot_ref, gw2_ref)
    weight_tile(n2_ref, dpre_ref, gw1_ref)
    d_norm = back_sum.total()
    xhat, scale = layer_stats(mid_ref[...])
    d_middle = cot_ref[f].astype(F32) + layer_back(d_norm, gain, xhat, scale)
    dmid_ref[...] = d_middle
    dml_ref[f] = d_middle.astype(BF16)
    dml_gather = QuadGather(f, c, dml_ref, d_s, d_r)
    dml_gather.begin()
    out_sum.cross()
    vec_ref[...] = jnp.zeros_like(vec_ref)
    vec_ref[0:1, :] = jnp.sum(d_norm * xhat, axis=0, keepdims=True)
    vec_ref[1:2, :] = jnp.sum(d_norm, axis=0, keepdims=True)
    vec_ref[2:3, :] = jnp.sum(cot_ref[f].astype(F32), axis=0, keepdims=True)
    total = jnp.zeros((1, quarter), F32)
    for r in range(4):
        total = total + jnp.sum(dpre_ref[r].astype(F32), axis=0, keepdims=True)
    vec_ref[3:4, :] = total
    lane = lax.broadcasted_iota(jnp.int32, (tokens, LANES), 1)

    def leave(k):
        r = f ^ k
        d_attn = jnp.zeros((tokens, LANES), F32)
        select = jnp.zeros((tokens, LANES), F32)
        result = o_ref[r].astype(F32)
        d_mixed = mm_t(dml_ref[r], wout_ref[...])
        for e in range(5):
            part = d_mixed[:, e * LANES : (e + 1) * LANES]
            d_attn = d_attn + gates_ref[r, :, e : e + 1] * part
            column = jnp.sum(result * part, axis=1, keepdims=True) * gates_ref[r, :, 8 + e : 9 + e]
            select = jnp.where(lane == e, column, select)
        da_ref[r] = d_attn.astype(BF16)
        gsel_ref[r] = select

    leave(0)
    dml_gather.got(f ^ 1)
    leave(1)
    dml_gather.relay()
    leave(2)
    dml_gather.got(f ^ 3)
    leave(3)

    def out_tile(i, _):
        spot = pl.multiple_of(i * LANES, LANES)
        left = mixed_ref[:, :, pl.ds(spot, LANES)].reshape(all_tokens, LANES)
        right = dml_ref[...].reshape(all_tokens, width)
        gwout_ref[pl.ds(spot, LANES), :] = mm_left_t(left, right).astype(BF16)
        return 0

    lax.fori_loop(0, 5, out_tile, 0)
    second_bias = spread_vector(small_ref[:, 4, :], width // n)
    out_ref[...] = (mid_ref[...] + out_sum.total() + second_bias).astype(BF16)
    for one in (attn_sum, back_sum, out_sum, n2_gather, dml_gather):
        one.sent()


def feed(n, x, cot, gates, o, wout, small, w1, w2):
    t, d = x.shape
    quarter = w1.shape[1] // 4
    g = n // 4
    return pl.pallas_call(
        functools.partial(feed_kernel, n),
        out_shape=[
            sds((t, d), BF16), sds((t, d), F32), sds((640, d), BF16), sds((d, quarter), BF16),
            sds((quarter, d), BF16), sds((4, t, LANES), BF16), sds((4, t, LANES), F32), sds((8, d), F32),
        ],
        in_specs=[VMEM] * 6 + [ANY, ANY],
        out_specs=[VMEM] * 8,
        scratch_shapes=[
            pltpu.VMEM((d, quarter), BF16), pltpu.VMEM((quarter, d), BF16), pltpu.VMEM((4, t, d), BF16),
            pltpu.VMEM((4, t, quarter), BF16), pltpu.VMEM((4, t, quarter), F32), pltpu.VMEM((4, t, quarter), BF16),
            pltpu.VMEM((4, t, 640), BF16), pltpu.VMEM((4, t, d), BF16), pltpu.VMEM((t, d), F32),
        ]
        + quad_sum_scratch(t, d) * 3
        + [DMA((n,))] * 4 + [DMA((g,))] * 4
        + [DMA((3,)), DMA((4,)), DMA((3,)), DMA((4,)), DMA((2,))],
        compiler_params=pltpu.CompilerParams(
            collective_id=1, has_side_effects=True, vmem_limit_bytes=60 << 20
        ),
        name="feed",
    )(x, cot, gates, o, wout, small, w1, w2)


class LineSum:
    def __init__(self, f, c, n, source, got, inbox, stage, pair_s, pair_r, line_s, line_r, subs, lone=False):
        self.f, self.c, self.n, self.size = f, c, n, n // 2
        self.place, self.bit = c // 2, lax.rem(c, 2)
        self.source = source
        self.got, self.inbox, self.stage = got, inbox, stage
        self.pair_s, self.pair_r, self.line_s, self.line_r = pair_s, pair_r, line_s, line_r
        self.subs, self.lone = subs, lone
        self.span = self.size // 4 if lone else self.size
        self.first = f * self.span if lone else 0

    def valid(self, o):
        return jnp.logical_and(o >= self.first, o < self.first + self.span)

    def index(self, o, sub):
        return (o - self.first) * self.subs + sub

    def term(self, o, sub, bit):
        return self.source(2 * (o - self.first) + bit, sub)

    def pair_copy(self, o, sub):
        i = self.index(o, sub)
        return copy_to(
            self.term(o, sub, 1 - self.bit), self.got.at[i], self.pair_s.at[i], self.pair_r.at[i],
            self.f, self.c + 1 - 2 * self.bit,
        )

    def line_copy(self, i, slot, c):
        return copy_to(self.stage.at[i], self.inbox.at[slot], self.line_s.at[i], self.line_r.at[slot], self.f, c)

    def each(self, work):
        def one(k, _):
            work(self.first + k // self.subs, lax.rem(k, self.subs))
            return 0

        lax.fori_loop(0, self.span * self.subs, one, 0)

    def begin(self):
        self.each(lambda o, sub: self.pair_copy(o, sub).start())

    def gathered(self, o, sub):
        self.pair_copy(o, sub).wait_recv()
        return self.term(o, sub, self.bit)[...].astype(F32) + self.got[self.index(o, sub)].astype(F32)

    def extra(self, sub):
        return self.span * self.subs + sub

    def move(self, o, sub, go_right):
        i = self.index(o, sub)
        total = self.gathered(o, sub)
        starts = self.place == 0 if go_right else self.place == self.size - 1

        @pl.when(starts)
        def _():
            self.stage[i] = total.astype(BF16)

        @pl.when(jnp.logical_not(starts))
        def _():
            self.line_copy(i, i, self.c).wait_recv()
            self.stage[i] = (total + self.inbox[i].astype(F32)).astype(BF16)

        if go_right:
            self.line_copy(i, i, self.c + 2).start()
        else:
            slot = jnp.where(o == self.place - 1, self.extra(sub), i)
            self.line_copy(i, slot, self.c - 2).start()

    def step(self, k):
        def one(sub, _):
            far, near = self.size - 1 - k, k

            @pl.when(jnp.logical_and(self.valid(far), far > self.place))
            def _():
                self.move(far, sub, True)

            @pl.when(jnp.logical_and(self.valid(near), near < self.place))
            def _():
                self.move(near, sub, False)

            return 0

        lax.fori_loop(0, self.subs, one, 0)

    def settle(self, sub):
        i = self.index(self.place, sub)
        self.stage[i] = self.gathered(self.place, sub).astype(BF16)
        own = self.gathered_again(self.place, sub)

        left = self.place > 0
        right = self.place < self.size - 1

        @pl.when(left)
        def _():
            self.line_copy(i, i, self.c).wait_recv()

        @pl.when(right)
        def _():
            self.line_copy(i, self.extra(sub), self.c).wait_recv()

        @pl.when(jnp.logical_and(left, right))
        def _():
            self.stage[i] = (
                own + self.inbox[i].astype(F32) + self.inbox[self.extra(sub)].astype(F32)
            ).astype(BF16)

        @pl.when(jnp.logical_and(left, jnp.logical_not(right)))
        def _():
            self.stage[i] = (own + self.inbox[i].astype(F32)).astype(BF16)

        @pl.when(jnp.logical_and(right, jnp.logical_not(left)))
        def _():
            self.stage[i] = (own + self.inbox[self.extra(sub)].astype(F32)).astype(BF16)

    def gathered_again(self, o, sub):
        return self.term(o, sub, self.bit)[...].astype(F32) + self.got[self.index(o, sub)].astype(F32)

    def finish(self):
        @pl.when(self.valid(self.place))
        def _():
            lax.fori_loop(0, self.subs, lambda sub, u: (self.settle(sub), u)[1], 0)

    def sent(self):
        def one(o, sub):
            self.pair_copy(o, sub).wait_send()

            @pl.when(o != self.place)
            def _():
                self.line_copy(self.index(o, sub), 0, self.c).wait_send()

        self.each(one)


class LoneShare:
    def __init__(self, total, out, send, recv):
        self.f, self.c = total.f, total.c
        self.owner = total.place // (total.size // 4)
        self.rel = total.f ^ self.owner
        start = jnp.where(self.rel == 0, (total.place - total.first) * total.subs, 0)
        self.held = total.stage.at[pl.ds(start, total.subs)]
        self.out, self.send, self.recv = out, send, recv
        self.local = pltpu.make_async_copy(self.held, out, recv)

    def copy(self, src, k, to):
        return copy_to(src, self.out, self.send.at[k], self.recv, to, self.c)

    def begin(self):
        @pl.when(self.rel == 0)
        def _():
            self.copy(self.held, 1, self.f ^ 2).start()
            self.copy(self.held, 0, self.f ^ 1).start()
            self.local.start()

    def relay(self):
        @pl.when(self.rel == 2)
        def _():
            self.copy(self.out, 0, self.f).wait_recv()
            self.copy(self.out, 0, self.f ^ 1).start()

    def finish(self):
        @pl.when(self.rel == 0)
        def _():
            self.local.wait()
            self.copy(self.held, 0, self.f).wait_send()
            self.copy(self.held, 1, self.f).wait_send()

        @pl.when(self.rel == 2)
        def _():
            self.copy(self.out, 0, self.f).wait_send()

        @pl.when(lax.rem(self.rel, 2) == 1)
        def _():
            self.copy(self.out, 0, self.f).wait_recv()


def back_kernel(
    n, far_kv,
    da_ref, gwout_ref, gw1_ref, gw2_ref, qcat_ref, qpos_ref, kv_ref, lse_ref, of_ref,
    tok_ref, p1_ref, ev_ref, gates_ref, gsel_ref, x_ref, small_ref, dmid_ref, vec_ref, table_ref,
    din_ref, gp_ref, g1_ref, g2_ref, go_ref, vq_ref, dkv_ref,
    do_ref, delta_ref, grad_ref, kcat_ref, acc_ref, ring_ref, drel_ref, dqs_ref, dq_ref, part_ref, dp_ref,
    gpart_ref, mine_ref, vin_ref,
    s0, s1, s2, s3, s4, s5, s6,
    p0, p1, p2, p3, p4, p5, p6, u0, u1, u2, u3, u4, u5, u6,
    v0, v1, v2, v3, v4, v5, v6, w0, w1, w2, w3, w4, w5, w6,
    da_s, da_r, kv_s, kv_r, dq_s, dq_r, gp_s, gp_r, g1_s, g1_r, g2_s, g2_r, go_s, go_r,
    vc_s, vc_r, vf_s, vf_r, loc,
):
    f, c = lax.axis_index("fsdp"), lax.axis_index("ctx")
    groups = n // 4
    seq, turn = c // groups, lax.rem(c, groups)
    tokens, width = x_ref.shape
    scale = 1.0 / math.sqrt(112)
    own_turn, own_slot = holder_of(c, groups)
    rows = width // n
    greet(f, c, 4, n)

    def send_da(s, _):
        to = s * groups + own_turn

        @pl.when(to != c)
        def _():
            copy_to(da_ref.at[s], do_ref.at[own_slot], da_s.at[s], da_r.at[own_slot], f, to).start()

        @pl.when(to == c)
        def _():
            do_ref[own_slot] = da_ref[s]

        return 0

    lax.fori_loop(0, 4, send_da, 0)
    sub_out, sub_two = p0.shape[0] // max(1, groups // 2), v0.shape[0] // max(1, groups // 2)

    def rows_at(ref, count):
        return lambda block, sub: ref.at[pl.ds(pl.multiple_of(block * count, count), count), :]

    def piece_at(ref, subs):
        count = ref.shape[1] // subs
        return lambda block, sub: ref.at[block, pl.ds(pl.multiple_of(sub * count, count), count), :]

    sum_out = LineSum(f, c, n, piece_at(gwout_ref, sub_out), p0, p1, p2, p3, p4, p5, p6, sub_out, lone=True)
    sum_one = LineSum(f, c, n, rows_at(gw1_ref, rows), u0, u1, u2, u3, u4, u5, u6, 1)
    sum_two = LineSum(f, c, n, piece_at(gw2_ref, sub_two), v0, v1, v2, v3, v4, v5, v6, sub_two, lone=True)
    sum_in = LineSum(f, c, n, rows_at(gpart_ref, rows), w0, w1, w2, w3, w4, w5, w6, 1)
    big = (sum_two, sum_one, sum_out)
    for one in big:
        one.begin()

    def prepare(i, _):
        @pl.when(block_of(turn, i, groups) != c)
        def _():
            copy_to(da_ref.at[0], do_ref.at[i], da_s.at[0], da_r.at[i], f, c).wait_recv()

        delta_ref[i] = jnp.sum(do_ref[i].astype(F32) * of_ref[i], axis=1, keepdims=True)
        grad_ref[i] = jnp.zeros((tokens, width + LANES), F32)
        return 0

    lax.fori_loop(0, 4, prepare, 0)
    row_in = lax.broadcasted_iota(jnp.int32, (tokens, tokens), 0)
    col_in = lax.broadcasted_iota(jnp.int32, (tokens, tokens), 1)
    lane = lax.broadcasted_iota(jnp.int32, (tokens, LANES), 1)
    spots = jnp.logical_or(lane == SPOT_A, lane == SPOT_B)
    last_own = block_of(turn, 3, groups)
    mine_ref[...] = vec_ref[...]

    def close_query(i, sine, cosine):
        first = grad_ref[i, :, 0 : width // 2]
        second = grad_ref[i, :, width // 2 : width]
        drel_ref[i, :, 0 : width // 2] = ((first * sine - second * cosine) * scale).astype(BF16)
        drel_ref[i, :, width // 2 : width] = ((first * cosine + second * sine) * scale).astype(BF16)
        d_place = mm(drel_ref[i], p1_ref[:, :, 896:].reshape(width, LANES))
        d_content = jnp.where(spots, 0.0, grad_ref[i, :, width:] * scale)
        dqs_ref[i] = (d_content + d_place).astype(BF16)
        mine_ref[6:7, 0:LANES] += jnp.sum(d_content, axis=0, keepdims=True)
        mine_ref[7:8, 0:LANES] += jnp.sum(d_place, axis=0, keepdims=True)
        block = block_of(turn, i, groups)

        @pl.when(block != c)
        def _():
            copy_to(dqs_ref.at[i], dq_ref.at[seq], dq_s.at[i], dq_r.at[seq], f, block).start()

        @pl.when(block == c)
        def _():
            dq_ref[seq] = dqs_ref[i]

    def ring_copy(slot, to):
        return copy_to(ring_ref.at[slot], dkv_ref.at[c], kv_s.at[slot], kv_r.at[c], f, to)

    def ring_local(slot):
        return pltpu.make_async_copy(ring_ref.at[slot], dkv_ref.at[c], kv_s.at[slot])

    def ring_free(kb):
        slot = lax.rem(kb, 4)

        @pl.when(jnp.logical_and(kb != c, kb <= last_own))
        def _():
            ring_copy(slot, c).wait_send()

        @pl.when(jnp.logical_and(kb == c, kb <= last_own))
        def _():
            ring_local(slot).wait()

    def key_block(kb, _):
        own = [block_of(turn, i, groups) for i in range(4)]
        first = sum((b < kb).astype(jnp.int32) for b in own)
        ready = sum((b == kb).astype(jnp.int32) for b in own)
        sine, cosine = sin_cos(key_places(kv_ref[kb]), table_ref)
        kcat_ref[:, 0 : width // 2] = cosine.astype(BF16)
        kcat_ref[:, width // 2 : width] = sine.astype(BF16)
        kcat_ref[:, width:] = kv_ref[kb, :, 0:128]
        acc_ref[...] = jnp.zeros_like(acc_ref)

        def query_block(i, _):
            gap = (block_of(turn, i, groups) - kb) * tokens
            scores = mm_t(qcat_ref[i], kcat_ref[...])
            probs = jnp.where(col_in <= row_in + gap, jnp.exp(scores - lse_ref[i]), 0.0)
            d_probs = mm_t(do_ref[i], kv_ref[kb, :, 128:256])
            d_scores = (probs * (d_probs - delta_ref[i])).astype(BF16)
            acc_ref[:, 0:128] += mm_left_t(d_scores, qcat_ref[i, :, width:])
            acc_ref[:, 128:256] += mm_left_t(probs.astype(BF16), do_ref[i])
            grad_ref[i] += mm(d_scores, kcat_ref[...])
            return 0

        lax.fori_loop(first, 4, query_block, 0)

        @pl.when(ready == 1)
        def _():
            close_query(first, sine, cosine)

        @pl.when(kb >= 4)
        def _():
            ring_free(kb - 4)

        @pl.when(kb <= last_own)
        def _():
            slot = lax.rem(kb, 4)
            ring_ref[slot] = acc_ref[...].astype(BF16)

            @pl.when(kb != c)
            def _():
                ring_copy(slot, kb).start()

            @pl.when(kb == c)
            def _():
                ring_local(slot).start()

        @pl.when(kb >= n // 2)
        def _():
            def progress(k, _):
                index = (kb - n // 2) * 3 + k
                for which, one in enumerate(big):
                    @pl.when(index // (n // 2) == which)
                    def _():
                        one.step(lax.rem(index, n // 2))

                return 0

            lax.fori_loop(0, 3, progress, 0)

        return 0

    lax.fori_loop(0, n, key_block, 0)
    for one in big:
        one.finish()
    share_two = LoneShare(sum_two, g2_ref, g2_s, g2_r)
    share_out = LoneShare(sum_out, go_ref, go_s, go_r)
    gather_one = QuadGather(f, c, g1_ref, g1_s, g1_r)
    local_one = pltpu.make_async_copy(u2.at[c // 2], g1_ref.at[f], loc.at[0])
    local_one.start()
    share_two.begin()
    gather_one.begin(u2.at[c // 2])
    share_out.begin()

    all_tokens = 4 * tokens
    d_rel = drel_ref[...].reshape(all_tokens, width)
    gpart_ref[:, 896:] = mm_left_t(d_rel, qpos_ref[...].reshape(all_tokens, LANES)).astype(BF16)

    def collect(s, _):
        to = s * groups + own_turn

        @pl.when(to != c)
        def _():
            copy_to(dqs_ref.at[0], dq_ref.at[s], dq_s.at[0], dq_r.at[s], f, c).wait_recv()

        acc_ref[...] = jnp.zeros_like(acc_ref)

        def add(k, _):
            at = s * groups + k

            @pl.when(block_of(k, 3, groups) >= c)
            def _():
                @pl.when(at != c)
                def _():
                    copy_to(ring_ref.at[0], dkv_ref.at[at], kv_s.at[0], kv_r.at[at], f, c).wait_recv()

                if far_kv:
                    bring = pltpu.make_async_copy(dkv_ref.at[at], part_ref, loc.at[1])
                    bring.start()
                    bring.wait()
                    acc_ref[...] += part_ref[...].astype(F32)
                else:
                    acc_ref[...] += dkv_ref[at].astype(F32)

            return 0

        lax.fori_loop(0, groups, add, 0)
        dp_ref[s, :, 0:128] = dq_ref[s]
        dp_ref[s, :, 128:256] = acc_ref[:, 0:128].astype(BF16)
        d_values = acc_ref[:, 128:256]
        for e in range(5):
            values = ev_ref[s, :, e * LANES : (e + 1) * LANES].astype(F32)
            column = jnp.sum(values * d_values, axis=1, keepdims=True) * gates_ref[s, :, 24 + e : 25 + e]
            part = gates_ref[s, :, 16 + e : 17 + e] * d_values
            part = jnp.where(lane == SPOT_A, column, part)
            part = jnp.where(lane == SPOT_B, gsel_ref[s, :, e : e + 1], part)
            dp_ref[s, :, 256 + e * LANES : 384 + e * LANES] = part.astype(BF16)
        return 0

    def ring_drain(k, _):
        ring_free(n - 4 + k)
        return 0

    lax.fori_loop(0, 4, ring_drain, 0)
    lax.fori_loop(0, 4, collect, 0)
    tile = 256

    def weight_tile(i, _):
        spot = pl.multiple_of(i * tile, tile)
        left = tok_ref[:, :, pl.ds(spot, tile)].reshape(all_tokens, tile)
        right = dp_ref[...].reshape(all_tokens, 896)
        gpart_ref[pl.ds(spot, tile), 0:896] = mm_left_t(left, right).astype(BF16)
        return 0

    lax.fori_loop(0, width // tile, weight_tile, 0)
    sum_in.begin()
    share_two.relay()
    gather_one.relay()
    share_out.relay()
    in_sum = QuadSum(f, c, s0, s1, s2, s3, s4, s5, s6)
    for k in (3, 2, 1, 0):
        weights = p1_ref[:, :, 0:896].reshape(width, 896)
        in_sum.put(k, mm_t(dp_ref[f ^ k], weights))
        if k == 2:
            in_sum.cross()
    lax.fori_loop(0, n // 2, lambda k, u: (sum_in.step(k), u)[1], 0)
    d_norm = in_sum.total()
    xhat, spread = layer_stats(x_ref[...].astype(F32))
    gain = spread_vector(small_ref[:, 0, :], width // n)
    din_ref[...] = dmid_ref[...] + layer_back(d_norm, gain, xhat, spread)
    mine_ref[4:5, :] = jnp.sum(d_norm * xhat, axis=0, keepdims=True)
    mine_ref[5:6, :] = jnp.sum(d_norm, axis=0, keepdims=True)

    def vec_send(k, _):
        to = lax.rem(c + k, n)
        copy_to(mine_ref, vin_ref.at[c], vc_s.at[to], vc_r.at[c], f, to).start()
        return 0

    lax.fori_loop(1, n, vec_send, 0)
    vin_ref[c] = mine_ref[...]
    sum_in.finish()
    gather_in = QuadGather(f, c, gp_ref, gp_s, gp_r)
    local_in = pltpu.make_async_copy(w2.at[c // 2], gp_ref.at[f], loc.at[1])
    local_in.start()
    gather_in.begin(w2.at[c // 2])

    def vec_wait(k, _):
        to = lax.rem(c + k, n)
        copy_to(mine_ref, vin_ref.at[to], vc_s.at[to], vc_r.at[to], f, to).wait()
        return 0

    lax.fori_loop(1, n, vec_wait, 0)
    vq_ref[f] = jnp.sum(vin_ref[...], axis=0)
    for k in range(1, 4):
        copy_to(vq_ref.at[f], vq_ref.at[f], vf_s.at[k], vf_r.at[f], f ^ k, c).start()
    gather_in.relay()
    for k in range(1, 4):
        copy_to(vq_ref.at[f ^ k], vq_ref.at[f ^ k], vf_s.at[k], vf_r.at[f ^ k], f, c).wait_recv()
        copy_to(vq_ref.at[f], vq_ref.at[f], vf_s.at[k], vf_r.at[f], f, c).wait_send()
    for one in (gather_one, gather_in):
        one.got(f ^ 1)
        one.got(f ^ 3)
        one.sent()
    local_one.wait()
    local_in.wait()
    share_two.finish()
    share_out.finish()
    for one in big + (sum_in,):
        one.sent()
    in_sum.sent()

    def drain(i, _):
        @pl.when(i * groups + own_turn != c)
        def _():
            copy_to(da_ref.at[i], do_ref.at[0], da_s.at[i], da_r.at[0], f, c).wait_send()

        @pl.when(block_of(turn, i, groups) != c)
        def _():
            copy_to(dqs_ref.at[i], dq_ref.at[0], dq_s.at[i], dq_r.at[0], f, c).wait_send()

        return 0

    lax.fori_loop(0, 4, drain, 0)


def cuts(count):
    parts = max(1, count // 128)
    return parts if count % (16 * parts) == 0 else 1


def line_sum_scratch(blocks, subs, rows, cols):
    return [
        pltpu.VMEM((blocks * subs, rows // subs, cols), BF16), pltpu.VMEM(((blocks + 1) * subs, rows // subs, cols), BF16),
        pltpu.VMEM((blocks * subs, rows // subs, cols), BF16),
        DMA((blocks * subs,)), DMA((blocks * subs,)), DMA((blocks * subs,)), DMA(((blocks + 1) * subs,)),
    ]


def back(n, da, gwout, gw1, gw2, qcat, qpos, kv, lse, of, tok, p1, ev, gates, gsel, x, small, dmid, vec, table):
    t, d = x.shape
    g = n // 4
    quarter = gw1.shape[1]
    rows, out_rows, two_rows = d // n, gwout.shape[1], gw2.shape[1]
    sub_out, sub_two = cuts(out_rows), cuts(two_rows)
    lone = n // 8
    far_kv = g > 4
    return pl.pallas_call(
        functools.partial(back_kernel, n, far_kv),
        out_shape=[
            sds((t, d), F32), sds((4, rows, d), BF16), sds((4, rows, quarter), BF16),
            sds((sub_two, two_rows // sub_two, d), BF16), sds((sub_out, out_rows // sub_out, d), BF16),
            sds((4, 8, d), F32), sds((n, t, 256), BF16),
        ],
        in_specs=[VMEM] * 19,
        out_specs=[VMEM, ANY, ANY, ANY, ANY, VMEM, ANY if far_kv else VMEM],
        scratch_shapes=[
            pltpu.VMEM((4, t, LANES), BF16), pltpu.VMEM((4, t, 1), F32), pltpu.VMEM((4, t, d + LANES), F32),
            pltpu.VMEM((t, d + LANES), BF16), pltpu.VMEM((t, 256), F32), pltpu.VMEM((4, t, 256), BF16),
            pltpu.VMEM((4, t, d), BF16), pltpu.VMEM((4, t, LANES), BF16), pltpu.VMEM((4, t, LANES), BF16),
            pltpu.VMEM((t, 256), BF16), pltpu.VMEM((4, t, 896), BF16), pltpu.VMEM((d, d), BF16),
            pltpu.VMEM((8, d), F32), pltpu.VMEM((n, 8, d), F32),
        ]
        + quad_sum_scratch(t, d)
        + line_sum_scratch(lone, sub_out, out_rows, d)
        + line_sum_scratch(n // 2, 1, rows, quarter)
        + line_sum_scratch(lone, sub_two, two_rows, d)
        + line_sum_scratch(n // 2, 1, rows, d)
        + [
            DMA((4,)), DMA((4,)), DMA((4,)), DMA((n,)), DMA((4,)), DMA((4,)), DMA((3,)), DMA((4,)),
            DMA((3,)), DMA((4,)), DMA((2,)), DMA, DMA((2,)), DMA, DMA((n,)), DMA((n,)), DMA((4,)), DMA((4,)), DMA((2,)),
        ],
        compiler_params=pltpu.CompilerParams(
            collective_id=2, has_side_effects=True, vmem_limit_bytes=63 << 20
        ),
        name="back",
    )(da, gwout, gw1, gw2, qcat, qpos, kv, lse, of, tok, p1, ev, gates, gsel, x, small, dmid, vec, table)


def pad_channels(v, group):
    lead = v.shape[:-1]
    v = v.reshape(lead + (112 // group, group))
    v = jnp.pad(v, [(0, 0)] * len(lead) + [(0, 0), (0, group // 7)])
    return v.reshape(lead + (LANES,))


def head_pick(w, f, heads=4):
    w = w.reshape(w.shape[0], heads, -1)
    return lax.dynamic_index_in_dim(w, f, 1, keepdims=False)


def route_lanes(routes):
    hot = routes[..., None] == jnp.arange(8, dtype=jnp.int32)
    return jnp.sum(hot.astype(F32), axis=-2)


def pack_inputs(
    n, f, positions, value_routes, output_routes, ln1_gain, ln1_bias, wq, wk, wrel, u_bias, v_bias,
    wvsel, wv, wosel, wout, ln2_gain, ln2_bias, b1, b2,
):
    t = positions.shape[0]
    rows = wq.shape[0]
    group = math.gcd(112, wout.shape[0])
    masks = jnp.concatenate([route_lanes(value_routes), route_lanes(output_routes)], axis=-1).reshape(t, 64)
    place = jnp.stack([positions // 128, positions % 128], axis=-1).astype(F32)
    aux = jnp.concatenate([masks, place, jnp.zeros((t, 62), F32)], axis=-1).astype(BF16)
    lane = jnp.arange(LANES)
    experts = pad_channels(head_pick(wv, f).reshape(rows, 5, 112), group)
    experts = jnp.where(lane == SPOT_A, head_pick(wvsel, f)[..., None], experts)
    experts = jnp.where(lane == SPOT_B, head_pick(wosel, f)[..., None], experts)
    p1 = jnp.concatenate(
        [
            pad_channels(head_pick(wq, f), group), pad_channels(head_pick(wk, f), group),
            experts.reshape(rows, 640), pad_channels(head_pick(wrel, f), group),
        ],
        axis=-1,
    )
    piece = min(LANES, b1.shape[0])
    vectors = [ln1_gain, ln1_bias, ln2_gain, ln2_bias, b2]
    vectors = [jnp.pad(v, (0, LANES - v.shape[0])) for v in vectors]
    extra = jnp.pad(b1.reshape(-1, piece), ((0, 0), (0, LANES - piece)))
    small = jnp.concatenate([jnp.stack(vectors), extra]).astype(F32)
    small = jnp.pad(small, ((0, 16 - small.shape[0]), (0, 0)))
    pieces = wout.reshape(-1, group, wout.shape[1])
    pieces = jnp.pad(pieces, ((0, 0), (0, group // 7), (0, 0))).reshape(-1, wout.shape[1])
    pieces = jnp.pad(pieces, ((0, -pieces.shape[0] % 16), (0, 0)))
    bias = jnp.concatenate([pad_channels(u_bias, group), pad_channels(v_bias, group)]).astype(F32)
    return aux, p1, small, pieces, bias


def drop_pads(v, group):
    lead = v.shape[:-1]
    wide = group * 8 // 7
    return v.reshape(lead + (LANES // wide, wide))[..., :group].reshape(lead + (112,))


def on_device(n, *args):
    (
        x, positions, value_routes, output_routes, ln1_gain, ln1_bias, wq, wk, wrel, u_bias, v_bias,
        wvsel, wv, wosel, wout, ln2_gain, ln2_bias, w1, b1, w2, b2, cot,
    ) = args
    f, c = lax.axis_index("fsdp"), lax.axis_index("ctx")
    d = x.shape[1]
    g = n // 4
    group = math.gcd(112, wout.shape[0])
    aux, p1, small, pieces, bias = pack_inputs(
        n, f, positions, value_routes, output_routes, ln1_gain, ln1_bias, wq, wk, wrel, u_bias, v_bias,
        wvsel, wv, wosel, wout, ln2_gain, ln2_bias, b1, b2,
    )
    table = jnp.asarray(turn_table(d))
    tok, p1g, smallg, woutg, cotg, ev, gates, o, qcat, qpos, kv, lse, of = attend(
        n, x, aux, cot, p1, small, pieces, bias, table
    )
    block = 640 // g
    out, dmid, gwout, gw1, gw2, da, gsel, vec = feed(
        n, x, cotg, gates, o, woutg[:, :block].reshape(640, d), smallg, w1, w2
    )
    gwout = gwout.reshape(g, block, d)
    gwout = jnp.pad(gwout, ((0, 0), (0, pieces.shape[0] - block), (0, 0)))
    d_in, gp, g1, g2, go, vq, _ = back(
        n, da, gwout, gw1, gw2.reshape(g, -1, d), qcat, qpos, kv, lse, of, tok, p1g, ev, gates, gsel,
        x, smallg, dmid, vec, table,
    )
    gp = jnp.transpose(gp, (1, 0, 2))
    rows = gp.shape[0]
    g_query = drop_pads(gp[..., 0:128], group).reshape(rows, 448).astype(F32)
    g_key = drop_pads(gp[..., 128:256], group).reshape(rows, 448).astype(F32)
    g_rel = drop_pads(gp[..., 896:], group).reshape(rows, 448).astype(F32)
    experts = gp[..., 256:896].reshape(rows, 4, 5, LANES)
    g_value = drop_pads(experts, group).reshape(rows, 2240).astype(F32)
    g_vsel = experts[..., SPOT_A].reshape(rows, 20).astype(F32)
    g_osel = experts[..., SPOT_B].reshape(rows, 20).astype(F32)
    g_one = jnp.transpose(g1, (1, 0, 2)).reshape(rows, -1).astype(F32)
    g_two = g2.reshape(-1, d).astype(F32)
    g_out = go.reshape(-1, d)[:block].reshape(-1, group * 8 // 7, d)[:, :group].reshape(-1, d).astype(F32)
    sums = jnp.sum(vq, axis=0)
    own = lax.dynamic_slice_in_dim(sums, c * rows, rows, 1)
    b1_rows = b1.shape[0]
    g_b1 = lax.dynamic_slice_in_dim(vq[:, 3, :].reshape(-1), c * b1_rows, b1_rows, 0)
    g_u = drop_pads(vq[:, 6, 0:LANES], group)
    g_v = drop_pads(vq[:, 7, 0:LANES], group)
    return (
        out, d_in, own[4], own[5], g_query, g_key, g_rel, g_u, g_v, g_vsel, g_value, g_osel, g_out,
        own[0], own[1], g_one, g_b1, g_two, own[2],
    )


def solution(mesh):
    both = ("fsdp", "ctx")
    row, vector, matrix = P(both, None), P("ctx"), P("ctx", None)
    in_specs = (
        row, P(both), P(both, None, None), P(both, None, None), vector, vector, matrix, matrix, matrix,
        P(), P(), matrix, matrix, matrix, matrix, vector, vector, matrix, vector, matrix, vector, row,
    )
    out_specs = (
        row, row, vector, vector, matrix, matrix, matrix, P(), P(), matrix, matrix, matrix, matrix,
        vector, vector, matrix, vector, matrix, vector,
    )
    return jax.shard_map(
        functools.partial(on_device, mesh.shape["ctx"]),
        mesh=mesh, in_specs=in_specs, out_specs=out_specs, check_vma=False,
    )
```

time: 2140 us -> 514 us (0.24)
  waiting for transfers between devices: 1530 us -> 0 us
  Pallas kernels: 0 us -> 473 us
  blocking collectives: 346 us -> 0 us
  matrix products: 111 us -> 0 us
  other arithmetic: 71.4 us -> 12.9 us
  local copies, waits for them, and re-layouts: 54.4 us -> 19.9 us
    reduce_scatter x10 -> x0, waiting for transfers between devices: 1220 us -> none  [the longest x1 283 us: on_device(): lax.psum_scatter(grad_ffn_out, 'ctx', scatter_dimension=0, tiled=True)]
    pallas_call x0 -> x3, Pallas kernels: none -> 473 us  [the longest x1 250 us: back(): pl.pallas_call(functools.partial(back_kernel, n, far_kv), out_shape=[sds(...]
    all_gather x12 -> x0, blocking collectives: 262 us -> none  [the longest x1 44.4 us: on_device(): lax.all_gather(relative_weight, 'ctx', axis=0, tiled=True)]
    all_gather x6 -> x0, waiting for transfers between devices: 238 us -> none  [the longest x1 119 us: on_device(): lax.all_gather(feedforward_out_weight2, 'ctx', axis=0, tiled=True)]
    dot_general x37 -> x0, matrix products: 111 us -> none  [the longest x1 12.9 us: on_device(): jnp.dot(normed_two_low, feedforward_in_matrix, preferred_element_type=sin...]
    psum x1 -> x0, waiting for transfers between devices: 66.4 us -> none  [on_device(): lax.psum(seq_owned[2].astype(jnp.bfloat16), 'fsdp').astype(jnp.float32)]
    psum x2 -> x0, blocking collectives: 59 us -> none  [the longest x1 48.1 us: on_device(): bias_sums = lax.psum((grad_ubias, grad_vbias), ('fsdp', 'ctx'))]
    convert_element_type x42 -> x9, other arithmetic: 35.3 us -> 8.17 us  [the longest x1 1.63 us: on_device(): g_two = g2.reshape(-1, d).astype(F32)]
  transfers between devices with their start and end apart: 17 -> 0, of which waited for: 13 -> 0; matrix products, arithmetic and copies ran while one was open for 7% -> 0% of each run, Pallas kernels for 0% -> 0%
where the time goes in v1:
time: 514 us; the launch traced here: 508 us
  Pallas kernels  473 us (92%)
  local copies, waits for them, and re-layouts  19.9 us (4%)
  other arithmetic  12.9 us (3%)
    pallas_call x1, Pallas kernels, back(): pl.pallas_call(functools.partial(back_kernel, n, far_kv), out_shape=[sds(...  250 us
    pallas_call x1, Pallas kernels, feed(): pl.pallas_call(functools.partial(feed_kernel, n), out_shape=[sds((t, d),...  119 us
    pallas_call x1, Pallas kernels, attend(): pl.pallas_call(functools.partial(attend_kernel, n), out_shape=[sds((4, t,...  104 us

profile of v1, /device:TPU:15, one launch (start us, length us, event | category | flops | bytes accessed | tf_op | source)
XLA Modules:
  0.0 507.6 jit_solution(17760796752423931823)
XLA Ops:
  0.7 0.7 and_select_fusion.1
  1.7 0.8 convert_reduce_fusion
  2.7 0.7 maximum_maximum_fusion.aux_ref
  3.4 0.8 constant_dynamic-slice_fusion.1
  6.6 0.8 constant_dynamic-slice_fusion.4
  7.4 0.7 pad_maximum_fusion.p1_ref
  8.9 0.9 pad.37
  10.8 104.2 %attend.1 = (bf16[4,256,1152]{2,1,0:T(8,128)(2,1)}, bf16[8,128,1024]{2,1,0:T(8,128)(2,1)}, f32[8,16,128]{2,1,0:T(8,128)}, bf16[2,320,1024]{2,1,0:T(8,128)(2,1)},...) custom-call(bf16[256,1024]{1,0:T(8,128)(2,1)} %x_ref.5, ...), custom_call_target="tpu_custom_call" | custom-call | tf_op jit(solution)/shard_map/attend/pallas_call | solution.py:481
  115.1 119.2 %feed.1 = (bf16[256,1024]{1,0:T(8,128)(2,1)}, f32[256,1024]{1,0:T(8,128)}, bf16[640,1024]{1,0:T(8,128)(2,1)}, bf16[1024,1024]{1,0:T(8,128)(2,1)}, bf16[1024,1024...) custom-call(bf16[256,1024]{1,0:T(8,128)(2,1)} %x_ref.5, ...), custom_call_target="tpu_custom_call" | custom-call | tf_op jit(solution)/shard_map/feed/pallas_call | solution.py:742
  234.3 249.9 %back.1 = (f32[256,1024]{1,0:T(8,128)}, bf16[4,128,1024]{2,1,0:T(8,128)(2,1)}, bf16[4,128,1024]{2,1,0:T(8,128)(2,1)}, bf16[4,128,1024]{2,1,0:T(8,128)(2,1)}, bf1...) custom-call(bf16[4,256,128]{2,1,0:T(8,128)(2,1)} %get-tuple-element.52.da_ref, ...), custom_call_target="tpu_custom_call" | custom-call | tf_op jit(solution)/shard_map/back/pallas_call | solution.py:1269
  484.2 1.0 reduce_sum.29
  485.8 1.1 fusion.3
  487.0 0.7 bitcast_convert_fusion.5
  487.9 0.7 bitcast_convert_fusion.4
  489.4 0.8 slice_reduce_fusion
  492.9 1.1 bitcast_convert_fusion.2
  494.7 1.2 bitcast_convert_fusion.1
  495.8 1.5 convert_bitcast_fusion
  497.3 1.8 copy.102
  499.1 3.0 copy.103
  502.1 1.0 slice.82
  503.7 1.6 bitcast_convert_fusion
  505.4 0.8 copy.108
  506.1 1.0 copy.109
  (86 shorter events, 10.1 us)
Async XLA Ops:
  0.7 5.5 %copy-start = (bf16[128,2240]{0,1:T(8,128)(2,1)S(1)}, bf16[128,2240]{0,1:T(8,128)(2,1)}, u32[]{:S(2)}) copy-start(bf16[128,2240]{0,1:T(8,128)(2,1)} %param.35) | copy-start | bytes 1720324
  1.6 6.6 %copy-start.7 = (bf16[512]{0:T(512)(128)(2,1)S(1)}, bf16[512]{0:T(512)(128)(2,1)}, u32[]{:S(2)}) copy-start(bf16[512]{0:T(512)(128)(2,1)} %param.41) | copy-start | bytes 3076
  1.6 6.6 %copy-start.10 = (bf16[128]{0:T(256)(128)(2,1)S(1)}, bf16[128]{0:T(256)(128)(2,1)}, u32[]{:S(2)}) copy-start(bf16[128]{0:T(256)(128)(2,1)} %param.27) | copy-start | bytes 772
  1.6 6.6 %copy-start.11 = (bf16[128]{0:T(256)(128)(2,1)S(1)}, bf16[128]{0:T(256)(128)(2,1)}, u32[]{:S(2)}) copy-start(bf16[128]{0:T(256)(128)(2,1)} %param.28) | copy-start | bytes 772
  1.6 6.6 %copy-start.12 = (bf16[128]{0:T(256)(128)(2,1)S(1)}, bf16[128]{0:T(256)(128)(2,1)}, u32[]{:S(2)}) copy-start(bf16[128]{0:T(256)(128)(2,1)} %param.38) | copy-start | bytes 772
  1.6 6.6 %copy-start.13 = (bf16[128]{0:T(256)(128)(2,1)S(1)}, bf16[128]{0:T(256)(128)(2,1)}, u32[]{:S(2)}) copy-start(bf16[128]{0:T(256)(128)(2,1)} %param.39) | copy-start | bytes 772
  1.6 6.6 %copy-start.14 = (bf16[128]{0:T(256)(128)(2,1)S(1)}, bf16[128]{0:T(256)(128)(2,1)}, u32[]{:S(2)}) copy-start(bf16[128]{0:T(256)(128)(2,1)} %param.43) | copy-start | bytes 772
  1.6 7.3 %copy-start.4 = (bf16[280,1024]{1,0:T(8,128)(2,1)S(1)}, bf16[280,1024]{1,0:T(8,128)(2,1)}, u32[]{:S(2)}) copy-start(bf16[280,1024]{1,0:T(8,128)(2,1)} %param.37) | copy-start | bytes 1720324
  5.9 3.9 copy-start.8
  5.9 4.1 copy-start.9
  484.2 7.5 %copy-start.2 = (bf16[4,128,1024]{2,1,0:T(8,128)(2,1)S(1)}, bf16[4,128,1024]{2,1,0:T(8,128)(2,1)}, u32[]{:S(2)}) copy-start(bf16[4,128,1024]{2,1,0:T(8,128)(2,1)} %get-tuple-element.69) | copy-start | bytes 3145732
  491.8 2.8 copy-start.6
  499.1 4.6 copy-start.1
  502.1 3.3 copy-start.5
  503.7 2.4 copy-start.3

commit v2 on v1

--- a/solution.py
+++ b/solution.py
@@ -90,12 +90,12 @@
 
 
 class LineGather:
-    def __init__(self, f, c, n, own, at, recv, right, left, pair, lone=False):
+    def __init__(self, f, c, n, own, at, recv, right, left, pair, subs=1, lone=False):
         self.f, self.c, self.n, self.size = f, c, n, n // 2
         self.place, self.bit = c // 2, lax.rem(c, 2)
         self.own, self.at = own, at
         self.recv, self.right, self.left, self.pair = recv, right, left, pair
-        self.lone = lone
+        self.subs, self.lone = subs, lone
 
     def valid(self, o):
         ok = jnp.logical_and(o >= 0, o < self.size)
@@ -107,30 +107,43 @@
     def slot(self, block):
         return block - self.f * (self.n // 4) if self.lone else block
 
-    def copy(self, src, block, sems, c):
+    def copy(self, src, block, sub, sems, c):
         slot = self.slot(block)
-        return copy_to(src, self.at(slot), sems.at[slot], self.recv.at[slot], self.f, c)
-
-    def spread(self, src, block, go_right, go_left):
+        i = slot * self.subs + sub
+        return copy_to(src, self.at(slot, sub), sems.at[i], self.recv.at[i], self.f, c)
+
+    def held(self, block, sub):
+        return self.at(self.slot(block), sub)
+
+    def each(self, work):
+        if self.subs == 1:
+            work(0)
+        else:
+            lax.fori_loop(0, self.subs, lambda sub, u: (work(sub), u)[1], 0)
+
+    def spread(self, src, block, sub, go_right, go_left):
         @pl.when(go_right)
         def _():
-            self.copy(src, block, self.right, self.c + 2).start()
+            self.copy(src, block, sub, self.right, self.c + 2).start()
 
         @pl.when(go_left)
         def _():
-            self.copy(src, block, self.left, self.c - 2).start()
-
-        self.copy(src, block, self.pair, self.c + 1 - 2 * self.bit).start()
+            self.copy(src, block, sub, self.left, self.c - 2).start()
+
+        self.copy(src, block, sub, self.pair, self.c + 1 - 2 * self.bit).start()
 
     def begin(self, local):
         @pl.when(self.valid(self.place))
         def _():
-            self.spread(self.own, self.c, self.place < self.size - 1, self.place > 0)
+            self.each(
+                lambda sub: self.spread(
+                    self.own(sub), self.c, sub, self.place < self.size - 1, self.place > 0
+                )
+            )
             local()
 
-    def arrived(self, block):
-        slot = self.slot(block)
-        self.copy(self.at(slot), block, self.pair, self.c).wait_recv()
+    def arrived(self, block, sub):
+        self.copy(self.held(block, sub), block, sub, self.pair, self.c).wait_recv()
 
     def step(self, t):
         for sign in (-1, 1):
@@ -139,33 +152,39 @@
 
             @pl.when(self.valid(o))
             def _():
-                self.arrived(block)
-                self.spread(
-                    self.at(self.slot(block)),
-                    block,
-                    jnp.logical_and(sign < 0, self.place < self.size - 1),
-                    jnp.logical_and(sign > 0, self.place > 0),
-                )
-
-    def steps(self):
-        lax.fori_loop(1, self.size, lambda t, u: (self.step(t), u)[1], 0)
+                def one(sub):
+                    self.arrived(block, sub)
+                    self.spread(
+                        self.held(block, sub), block, sub,
+                        jnp.logical_and(sign < 0, self.place < self.size - 1),
+                        jnp.logical_and(sign > 0, self.place > 0),
+                    )
+
+                self.each(one)
+
+    def steps(self, first=1):
+        lax.fori_loop(first, self.size, lambda t, u: (self.step(t), u)[1], 0)
 
     def finish(self):
         def one(o, _):
+            block = 2 * o + self.bit
+
+            def piece(sub):
+                self.arrived(2 * o + 1 - self.bit, sub)
+                source = self.held(block, sub)
+                self.copy(source, block, sub, self.pair, self.c).wait_send()
+
+                @pl.when(jnp.logical_and(o <= self.place, self.place < self.size - 1))
+                def _():
+                    self.copy(source, block, sub, self.right, self.c).wait_send()
+
+                @pl.when(jnp.logical_and(o >= self.place, self.place > 0))
+                def _():
+                    self.copy(source, block, sub, self.left, self.c).wait_send()
+
             @pl.when(self.valid(o))
             def _():
-                self.arrived(2 * o + 1 - self.bit)
-                block = 2 * o + self.bit
-                source = self.at(self.slot(block))
-                self.copy(source, block, self.pair, self.c).wait_send()
-
-                @pl.when(jnp.logical_and(o <= self.place, self.place < self.size - 1))
-                def _():
-                    self.copy(source, block, self.right, self.c).wait_send()
-
-                @pl.when(jnp.logical_and(o >= self.place, self.place > 0))
-                def _():
-                    self.copy(source, block, self.left, self.c).wait_send()
+                self.each(piece)
 
             return 0
 
@@ -223,12 +242,12 @@
 
 def attend_kernel(
     n,
-    x_ref, aux_ref, cot_ref, p1_ref, small_ref, wout_ref, bias_ref, table_ref,
-    tok_ref, p1g_ref, smallg_ref, woutg_ref, cotg_ref, ev_ref, gates_ref, o_ref,
+    x_ref, aux_ref, cot_ref, p1_ref, small_ref, wout_ref, w1_ref, bias_ref, table_ref,
+    tok_ref, p1g_ref, smallg_ref, woutg_ref, w1g_ref, cotg_ref, ev_ref, gates_ref, o_ref,
     qcat_ref, qpos_ref, kv_ref, lse_ref, of_ref,
     qs_ref, kvs_ref, qr_ref, os_ref, kcat_ref, m_ref, l_ref,
-    sm_s, sm_r, p_r, p_a, p_b, p_c, w_r, w_a, w_b, w_c,
-    t_s, t_r, c_s, c_r, q_s, q_r, kv_s, kv_r, o_s, o_r, loc,
+    sm_s, sm_r, p_r, p_a, p_b, p_c, w_r, w_a, w_b, w_c, h_r, h_a, h_b, h_c,
+    t_s, t_r, c_s, c_r, q_s, q_r, kv_s, kv_r, kv_p, o_s, o_r, loc,
 ):
     f, c = lax.axis_index("fsdp"), lax.axis_index("ctx")
     groups = n // 4
@@ -244,14 +263,23 @@
 
     lax.fori_loop(1, n, small_send, 0)
     smallg_ref[c] = small_ref[...]
-    gather_p = LineGather(f, c, n, p1_ref, lambda k: p1g_ref.at[k], p_r, p_a, p_b, p_c)
+    gather_p = LineGather(f, c, n, lambda sub: p1_ref, lambda k, sub: p1g_ref.at[k], p_r, p_a, p_b, p_c)
 
     def own_p():
         p1g_ref[c] = p1_ref[...]
 
     gather_p.begin(own_p)
     wout_copy = pltpu.make_async_copy(wout_ref, woutg_ref.at[c - f * groups], loc.at[0])
-    gather_w = LineGather(f, c, n, wout_ref, lambda k: woutg_ref.at[k], w_r, w_a, w_b, w_c, lone=True)
+    subs = w_r.shape[0] // groups
+    piece = wout_ref.shape[0] // subs
+    gather_w = LineGather(
+        f, c, n,
+        lambda sub: wout_ref.at[pl.ds(pl.multiple_of(sub * piece, piece), piece), :],
+        lambda k, sub: woutg_ref.at[k, pl.ds(pl.multiple_of(sub * piece, piece), piece), :],
+        w_r, w_a, w_b, w_c, subs=subs, lone=True,
+    )
+    w1_copy = pltpu.make_async_copy(w1_ref, w1g_ref.at[c], loc.at[2])
+    gather_h = LineGather(f, c, n, lambda sub: w1_ref, lambda k, sub: w1g_ref.at[k], h_r, h_a, h_b, h_c)
     cot_copy = pltpu.make_async_copy(cot_ref, cotg_ref.at[f], loc.at[1])
     cot_copy.start()
 
@@ -274,7 +302,6 @@
     tok_gather.begin()
     gather_p.steps()
     tok_gather.relay()
-    gather_w.begin(wout_copy.start)
     gather_p.finish()
     tok_gather.got(f ^ 1)
     tok_gather.got(f ^ 3)
@@ -290,6 +317,8 @@
         jnp.logical_and(source == wanted, jnp.logical_and(target < 32, lax.rem(target, 8) < 5)), 1.0, 0.0
     ).astype(BF16)
     own_turn, own_slot = holder_of(c, groups)
+    bit = lax.rem(c, 2)
+    spots = jnp.logical_or(lane == SPOT_A, lane == SPOT_B)
 
     def project(t, _):
         s = lax.rem(seq + 1 + t, 4)
@@ -312,12 +341,14 @@
         values = jnp.zeros((tokens, LANES), F32)
         for e in range(5):
             values = values + gates[:, 16 + e : 17 + e] * experts[:, e * LANES : (e + 1) * LANES]
-        spots = jnp.logical_or(lane == SPOT_A, lane == SPOT_B)
         values = jnp.where(spots, 0.0, values)
-        keys = jnp.where(lane == SPOT_A, aux[:, 64:65].astype(F32), qk[:, 128:256])
-        keys = jnp.where(lane == SPOT_B, aux[:, 65:66].astype(F32), keys)
-        qs_ref[s] = qk[:, 0:128].astype(BF16)
-        kvs_ref[s, :, 0:128] = keys.astype(BF16)
+        high, rest = aux[:, 64:65].astype(F32), aux[:, 65:66].astype(F32)
+
+        def with_place(v):
+            return jnp.where(lane == SPOT_A, high, jnp.where(lane == SPOT_B, rest, v)).astype(BF16)
+
+        qs_ref[s] = with_place(qk[:, 0:128])
+        kvs_ref[s, :, 0:128] = with_place(qk[:, 128:256])
         kvs_ref[s, :, 128:256] = values.astype(BF16)
         to = s * groups + own_turn
 
@@ -330,7 +361,7 @@
             qr_ref[own_slot] = qs_ref[s]
 
         def kv_send(k, _):
-            to = s * groups + k
+            to = s * groups + 2 * k + bit
 
             @pl.when(to != c)
             def _():
@@ -342,15 +373,27 @@
 
             return 0
 
-        lax.fori_loop(0, groups, kv_send, 0)
+        lax.fori_loop(0, groups // 2, kv_send, 0)
         return 0
 
     lax.fori_loop(0, 4, project, 0)
+    gather_w.begin(wout_copy.start)
+    gather_h.begin(w1_copy.start)
 
     def kv_wait(block):
+        copy_to(kvs_ref.at[0], kv_ref.at[block], kv_s.at[0], kv_r.at[block], f, c).wait_recv()
+
+    def kv_pass(block):
+        return copy_to(kv_ref.at[block], kv_ref.at[block], kv_p.at[block // 2], kv_r.at[block], f, c + 1 - 2 * bit)
+
+    def hand_on(m):
+        block = 2 * m + bit
+
         @pl.when(block != c)
         def _():
-            copy_to(kvs_ref.at[0], kv_ref.at[block], kv_s.at[block], kv_r.at[block], f, c).wait_recv()
+            kv_wait(block)
+
+        kv_pass(block).start()
 
     def prepare(i, _):
         block = block_of(turn, i, groups)
@@ -359,14 +402,14 @@
         def _():
             copy_to(qs_ref.at[0], qr_ref.at[i], q_s.at[0], q_r.at[i], f, c).wait_recv()
 
-        kv_wait(block)
-        query = qr_ref[i].astype(F32)
+        places = key_places(qr_ref[i])
+        query = jnp.where(spots, 0.0, qr_ref[i].astype(F32))
         q_position = (query + bias_ref[pl.ds(4 + f, 1), :]).astype(BF16)
         qpos_ref[i] = q_position
         qcat_ref[i, :, width:] = ((query + bias_ref[pl.ds(f, 1), :]) * scale).astype(BF16)
         rel = p1g_ref[:, :, 896:].reshape(width, LANES)
         rel_query = mm_t(q_position, rel)
-        sine, cosine = sin_cos(key_places(kv_ref[block]), table_ref)
+        sine, cosine = sin_cos(places, table_ref)
         first, second = rel_query[:, : width // 2], rel_query[:, width // 2 :]
         qcat_ref[i, :, 0 : width // 2] = ((first * sine + second * cosine) * scale).astype(BF16)
         qcat_ref[i, :, width // 2 : width] = ((second * sine - first * cosine) * scale).astype(BF16)
@@ -376,17 +419,38 @@
         return 0
 
     lax.fori_loop(0, 4, prepare, 0)
+    hand_on(0)
     row_in = lax.broadcasted_iota(jnp.int32, (tokens, tokens), 0)
     col_in = lax.broadcasted_iota(jnp.int32, (tokens, tokens), 1)
+
+    def give(i):
+        total = l_ref[i]
+        result = of_ref[i] / total
+        of_ref[i] = result
+        lse_ref[i] = m_ref[i] + jnp.log(total)
+        os_ref[i] = result.astype(BF16)
+        block = block_of(turn, i, groups)
+
+        @pl.when(block != c)
+        def _():
+            copy_to(os_ref.at[i], o_ref.at[seq], o_s.at[i], o_r.at[seq], f, block).start()
+
+        @pl.when(block == c)
+        def _():
+            o_ref[seq] = os_ref[i]
 
     def key_block(kb, _):
         own = [block_of(turn, i, groups) for i in range(4)]
         first = sum((b < kb).astype(jnp.int32) for b in own)
         ready = sum((b == kb).astype(jnp.int32) for b in own)
 
-        @pl.when(ready == 0)
+        @pl.when(lax.rem(kb, 2) != bit)
         def _():
             kv_wait(kb)
+
+        @pl.when(jnp.logical_and(lax.rem(kb, 2) == 0, kb < n - 2))
+        def _():
+            hand_on(kb // 2 + 1)
 
         sine, cosine = sin_cos(key_places(kv_ref[kb]), table_ref)
         kcat_ref[:, 0 : width // 2] = cosine.astype(BF16)
@@ -407,35 +471,29 @@
             return 0
 
         lax.fori_loop(first, 4, query_block, 0)
+
+        @pl.when(ready == 1)
+        def _():
+            give(first)
+
+        @pl.when(kb == n // 2 - 1)
+        def _():
+            cot_gather.relay()
+
+        @pl.when(jnp.logical_and(kb >= n // 2, kb < n - 1))
+        def _():
+            gather_w.step(kb - n // 2 + 1)
+            gather_h.step(kb - n // 2 + 1)
+
         return 0
 
     lax.fori_loop(0, n, key_block, 0)
-
-    def give(i, _):
-        block = block_of(turn, i, groups)
-        total = l_ref[i]
-        result = of_ref[i] / total
-        of_ref[i] = result
-        lse_ref[i] = m_ref[i] + jnp.log(total)
-        os_ref[i] = result.astype(BF16)
-
-        @pl.when(block != c)
-        def _():
-            copy_to(os_ref.at[i], o_ref.at[seq], o_s.at[i], o_r.at[seq], f, block).start()
-
-        @pl.when(block == c)
-        def _():
-            o_ref[seq] = os_ref[i]
-
-        return 0
-
-    lax.fori_loop(0, 4, give, 0)
-    gather_w.steps()
-    cot_gather.relay()
     cot_gather.got(f ^ 1)
     cot_gather.got(f ^ 3)
     cot_gather.sent()
     gather_w.finish()
+    gather_h.finish()
+    w1_copy.wait()
 
     @pl.when(gather_w.valid(c // 2))
     def _():
@@ -459,49 +517,54 @@
 
     lax.fori_loop(0, 4, drain, 0)
 
-    def kv_drain(to, _):
+    def kv_drain(k, _):
+        to = 2 * k + bit
+
         @pl.when(to != c)
         def _():
             copy_to(kvs_ref.at[0], kv_ref.at[0], kv_s.at[to], kv_r.at[0], f, c).wait_send()
 
-        return 0
-
-    lax.fori_loop(0, n, kv_drain, 0)
+        kv_pass(to).wait_send()
+        return 0
+
+    lax.fori_loop(0, n // 2, kv_drain, 0)
 
 
 def sds(shape, dtype):
     return jax.ShapeDtypeStruct(shape, dtype)
 
 
-def attend(n, x, aux, cot, p1, small, wout, bias, table):
+def attend(n, x, aux, cot, p1, small, wout, w1, bias, table):
     t, d = x.shape
     rows = p1.shape[0]
     out_rows = wout.shape[0]
     g = n // 4
+    subs = cuts(out_rows)
     return pl.pallas_call(
         functools.partial(attend_kernel, n),
         out_shape=[
             sds((4, t, d + LANES), BF16), sds((n, rows, d), BF16), sds((n, 16, LANES), F32),
-            sds((g, out_rows, d), BF16), sds((4, t, d), BF16), sds((4, t, 640), BF16),
+            sds((g, out_rows, d), BF16), sds((n,) + w1.shape, BF16), sds((4, t, d), BF16), sds((4, t, 640), BF16),
             sds((4, t, LANES), F32), sds((4, t, LANES), BF16), sds((4, t, d + LANES), BF16),
             sds((4, t, LANES), BF16), sds((n, t, 256), BF16), sds((4, t, 1), F32), sds((4, t, LANES), F32),
         ],
-        in_specs=[VMEM, VMEM, ANY, VMEM, VMEM, ANY, VMEM, VMEM],
-        out_specs=[VMEM, VMEM, VMEM, ANY, ANY] + [VMEM] * 8,
+        in_specs=[VMEM, VMEM, ANY, VMEM, VMEM, ANY, ANY, VMEM, VMEM],
+        out_specs=[VMEM, VMEM, VMEM, ANY, ANY, ANY] + [VMEM] * 8,
         scratch_shapes=[
             pltpu.VMEM((4, t, LANES), BF16), pltpu.VMEM((4, t, 256), BF16), pltpu.VMEM((4, t, LANES), BF16),
             pltpu.VMEM((4, t, LANES), BF16), pltpu.VMEM((t, d + LANES), BF16),
             pltpu.VMEM((4, t, 1), F32), pltpu.VMEM((4, t, 1), F32),
             DMA((n,)), DMA((n,)), DMA((n,)), DMA((n,)), DMA((n,)), DMA((n,)),
-            DMA((g,)), DMA((g,)), DMA((g,)), DMA((g,)),
+            DMA((g * subs,)), DMA((g * subs,)), DMA((g * subs,)), DMA((g * subs,)),
+            DMA((n,)), DMA((n,)), DMA((n,)), DMA((n,)),
             DMA((3,)), DMA((4,)), DMA((3,)), DMA((4,)), DMA((4,)), DMA((4,)),
-            DMA((n,)), DMA((n,)), DMA((4,)), DMA((4,)), DMA((2,)),
+            DMA((n,)), DMA((n,)), DMA((n // 2,)), DMA((4,)), DMA((4,)), DMA((3,)),
         ],
         compiler_params=pltpu.CompilerParams(
             collective_id=0, has_side_effects=True, vmem_limit_bytes=56 << 20
         ),
         name="attend",
-    )(x, aux, cot, p1, small, wout, bias, table)
+    )(x, aux, cot, p1, small, wout, w1, bias, table)
 
 
 class QuadSum:
@@ -569,46 +632,191 @@
     return v * half, half + 0.5 * v * (1.0 - t * t) * (k * (1.0 + 3 * 0.044715 * square))
 
 
-def bias_quarter(small_ref, f, n, quarter):
-    span = n // 4
-    shard = quarter // span
-    piece = min(LANES, shard)
-    lane = lax.broadcasted_iota(jnp.int32, (LANES, quarter), 0)
-    column = lax.broadcasted_iota(jnp.int32, (LANES, quarter), 1)
-    onehot = jnp.where(lane == lax.rem(column, piece), 1.0, 0.0).astype(BF16)
-    row = lax.broadcasted_iota(jnp.int32, (span, quarter), 0)
-    column = lax.broadcasted_iota(jnp.int32, (span, quarter), 1)
-    total = jnp.zeros((1, quarter), F32)
-    for k in range(shard // piece):
-        rows = small_ref[pl.ds(f * span, span), 5 + k, :]
-        wide = mm(rows.astype(BF16), onehot)
-        keep = jnp.logical_and(column // shard == row, lax.rem(column, shard) // piece == k)
-        total = total + jnp.sum(jnp.where(keep, wide, 0.0), axis=0, keepdims=True)
-    return total
+class PairSum:
+    def __init__(self, f, c, n, source, got, out, send, recv):
+        self.f, self.c, self.size = f, c, n // 2
+        self.bit = lax.rem(c, 2)
+        self.source, self.got, self.out, self.send, self.recv = source, got, out, send, recv
+
+    def copy(self, o):
+        return copy_to(
+            self.source(2 * o + 1 - self.bit), self.got.at[o], self.send.at[o], self.recv.at[o],
+            self.f, self.c + 1 - 2 * self.bit,
+        )
+
+    def begin(self):
+        lax.fori_loop(0, self.size, lambda o, u: (self.copy(o).start(), u)[1], 0)
+
+    def finish(self):
+        def one(o, _):
+            self.copy(o).wait_recv()
+            term = self.source(2 * o + self.bit)[...].astype(F32)
+            self.out[o] = (term + self.got[o].astype(F32)).astype(BF16)
+            self.copy(o).wait_send()
+            return 0
+
+        lax.fori_loop(0, self.size, one, 0)
+
+
+class LineSum:
+    def __init__(self, f, c, n, source, inbox, stage, line_s, line_r, pair=None, subs=1, lone=False):
+        self.f, self.c, self.n, self.size = f, c, n, n // 2
+        self.place, self.bit = c // 2, lax.rem(c, 2)
+        self.source = source
+        self.inbox, self.stage, self.line_s, self.line_r = inbox, stage, line_s, line_r
+        self.pair = pair
+        self.subs = subs
+        self.span = self.size // 4 if lone else self.size
+        self.first = f * self.span if lone else 0
+
+    def valid(self, o):
+        return jnp.logical_and(o >= self.first, o < self.first + self.span)
+
+    def index(self, o, sub):
+        return (o - self.first) * self.subs + sub
+
+    def pair_copy(self, o, sub):
+        i = self.index(o, sub)
+        got, send, recv = self.pair
+        return copy_to(
+            self.source(2 * (o - self.first) + 1 - self.bit, sub), got.at[i], send.at[i], recv.at[i],
+            self.f, self.c + 1 - 2 * self.bit,
+        )
+
+    def line_copy(self, i, slot, c):
+        return copy_to(self.stage.at[i], self.inbox.at[slot], self.line_s.at[i], self.line_r.at[slot], self.f, c)
+
+    def each(self, work):
+        def one(k, _):
+            work(self.first + k // self.subs, lax.rem(k, self.subs))
+            return 0
+
+        lax.fori_loop(0, self.span * self.subs, one, 0)
+
+    def begin(self):
+        self.each(lambda o, sub: self.pair_copy(o, sub).start())
+
+    def begin_block(self, block):
+        @pl.when(lax.rem(block, 2) != self.bit)
+        def _():
+            self.pair_copy(block // 2, 0).start()
+
+    def term(self, o, sub):
+        if self.pair is None:
+            return self.source(o - self.first, sub)[...].astype(F32)
+        self.pair_copy(o, sub).wait_recv()
+        own = self.source(2 * (o - self.first) + self.bit, sub)[...].astype(F32)
+        return own + self.pair[0][self.index(o, sub)].astype(F32)
+
+    def extra(self, sub):
+        return self.span * self.subs + sub
+
+    def move(self, o, sub, go_right):
+        i = self.index(o, sub)
+        total = self.term(o, sub)
+        starts = self.place == 0 if go_right else self.place == self.size - 1
+
+        @pl.when(starts)
+        def _():
+            self.stage[i] = total.astype(BF16)
+
+        @pl.when(jnp.logical_not(starts))
+        def _():
+            self.line_copy(i, i, self.c).wait_recv()
+            self.stage[i] = (total + self.inbox[i].astype(F32)).astype(BF16)
+
+        if go_right:
+            self.line_copy(i, i, self.c + 2).start()
+        else:
+            slot = jnp.where(o == self.place - 1, self.extra(sub), i)
+            self.line_copy(i, slot, self.c - 2).start()
+
+    def turn(self, time):
+        far = self.size - 1 - (time - self.place)
+        near = time - (self.size - 1 - self.place)
+
+        def one(sub, _):
+            @pl.when(jnp.logical_and(jnp.logical_and(far < self.size, self.valid(far)), far > self.place))
+            def _():
+                self.move(far, sub, True)
+
+            @pl.when(jnp.logical_and(jnp.logical_and(near >= 0, self.valid(near)), near < self.place))
+            def _():
+                self.move(near, sub, False)
+
+            return 0
+
+        lax.fori_loop(0, self.subs, one, 0)
+
+    def settle(self, sub):
+        i = self.index(self.place, sub)
+        own = self.term(self.place, sub)
+        left = self.place > 0
+        right = self.place < self.size - 1
+
+        @pl.when(left)
+        def _():
+            self.line_copy(i, i, self.c).wait_recv()
+
+        @pl.when(right)
+        def _():
+            self.line_copy(i, self.extra(sub), self.c).wait_recv()
+
+        @pl.when(jnp.logical_and(left, right))
+        def _():
+            self.stage[i] = (
+                own + self.inbox[i].astype(F32) + self.inbox[self.extra(sub)].astype(F32)
+            ).astype(BF16)
+
+        @pl.when(jnp.logical_and(left, jnp.logical_not(right)))
+        def _():
+            self.stage[i] = (own + self.inbox[i].astype(F32)).astype(BF16)
+
+        @pl.when(jnp.logical_and(right, jnp.logical_not(left)))
+        def _():
+            self.stage[i] = (own + self.inbox[self.extra(sub)].astype(F32)).astype(BF16)
+
+    def finish(self):
+        @pl.when(self.valid(self.place))
+        def _():
+            lax.fori_loop(0, self.subs, lambda sub, u: (self.settle(sub), u)[1], 0)
+
+    def sent(self):
+        def one(o, sub):
+            if self.pair is not None:
+                self.pair_copy(o, sub).wait_send()
+
+            @pl.when(o != self.place)
+            def _():
+                self.line_copy(self.index(o, sub), 0, self.c).wait_send()
+
+        self.each(one)
 
 
 def feed_kernel(
     n,
-    x_ref, cot_ref, gates_ref, o_ref, wout_ref, small_ref, w1_ref, w2_ref,
-    out_ref, dmid_ref, gwout_ref, gw1_ref, gw2_ref, da_ref, gsel_ref, vec_ref,
-    w1g, w2g, n2_ref, act_ref, slope_ref, dpre_ref, mixed_ref, dml_ref, mid_ref,
+    x_ref, cot_ref, gates_ref, o_ref, wout_ref, small_ref, w1g, w2_ref,
+    out_ref, dmid_ref, gwout_ref, s1_ref, s2_ref, da_ref, gsel_ref, vec_ref,
+    w2g, n2_ref, act_ref, slope_ref, dpre_ref, mixed_ref, dml_ref, mid_ref, gw1_ref, gw2_ref, got1, in2, stage2,
     a0, a1, a2, a3, a4, a5, a6, b0, b1, b2, b3, b4, b5, b6, e0, e1, e2, e3, e4, e5, e6,
-    w1_r, w1_a, w1_b, w1_c, w2_r, w2_a, w2_b, w2_c, n_s, n_r, d_s, d_r, loc,
+    w2_r, w2_a, w2_b, w2_c, h1_s, h1_r, h2_s, h2_r, n_s, n_r, d_s, d_r, loc,
 ):
     f, c = lax.axis_index("fsdp"), lax.axis_index("ctx")
     tokens, width = x_ref.shape
     quarter = w1g.shape[1]
     greet(f, c, 4, n)
-    rows1, rows2 = w1_ref.shape[0], w2_ref.shape[0]
-    own1 = w1_ref.at[:, pl.ds(pl.multiple_of(f * quarter, LANES), quarter)]
-    at1 = lambda k: w1g.at[pl.ds(pl.multiple_of(k * rows1, rows1), rows1), :]
-    at2 = lambda k: w2g.at[pl.ds(pl.multiple_of(k * rows2, rows2), rows2), :]
-    gather1 = LineGather(f, c, n, own1, at1, w1_r, w1_a, w1_b, w1_c)
-    gather2 = LineGather(f, c, n, w2_ref, at2, w2_r, w2_a, w2_b, w2_c, lone=True)
-    local1 = pltpu.make_async_copy(own1, at1(c), loc.at[0])
-    local2 = pltpu.make_async_copy(w2_ref, at2(c - f * (n // 4)), loc.at[1])
-    gather1.begin(local1.start)
+    rows1, rows2 = width // n, quarter // n
+
+    def rows_of(ref, count):
+        return lambda k: ref.at[pl.ds(pl.multiple_of(k * count, count), count), :]
+
+    own2 = w2_ref.at[pl.ds(pl.multiple_of(f * rows2, rows2), rows2), :]
+    at2 = rows_of(w2g, rows2)
+    gather2 = LineGather(f, c, n, lambda sub: own2, lambda k, sub: at2(k), w2_r, w2_a, w2_b, w2_c)
+    local2 = pltpu.make_async_copy(own2, at2(c), loc.at[0])
     gather2.begin(local2.start)
+    pair1 = PairSum(f, c, n, rows_of(gw1_ref, rows1), got1, s1_ref, h1_s, h1_r)
+    line2 = LineSum(f, c, n, lambda o, sub: rows_of(gw2_ref, rows2)(2 * o + sub), in2, stage2, h2_s, h2_r, subs=2)
     attn_sum = QuadSum(f, c, a0, a1, a2, a3, a4, a5, a6)
     back_sum = QuadSum(f, c, b0, b1, b2, b3, b4, b5, b6)
     out_sum = QuadSum(f, c, e0, e1, e2, e3, e4, e5, e6)
@@ -622,7 +830,7 @@
         attn_sum.put(k, mm(mixed_ref[r], wout_ref[...]))
         if k == 2:
             attn_sum.cross()
-    gather1.step(1)
+    gather2.step(1)
     middle = x_ref[...].astype(F32) + attn_sum.total()
     mid_ref[...] = middle
     xhat, scale = layer_stats(middle)
@@ -631,11 +839,7 @@
     n2_ref[f] = (xhat * gain + shift).astype(BF16)
     n2_gather = QuadGather(f, c, n2_ref, n_s, n_r)
     n2_gather.begin()
-    lax.fori_loop(2, n // 2, lambda t, u: (gather1.step(t), u)[1], 0)
-    gather1.finish()
-    local1.wait()
-    gather2.step(1)
-    first_bias = bias_quarter(small_ref, f, n, quarter)
+    first_bias = spread_vector(small_ref[:, pl.ds(5 + f, 1), :].reshape(n, LANES), rows2)
 
     def enter(k):
         r = f ^ k
@@ -643,19 +847,17 @@
         act_ref[r] = act.astype(BF16)
         slope_ref[r] = slope
 
+    gather2.step(2)
     enter(0)
     n2_gather.got(f ^ 1)
+    gather2.steps(3)
     enter(1)
     n2_gather.relay()
     enter(2)
     n2_gather.got(f ^ 3)
     enter(3)
-    lax.fori_loop(2, n // 2, lambda t, u: (gather2.step(t), u)[1], 0)
     gather2.finish()
-
-    @pl.when(gather2.valid(c // 2))
-    def _():
-        local2.wait()
+    local2.wait()
 
     for k in (3, 2, 1, 0):
         r = f ^ k
@@ -680,7 +882,9 @@
         lax.fori_loop(0, left_ref.shape[2] // tile, one, 0)
 
     weight_tile(act_ref, cot_ref, gw2_ref)
+    line2.turn(0)
     weight_tile(n2_ref, dpre_ref, gw1_ref)
+    pair1.begin()
     d_norm = back_sum.total()
     xhat, scale = layer_stats(mid_ref[...])
     d_middle = cot_ref[f].astype(F32) + layer_back(d_norm, gain, xhat, scale)
@@ -713,10 +917,12 @@
         da_ref[r] = d_attn.astype(BF16)
         gsel_ref[r] = select
 
+    line2.turn(1)
     leave(0)
     dml_gather.got(f ^ 1)
     leave(1)
     dml_gather.relay()
+    line2.turn(2)
     leave(2)
     dml_gather.got(f ^ 3)
     leave(3)
@@ -731,167 +937,45 @@
     lax.fori_loop(0, 5, out_tile, 0)
     second_bias = spread_vector(small_ref[:, 4, :], width // n)
     out_ref[...] = (mid_ref[...] + out_sum.total() + second_bias).astype(BF16)
+    lax.fori_loop(3, n // 2 - 1, lambda k, u: (line2.turn(k), u)[1], 0)
+    line2.finish()
+    own = 2 * (c // 2) + lax.rem(c, 2)
+    s2_ref[0] = stage2[own]
+    s2_ref[1] = stage2[own + 1 - 2 * lax.rem(c, 2)]
+    line2.sent()
+    pair1.finish()
     for one in (attn_sum, back_sum, out_sum, n2_gather, dml_gather):
         one.sent()
 
 
 def feed(n, x, cot, gates, o, wout, small, w1, w2):
     t, d = x.shape
-    quarter = w1.shape[1] // 4
-    g = n // 4
+    quarter = w1.shape[1]
+    line = n // 2
     return pl.pallas_call(
         functools.partial(feed_kernel, n),
         out_shape=[
-            sds((t, d), BF16), sds((t, d), F32), sds((640, d), BF16), sds((d, quarter), BF16),
-            sds((quarter, d), BF16), sds((4, t, LANES), BF16), sds((4, t, LANES), F32), sds((8, d), F32),
+            sds((t, d), BF16), sds((t, d), F32), sds((640, d), BF16), sds((line, d // n, quarter), BF16),
+            sds((2, quarter // n, d), BF16), sds((4, t, LANES), BF16), sds((4, t, LANES), F32), sds((8, d), F32),
         ],
-        in_specs=[VMEM] * 6 + [ANY, ANY],
+        in_specs=[VMEM] * 7 + [ANY],
         out_specs=[VMEM] * 8,
         scratch_shapes=[
-            pltpu.VMEM((d, quarter), BF16), pltpu.VMEM((quarter, d), BF16), pltpu.VMEM((4, t, d), BF16),
+            pltpu.VMEM((quarter, d), BF16), pltpu.VMEM((4, t, d), BF16),
             pltpu.VMEM((4, t, quarter), BF16), pltpu.VMEM((4, t, quarter), F32), pltpu.VMEM((4, t, quarter), BF16),
             pltpu.VMEM((4, t, 640), BF16), pltpu.VMEM((4, t, d), BF16), pltpu.VMEM((t, d), F32),
+            pltpu.VMEM((d, quarter), BF16), pltpu.VMEM((quarter, d), BF16),
+            pltpu.VMEM((line, d // n, quarter), BF16),
         ]
+        + line_scratch(line, 2, 2 * quarter // n, d)
         + quad_sum_scratch(t, d) * 3
-        + [DMA((n,))] * 4 + [DMA((g,))] * 4
-        + [DMA((3,)), DMA((4,)), DMA((3,)), DMA((4,)), DMA((2,))],
+        + [DMA((n,))] * 4 + [DMA((line,))] * 2 + line_sems(line, 2)
+        + [DMA((3,)), DMA((4,)), DMA((3,)), DMA((4,)), DMA((1,))],
         compiler_params=pltpu.CompilerParams(
-            collective_id=1, has_side_effects=True, vmem_limit_bytes=60 << 20
+            collective_id=1, has_side_effects=True, vmem_limit_bytes=62 << 20
         ),
         name="feed",
     )(x, cot, gates, o, wout, small, w1, w2)
-
-
-class LineSum:
-    def __init__(self, f, c, n, source, got, inbox, stage, pair_s, pair_r, line_s, line_r, subs, lone=False):
-        self.f, self.c, self.n, self.size = f, c, n, n // 2
-        self.place, self.bit = c // 2, lax.rem(c, 2)
-        self.source = source
-        self.got, self.inbox, self.stage = got, inbox, stage
-        self.pair_s, self.pair_r, self.line_s, self.line_r = pair_s, pair_r, line_s, line_r
-        self.subs, self.lone = subs, lone
-        self.span = self.size // 4 if lone else self.size
-        self.first = f * self.span if lone else 0
-
-    def valid(self, o):
-        return jnp.logical_and(o >= self.first, o < self.first + self.span)
-
-    def index(self, o, sub):
-        return (o - self.first) * self.subs + sub
-
-    def term(self, o, sub, bit):
-        return self.source(2 * (o - self.first) + bit, sub)
-
-    def pair_copy(self, o, sub):
-        i = self.index(o, sub)
-        return copy_to(
-            self.term(o, sub, 1 - self.bit), self.got.at[i], self.pair_s.at[i], self.pair_r.at[i],
-            self.f, self.c + 1 - 2 * self.bit,
-        )
-
-    def line_copy(self, i, slot, c):
-        return copy_to(self.stage.at[i], self.inbox.at[slot], self.line_s.at[i], self.line_r.at[slot], self.f, c)
-
-    def each(self, work):
-        def one(k, _):
-            work(self.first + k // self.subs, lax.rem(k, self.subs))
-            return 0
-
-        lax.fori_loop(0, self.span * self.subs, one, 0)
-
-    def begin(self):
-        self.each(lambda o, sub: self.pair_copy(o, sub).start())
-
-    def gathered(self, o, sub):
-        self.pair_copy(o, sub).wait_recv()
-        return self.term(o, sub, self.bit)[...].astype(F32) + self.got[self.index(o, sub)].astype(F32)
-
-    def extra(self, sub):
-        return self.span * self.subs + sub
-
-    def move(self, o, sub, go_right):
-        i = self.index(o, sub)
-        total = self.gathered(o, sub)
-        starts = self.place == 0 if go_right else self.place == self.size - 1
-
-        @pl.when(starts)
-        def _():
-            self.stage[i] = total.astype(BF16)
-
-        @pl.when(jnp.logical_not(starts))
-        def _():
-            self.line_copy(i, i, self.c).wait_recv()
-            self.stage[i] = (total + self.inbox[i].astype(F32)).astype(BF16)
-
-        if go_right:
-            self.line_copy(i, i, self.c + 2).start()
-        else:
-            slot = jnp.where(o == self.place - 1, self.extra(sub), i)
-            self.line_copy(i, slot, self.c - 2).start()
-
-    def step(self, k):
-        def one(sub, _):
-            far, near = self.size - 1 - k, k
-
-            @pl.when(jnp.logical_and(self.valid(far), far > self.place))
-            def _():
-                self.move(far, sub, True)
-
-            @pl.when(jnp.logical_and(self.valid(near), near < self.place))
-            def _():
-                self.move(near, sub, False)
-
-            return 0
-
-        lax.fori_loop(0, self.subs, one, 0)
-
-    def settle(self, sub):
-        i = self.index(self.place, sub)
-        self.stage[i] = self.gathered(self.place, sub).astype(BF16)
-        own = self.gathered_again(self.place, sub)
-
-        left = self.place > 0
-        right = self.place < self.size - 1
-
-        @pl.when(left)
-        def _():
-            self.line_copy(i, i, self.c).wait_recv()
-
-        @pl.when(right)
-        def _():
-            self.line_copy(i, self.extra(sub), self.c).wait_recv()
-
-        @pl.when(jnp.logical_and(left, right))
-        def _():
-            self.stage[i] = (
-                own + self.inbox[i].astype(F32) + self.inbox[self.extra(sub)].astype(F32)
-            ).astype(BF16)
-
-        @pl.when(jnp.logical_and(left, jnp.logical_not(right)))
-        def _():
-            self.stage[i] = (own + self.inbox[i].astype(F32)).astype(BF16)
-
-        @pl.when(jnp.logical_and(right, jnp.logical_not(left)))
-        def _():
-            self.stage[i] = (own + self.inbox[self.extra(sub)].astype(F32)).astype(BF16)
-
-    def gathered_again(self, o, sub):
-        return self.term(o, sub, self.bit)[...].astype(F32) + self.got[self.index(o, sub)].astype(F32)
-
-    def finish(self):
-        @pl.when(self.valid(self.place))
-        def _():
-            lax.fori_loop(0, self.subs, lambda sub, u: (self.settle(sub), u)[1], 0)
-
-    def sent(self):
-        def one(o, sub):
-            self.pair_copy(o, sub).wait_send()
-
-            @pl.when(o != self.place)
-            def _():
-                self.line_copy(self.index(o, sub), 0, self.c).wait_send()
-
-        self.each(one)
 
 
 class LoneShare:
@@ -938,15 +1022,15 @@
 
 def back_kernel(
     n, far_kv,
-    da_ref, gwout_ref, gw1_ref, gw2_ref, qcat_ref, qpos_ref, kv_ref, lse_ref, of_ref,
+    da_ref, gwout_ref, s1_ref, s2_ref, qcat_ref, qpos_ref, kv_ref, lse_ref, of_ref,
     tok_ref, p1_ref, ev_ref, gates_ref, gsel_ref, x_ref, small_ref, dmid_ref, vec_ref, table_ref,
-    din_ref, gp_ref, g1_ref, g2_ref, go_ref, vq_ref, dkv_ref,
-    do_ref, delta_ref, grad_ref, kcat_ref, acc_ref, ring_ref, drel_ref, dqs_ref, dq_ref, part_ref, dp_ref,
-    gpart_ref, mine_ref, vin_ref,
+    din_ref, gp_ref, gq_ref, g1_ref, g2_ref, go_ref, vq_ref, dkv_ref,
+    do_ref, delta_ref, grad_ref, kcat_ref, acc_ref, ring_ref, pin_ref, drel_ref, dqs_ref, dq_ref, part_ref, dp_ref,
+    gpa_ref, gpb_ref, mine_ref, vin_ref,
     s0, s1, s2, s3, s4, s5, s6,
-    p0, p1, p2, p3, p4, p5, p6, u0, u1, u2, u3, u4, u5, u6,
-    v0, v1, v2, v3, v4, v5, v6, w0, w1, w2, w3, w4, w5, w6,
-    da_s, da_r, kv_s, kv_r, dq_s, dq_r, gp_s, gp_r, g1_s, g1_r, g2_s, g2_r, go_s, go_r,
+    p0, p1, p2, p3, p4, p5, p6, u1, u2, u5, u6,
+    fin2, got2, two_s, two_r, w0, w1, w2, w3, w4, w5, w6, y1, y2, y5, y6, goty, swap_s, swap_r,
+    da_s, da_r, kv_s, kv_r, pin_r, dq_s, dq_r, gp_s, gp_r, gq_s, gq_r, g1_s, g1_r, g2_s, g2_r, go_s, go_r,
     vc_s, vc_r, vf_s, vf_r, loc,
 ):
     f, c = lax.axis_index("fsdp"), lax.axis_index("ctx")
@@ -972,22 +1056,25 @@
         return 0
 
     lax.fori_loop(0, 4, send_da, 0)
-    sub_out, sub_two = p0.shape[0] // max(1, groups // 2), v0.shape[0] // max(1, groups // 2)
-
-    def rows_at(ref, count):
-        return lambda block, sub: ref.at[pl.ds(pl.multiple_of(block * count, count), count), :]
-
-    def piece_at(ref, subs):
-        count = ref.shape[1] // subs
-        return lambda block, sub: ref.at[block, pl.ds(pl.multiple_of(sub * count, count), count), :]
-
-    sum_out = LineSum(f, c, n, piece_at(gwout_ref, sub_out), p0, p1, p2, p3, p4, p5, p6, sub_out, lone=True)
-    sum_one = LineSum(f, c, n, rows_at(gw1_ref, rows), u0, u1, u2, u3, u4, u5, u6, 1)
-    sum_two = LineSum(f, c, n, piece_at(gw2_ref, sub_two), v0, v1, v2, v3, v4, v5, v6, sub_two, lone=True)
-    sum_in = LineSum(f, c, n, rows_at(gpart_ref, rows), w0, w1, w2, w3, w4, w5, w6, 1)
-    big = (sum_two, sum_one, sum_out)
-    for one in big:
-        one.begin()
+    sub_out = p0.shape[0] // max(1, groups // 2)
+    cut = gwout_ref.shape[1] // sub_out
+    sum_out = LineSum(
+        f, c, n, lambda k, sub: gwout_ref.at[k, pl.ds(pl.multiple_of(sub * cut, cut), cut), :],
+        p1, p2, p5, p6, pair=(p0, p3, p4), subs=sub_out, lone=True,
+    )
+    sum_one = LineSum(f, c, n, lambda o, sub: s1_ref.at[o], u1, u2, u5, u6)
+    half = gpa_ref.shape[1]
+    pair_to = c + 1 - 2 * lax.rem(c, 2)
+
+    def block_rows(ref, k):
+        return ref.at[pl.ds(pl.multiple_of(k * rows, rows), rows), :]
+
+    sum_in = LineSum(
+        f, c, n, lambda k, sub: block_rows(gpa_ref, k), w1, w2, w5, w6, pair=(w0, w3, w4)
+    )
+    sum_late = LineSum(f, c, n, lambda o, sub: block_rows(gpb_ref, 2 * o + sub), y1, y2, y5, y6, subs=2)
+    swap_two = copy_to(s2_ref.at[1], got2, two_s, two_r, f, pair_to)
+    swap_late = copy_to(y2.at[pair_to], goty, swap_s, swap_r, f, pair_to)
 
     def prepare(i, _):
         @pl.when(block_of(turn, i, groups) != c)
@@ -999,6 +1086,8 @@
         return 0
 
     lax.fori_loop(0, 4, prepare, 0)
+    sum_out.begin()
+    swap_two.start()
     row_in = lax.broadcasted_iota(jnp.int32, (tokens, tokens), 0)
     col_in = lax.broadcasted_iota(jnp.int32, (tokens, tokens), 1)
     lane = lax.broadcasted_iota(jnp.int32, (tokens, LANES), 1)
@@ -1026,22 +1115,62 @@
         def _():
             dq_ref[seq] = dqs_ref[i]
 
-    def ring_copy(slot, to):
-        return copy_to(ring_ref.at[slot], dkv_ref.at[c], kv_s.at[slot], kv_r.at[c], f, to)
-
-    def ring_local(slot):
-        return pltpu.make_async_copy(ring_ref.at[slot], dkv_ref.at[c], kv_s.at[slot])
+    bit = lax.rem(c, 2)
+    pair_last = block_of(turn + 1 - 2 * bit, 3, groups)
+
+    def ring_pair(kb):
+        slot = lax.rem(kb, 4)
+        return copy_to(ring_ref.at[slot], pin_ref.at[kb // 2], kv_s.at[slot], pin_r.at[kb // 2], f, pair_to)
+
+    def ring_copy(kb):
+        slot = lax.rem(kb, 4)
+        return copy_to(ring_ref.at[slot], dkv_ref.at[c // 2], kv_s.at[slot], kv_r.at[c // 2], f, kb)
+
+    def ring_local(kb):
+        slot = lax.rem(kb, 4)
+        return pltpu.make_async_copy(ring_ref.at[slot], dkv_ref.at[c // 2], kv_s.at[slot])
+
+    def sums(kb):
+        return jnp.logical_and(lax.rem(kb, 2) == bit, kb <= jnp.maximum(last_own, pair_last))
+
+    def gives(kb):
+        return jnp.logical_and(lax.rem(kb, 2) != bit, kb <= last_own)
 
     def ring_free(kb):
-        slot = lax.rem(kb, 4)
-
-        @pl.when(jnp.logical_and(kb != c, kb <= last_own))
-        def _():
-            ring_copy(slot, c).wait_send()
-
-        @pl.when(jnp.logical_and(kb == c, kb <= last_own))
-        def _():
-            ring_local(slot).wait()
+        @pl.when(gives(kb))
+        def _():
+            ring_pair(kb).wait_send()
+
+        @pl.when(jnp.logical_and(sums(kb), kb != c))
+        def _():
+            ring_copy(kb).wait_send()
+
+        @pl.when(jnp.logical_and(sums(kb), kb == c))
+        def _():
+            ring_local(kb).wait()
+
+    def pass_on(kb):
+        @pl.when(sums(kb))
+        def _():
+            total = acc_ref[lax.rem(kb, 2)]
+            slot = lax.rem(kb, 4)
+
+            @pl.when(kb <= pair_last)
+            def _():
+                ring_pair(kb).wait_recv()
+                ring_ref[slot] = (total + pin_ref[kb // 2].astype(F32)).astype(BF16)
+
+            @pl.when(kb > pair_last)
+            def _():
+                ring_ref[slot] = total.astype(BF16)
+
+            @pl.when(kb != c)
+            def _():
+                ring_copy(kb).start()
+
+            @pl.when(kb == c)
+            def _():
+                ring_local(kb).start()
 
     def key_block(kb, _):
         own = [block_of(turn, i, groups) for i in range(4)]
@@ -1051,7 +1180,8 @@
         kcat_ref[:, 0 : width // 2] = cosine.astype(BF16)
         kcat_ref[:, width // 2 : width] = sine.astype(BF16)
         kcat_ref[:, width:] = kv_ref[kb, :, 0:128]
-        acc_ref[...] = jnp.zeros_like(acc_ref)
+        now = lax.rem(kb, 2)
+        acc_ref[now] = jnp.zeros((tokens, 256), F32)
 
         def query_block(i, _):
             gap = (block_of(turn, i, groups) - kb) * tokens
@@ -1059,8 +1189,8 @@
             probs = jnp.where(col_in <= row_in + gap, jnp.exp(scores - lse_ref[i]), 0.0)
             d_probs = mm_t(do_ref[i], kv_ref[kb, :, 128:256])
             d_scores = (probs * (d_probs - delta_ref[i])).astype(BF16)
-            acc_ref[:, 0:128] += mm_left_t(d_scores, qcat_ref[i, :, width:])
-            acc_ref[:, 128:256] += mm_left_t(probs.astype(BF16), do_ref[i])
+            acc_ref[now, :, 0:128] += mm_left_t(d_scores, qcat_ref[i, :, width:])
+            acc_ref[now, :, 128:256] += mm_left_t(probs.astype(BF16), do_ref[i])
             grad_ref[i] += mm(d_scores, kcat_ref[...])
             return 0
 
@@ -1074,49 +1204,48 @@
         def _():
             ring_free(kb - 4)
 
-        @pl.when(kb <= last_own)
-        def _():
-            slot = lax.rem(kb, 4)
-            ring_ref[slot] = acc_ref[...].astype(BF16)
-
-            @pl.when(kb != c)
-            def _():
-                ring_copy(slot, kb).start()
-
-            @pl.when(kb == c)
-            def _():
-                ring_local(slot).start()
-
-        @pl.when(kb >= n // 2)
-        def _():
-            def progress(k, _):
-                index = (kb - n // 2) * 3 + k
-                for which, one in enumerate(big):
-                    @pl.when(index // (n // 2) == which)
-                    def _():
-                        one.step(lax.rem(index, n // 2))
-
-                return 0
-
-            lax.fori_loop(0, 3, progress, 0)
+        @pl.when(gives(kb))
+        def _():
+            ring_ref[lax.rem(kb, 4)] = acc_ref[now].astype(BF16)
+            ring_pair(kb).start()
+
+        @pl.when(kb >= 1)
+        def _():
+            pass_on(kb - 1)
+
+        @pl.when(jnp.logical_and(now == 1, kb < n - 1))
+        def _():
+            sum_one.turn(kb // 2)
+
+        @pl.when(jnp.logical_and(now == 0, kb >= 4))
+        def _():
+            sum_out.turn(kb // 2 - 2)
 
         return 0
 
     lax.fori_loop(0, n, key_block, 0)
-    for one in big:
-        one.finish()
-    share_two = LoneShare(sum_two, g2_ref, g2_s, g2_r)
+    pass_on(n - 1)
+    sum_out.turn(n // 2 - 2)
+    swap_two.wait()
+    fin2[...] = (s2_ref[0].astype(F32) + got2[...].astype(F32)).astype(BF16)
+    sum_one.finish()
+    sum_out.finish()
     share_out = LoneShare(sum_out, go_ref, go_s, go_r)
-    gather_one = QuadGather(f, c, g1_ref, g1_s, g1_r)
-    local_one = pltpu.make_async_copy(u2.at[c // 2], g1_ref.at[f], loc.at[0])
-    local_one.start()
-    share_two.begin()
-    gather_one.begin(u2.at[c // 2])
+    gathers = []
+    def hand_out(held, out, send, recv):
+        local = pltpu.make_async_copy(held, out.at[f], loc.at[len(gathers)])
+        local.start()
+        gather = QuadGather(f, c, out, send, recv)
+        gather.begin(held)
+        gathers.append((gather, local))
+
+    hand_out(fin2, g2_ref, g2_s, g2_r)
+    hand_out(u2.at[c // 2], g1_ref, g1_s, g1_r)
     share_out.begin()
 
     all_tokens = 4 * tokens
     d_rel = drel_ref[...].reshape(all_tokens, width)
-    gpart_ref[:, 896:] = mm_left_t(d_rel, qpos_ref[...].reshape(all_tokens, LANES)).astype(BF16)
+    gpb_ref[:, 896 - half :] = mm_left_t(d_rel, qpos_ref[...].reshape(all_tokens, LANES)).astype(BF16)
 
     def collect(s, _):
         to = s * groups + own_turn
@@ -1125,31 +1254,33 @@
         def _():
             copy_to(dqs_ref.at[0], dq_ref.at[s], dq_s.at[0], dq_r.at[s], f, c).wait_recv()
 
-        acc_ref[...] = jnp.zeros_like(acc_ref)
+        acc_ref[0] = jnp.zeros((tokens, 256), F32)
 
         def add(k, _):
-            at = s * groups + k
-
-            @pl.when(block_of(k, 3, groups) >= c)
+            giver = 2 * k + bit
+            at = (s * groups + giver) // 2
+            last = jnp.maximum(block_of(giver, 3, groups), block_of(giver + 1 - 2 * bit, 3, groups))
+
+            @pl.when(last >= c)
             def _():
-                @pl.when(at != c)
+                @pl.when(s * groups + giver != c)
                 def _():
                     copy_to(ring_ref.at[0], dkv_ref.at[at], kv_s.at[0], kv_r.at[at], f, c).wait_recv()
 
                 if far_kv:
-                    bring = pltpu.make_async_copy(dkv_ref.at[at], part_ref, loc.at[1])
+                    bring = pltpu.make_async_copy(dkv_ref.at[at], part_ref, loc.at[4])
                     bring.start()
                     bring.wait()
-                    acc_ref[...] += part_ref[...].astype(F32)
+                    acc_ref[0] += part_ref[...].astype(F32)
                 else:
-                    acc_ref[...] += dkv_ref[at].astype(F32)
+                    acc_ref[0] += dkv_ref[at].astype(F32)
 
             return 0
 
-        lax.fori_loop(0, groups, add, 0)
+        lax.fori_loop(0, groups // 2, add, 0)
         dp_ref[s, :, 0:128] = dq_ref[s]
-        dp_ref[s, :, 128:256] = acc_ref[:, 0:128].astype(BF16)
-        d_values = acc_ref[:, 128:256]
+        dp_ref[s, :, 128:256] = acc_ref[0, :, 0:128].astype(BF16)
+        d_values = acc_ref[0, :, 128:256]
         for e in range(5):
             values = ev_ref[s, :, e * LANES : (e + 1) * LANES].astype(F32)
             column = jnp.sum(values * d_values, axis=1, keepdims=True) * gates_ref[s, :, 24 + e : 25 + e]
@@ -1171,13 +1302,16 @@
         spot = pl.multiple_of(i * tile, tile)
         left = tok_ref[:, :, pl.ds(spot, tile)].reshape(all_tokens, tile)
         right = dp_ref[...].reshape(all_tokens, 896)
-        gpart_ref[pl.ds(spot, tile), 0:896] = mm_left_t(left, right).astype(BF16)
+        result = mm_left_t(left, right).astype(BF16)
+        gpa_ref[pl.ds(spot, tile), :] = result[:, 0:half]
+        gpb_ref[pl.ds(spot, tile), 0 : 896 - half] = result[:, half:]
         return 0
 
     lax.fori_loop(0, width // tile, weight_tile, 0)
     sum_in.begin()
-    share_two.relay()
-    gather_one.relay()
+    sum_late.turn(0)
+    for gather, _ in gathers:
+        gather.relay()
     share_out.relay()
     in_sum = QuadSum(f, c, s0, s1, s2, s3, s4, s5, s6)
     for k in (3, 2, 1, 0):
@@ -1185,7 +1319,11 @@
         in_sum.put(k, mm_t(dp_ref[f ^ k], weights))
         if k == 2:
             in_sum.cross()
-    lax.fori_loop(0, n // 2, lambda k, u: (sum_in.step(k), u)[1], 0)
+    lax.fori_loop(1, n // 2 - 1, lambda k, u: (sum_late.turn(k), u)[1], 0)
+    sum_in.turn(0)
+    sum_late.finish()
+    swap_late.start()
+    lax.fori_loop(1, n // 2 - 1, lambda k, u: (sum_in.turn(k), u)[1], 0)
     d_norm = in_sum.total()
     xhat, spread = layer_stats(x_ref[...].astype(F32))
     gain = spread_vector(small_ref[:, 0, :], width // n)
@@ -1200,11 +1338,11 @@
 
     lax.fori_loop(1, n, vec_send, 0)
     vin_ref[c] = mine_ref[...]
+    swap_late.wait()
+    y2[c] = (y2[c].astype(F32) + goty[...].astype(F32)).astype(BF16)
+    hand_out(y2.at[c], gq_ref, gq_s, gq_r)
     sum_in.finish()
-    gather_in = QuadGather(f, c, gp_ref, gp_s, gp_r)
-    local_in = pltpu.make_async_copy(w2.at[c // 2], gp_ref.at[f], loc.at[1])
-    local_in.start()
-    gather_in.begin(w2.at[c // 2])
+    hand_out(w2.at[c // 2], gp_ref, gp_s, gp_r)
 
     def vec_wait(k, _):
         to = lax.rem(c + k, n)
@@ -1215,19 +1353,18 @@
     vq_ref[f] = jnp.sum(vin_ref[...], axis=0)
     for k in range(1, 4):
         copy_to(vq_ref.at[f], vq_ref.at[f], vf_s.at[k], vf_r.at[f], f ^ k, c).start()
-    gather_in.relay()
+    for gather, _ in gathers[2:]:
+        gather.relay()
     for k in range(1, 4):
         copy_to(vq_ref.at[f ^ k], vq_ref.at[f ^ k], vf_s.at[k], vf_r.at[f ^ k], f, c).wait_recv()
         copy_to(vq_ref.at[f], vq_ref.at[f], vf_s.at[k], vf_r.at[f], f, c).wait_send()
-    for one in (gather_one, gather_in):
+    for one, local in gathers:
         one.got(f ^ 1)
         one.got(f ^ 3)
         one.sent()
-    local_one.wait()
-    local_in.wait()
-    share_two.finish()
+        local.wait()
     share_out.finish()
-    for one in big + (sum_in,):
+    for one in (sum_one, sum_out, sum_in, sum_late):
         one.sent()
     in_sum.sent()
 
@@ -1246,56 +1383,69 @@
 
 
 def cuts(count):
-    parts = max(1, count // 128)
+    parts = max(1, count // 64)
     return parts if count % (16 * parts) == 0 else 1
 
 
-def line_sum_scratch(blocks, subs, rows, cols):
+def pair_scratch(blocks, subs, rows, cols):
+    return [pltpu.VMEM((blocks * subs, rows // subs, cols), BF16)]
+
+
+def line_scratch(blocks, subs, rows, cols):
     return [
-        pltpu.VMEM((blocks * subs, rows // subs, cols), BF16), pltpu.VMEM(((blocks + 1) * subs, rows // subs, cols), BF16),
+        pltpu.VMEM(((blocks + 1) * subs, rows // subs, cols), BF16),
         pltpu.VMEM((blocks * subs, rows // subs, cols), BF16),
-        DMA((blocks * subs,)), DMA((blocks * subs,)), DMA((blocks * subs,)), DMA(((blocks + 1) * subs,)),
     ]
 
 
-def back(n, da, gwout, gw1, gw2, qcat, qpos, kv, lse, of, tok, p1, ev, gates, gsel, x, small, dmid, vec, table):
+def line_sems(blocks, subs):
+    return [DMA((blocks * subs,)), DMA(((blocks + 1) * subs,))]
+
+
+def back(n, da, gwout, s1, s2, qcat, qpos, kv, lse, of, tok, p1, ev, gates, gsel, x, small, dmid, vec, table):
     t, d = x.shape
     g = n // 4
-    quarter = gw1.shape[1]
-    rows, out_rows, two_rows = d // n, gwout.shape[1], gw2.shape[1]
-    sub_out, sub_two = cuts(out_rows), cuts(two_rows)
-    lone = n // 8
+    quarter = s1.shape[2]
+    rows, out_rows, two_rows = d // n, gwout.shape[1], s2.shape[1]
+    half = d // 2
+    sub_out = cuts(out_rows)
+    lone, line = n // 8, n // 2
     far_kv = g > 4
     return pl.pallas_call(
         functools.partial(back_kernel, n, far_kv),
         out_shape=[
-            sds((t, d), F32), sds((4, rows, d), BF16), sds((4, rows, quarter), BF16),
-            sds((sub_two, two_rows // sub_two, d), BF16), sds((sub_out, out_rows // sub_out, d), BF16),
-            sds((4, 8, d), F32), sds((n, t, 256), BF16),
+            sds((t, d), F32), sds((4, rows, half), BF16), sds((4, rows, half), BF16), sds((4, rows, quarter), BF16),
+            sds((4, two_rows, d), BF16), sds((sub_out, out_rows // sub_out, d), BF16),
+            sds((4, 8, d), F32), sds((line, t, 256), BF16),
         ],
         in_specs=[VMEM] * 19,
-        out_specs=[VMEM, ANY, ANY, ANY, ANY, VMEM, ANY if far_kv else VMEM],
+        out_specs=[VMEM, ANY, ANY, ANY, ANY, ANY, VMEM, ANY if far_kv else VMEM],
         scratch_shapes=[
             pltpu.VMEM((4, t, LANES), BF16), pltpu.VMEM((4, t, 1), F32), pltpu.VMEM((4, t, d + LANES), F32),
-            pltpu.VMEM((t, d + LANES), BF16), pltpu.VMEM((t, 256), F32), pltpu.VMEM((4, t, 256), BF16),
+            pltpu.VMEM((t, d + LANES), BF16), pltpu.VMEM((2, t, 256), F32), pltpu.VMEM((4, t, 256), BF16),
+            pltpu.VMEM((line, t, 256), BF16),
             pltpu.VMEM((4, t, d), BF16), pltpu.VMEM((4, t, LANES), BF16), pltpu.VMEM((4, t, LANES), BF16),
-            pltpu.VMEM((t, 256), BF16), pltpu.VMEM((4, t, 896), BF16), pltpu.VMEM((d, d), BF16),
+            pltpu.VMEM((t, 256), BF16), pltpu.VMEM((4, t, 896), BF16), pltpu.VMEM((d, half), BF16), pltpu.VMEM((d, half), BF16),
             pltpu.VMEM((8, d), F32), pltpu.VMEM((n, 8, d), F32),
         ]
         + quad_sum_scratch(t, d)
-        + line_sum_scratch(lone, sub_out, out_rows, d)
-        + line_sum_scratch(n // 2, 1, rows, quarter)
-        + line_sum_scratch(lone, sub_two, two_rows, d)
-        + line_sum_scratch(n // 2, 1, rows, d)
+        + pair_scratch(lone, sub_out, out_rows, d) + line_scratch(lone, sub_out, out_rows, d)
+        + [DMA((lone * sub_out,))] * 2 + line_sems(lone, sub_out)
+        + line_scratch(line, 1, rows, quarter) + line_sems(line, 1)
+        + [pltpu.VMEM((two_rows, d), BF16), pltpu.VMEM((two_rows, d), BF16), DMA, DMA]
+        + pair_scratch(line, 1, rows, half) + line_scratch(line, 1, rows, half)
+        + [DMA((line,))] * 2 + line_sems(line, 1)
+        + line_scratch(line, 2, 2 * rows, half) + line_sems(line, 2)
+        + [pltpu.VMEM((rows, half), BF16), DMA, DMA]
         + [
-            DMA((4,)), DMA((4,)), DMA((4,)), DMA((n,)), DMA((4,)), DMA((4,)), DMA((3,)), DMA((4,)),
-            DMA((3,)), DMA((4,)), DMA((2,)), DMA, DMA((2,)), DMA, DMA((n,)), DMA((n,)), DMA((4,)), DMA((4,)), DMA((2,)),
+            DMA((4,)), DMA((4,)), DMA((4,)), DMA((line,)), DMA((line,)), DMA((4,)), DMA((4,)), DMA((3,)), DMA((4,)),
+            DMA((3,)), DMA((4,)), DMA((3,)), DMA((4,)), DMA((3,)), DMA((4,)), DMA((2,)), DMA, DMA((n,)), DMA((n,)), DMA((4,)), DMA((4,)), DMA((5,)),
         ],
         compiler_params=pltpu.CompilerParams(
             collective_id=2, has_side_effects=True, vmem_limit_bytes=63 << 20
         ),
         name="back",
-    )(da, gwout, gw1, gw2, qcat, qpos, kv, lse, of, tok, p1, ev, gates, gsel, x, small, dmid, vec, table)
+    )(da, gwout, s1, s2, qcat, qpos, kv, lse, of, tok, p1, ev, gates, gsel, x, small, dmid, vec, table)
 
 
 def pad_channels(v, group):
@@ -1336,7 +1486,7 @@
         ],
         axis=-1,
     )
-    piece = min(LANES, b1.shape[0])
+    piece = b1.shape[0] // 4
     vectors = [ln1_gain, ln1_bias, ln2_gain, ln2_bias, b2]
     vectors = [jnp.pad(v, (0, LANES - v.shape[0])) for v in vectors]
     extra = jnp.pad(b1.reshape(-1, piece), ((0, 0), (0, LANES - piece)))
@@ -1369,21 +1519,22 @@
         wvsel, wv, wosel, wout, ln2_gain, ln2_bias, b1, b2,
     )
     table = jnp.asarray(turn_table(d))
-    tok, p1g, smallg, woutg, cotg, ev, gates, o, qcat, qpos, kv, lse, of = attend(
-        n, x, aux, cot, p1, small, pieces, bias, table
+    rows, hidden = w1.shape
+    part = hidden // n // 4
+    w1_own = lax.dynamic_index_in_dim(w1.reshape(rows, n, 4, part), f, 2, keepdims=False).reshape(rows, n * part)
+    tok, p1g, smallg, woutg, w1g, cotg, ev, gates, o, qcat, qpos, kv, lse, of = attend(
+        n, x, aux, cot, p1, small, pieces, w1_own, bias, table
     )
     block = 640 // g
-    out, dmid, gwout, gw1, gw2, da, gsel, vec = feed(
-        n, x, cotg, gates, o, woutg[:, :block].reshape(640, d), smallg, w1, w2
+    out, dmid, gwout, s1, s2, da, gsel, vec = feed(
+        n, x, cotg, gates, o, woutg[:, :block].reshape(640, d), smallg, w1g.reshape(d, n * part), w2
     )
     gwout = gwout.reshape(g, block, d)
     gwout = jnp.pad(gwout, ((0, 0), (0, pieces.shape[0] - block), (0, 0)))
-    d_in, gp, g1, g2, go, vq, _ = back(
-        n, da, gwout, gw1, gw2.reshape(g, -1, d), qcat, qpos, kv, lse, of, tok, p1g, ev, gates, gsel,
-        x, smallg, dmid, vec, table,
+    d_in, gp, gq, g1, g2, go, vq, _ = back(
+        n, da, gwout, s1, s2, qcat, qpos, kv, lse, of, tok, p1g, ev, gates, gsel, x, smallg, dmid, vec, table
     )
-    gp = jnp.transpose(gp, (1, 0, 2))
-    rows = gp.shape[0]
+    gp = jnp.transpose(jnp.concatenate([gp, gq], axis=-1), (1, 0, 2))
     g_query = drop_pads(gp[..., 0:128], group).reshape(rows, 448).astype(F32)
     g_key = drop_pads(gp[..., 128:256], group).reshape(rows, 448).astype(F32)
     g_rel = drop_pads(gp[..., 896:], group).reshape(rows, 448).astype(F32)
@@ -1391,13 +1542,12 @@
     g_value = drop_pads(experts, group).reshape(rows, 2240).astype(F32)
     g_vsel = experts[..., SPOT_A].reshape(rows, 20).astype(F32)
     g_osel = experts[..., SPOT_B].reshape(rows, 20).astype(F32)
-    g_one = jnp.transpose(g1, (1, 0, 2)).reshape(rows, -1).astype(F32)
+    g_one = jnp.transpose(g1.reshape(4, rows, n, part), (1, 2, 0, 3)).reshape(rows, hidden).astype(F32)
     g_two = g2.reshape(-1, d).astype(F32)
     g_out = go.reshape(-1, d)[:block].reshape(-1, group * 8 // 7, d)[:, :group].reshape(-1, d).astype(F32)
     sums = jnp.sum(vq, axis=0)
     own = lax.dynamic_slice_in_dim(sums, c * rows, rows, 1)
-    b1_rows = b1.shape[0]
-    g_b1 = lax.dynamic_slice_in_dim(vq[:, 3, :].reshape(-1), c * b1_rows, b1_rows, 0)
+    g_b1 = lax.dynamic_slice_in_dim(vq[:, 3, :], c * part, part, 1).reshape(-1)
     g_u = drop_pads(vq[:, 6, 0:LANES], group)
     g_v = drop_pads(vq[:, 7, 0:LANES], group)
     return (

time: 514 us -> 396 us (0.77)
  Pallas kernels: 473 us -> 352 us
  local copies, waits for them, and re-layouts: 19.9 us -> 25.5 us
    pallas_call x1, Pallas kernels: 250 us -> 154 us  [back(): pl.pallas_call(functools.partial(back_kernel, n, far_kv), out_shape=[sds(...]
    pallas_call x1, Pallas kernels: 119 us -> 91.5 us  [feed(): pl.pallas_call(functools.partial(feed_kernel, n), out_shape=[sds((t, d),...]
where the time goes in v2:
time: 396 us; the launch traced here: 391 us
  Pallas kernels  352 us (89%)
  local copies, waits for them, and re-layouts  25.5 us (6%)
  other arithmetic  12.6 us (3%)
    pallas_call x1, Pallas kernels, back(): pl.pallas_call(functools.partial(back_kernel, n, far_kv), out_shape=[sds(...  154 us
    pallas_call x1, Pallas kernels, attend(): pl.pallas_call(functools.partial(attend_kernel, n), out_shape=[sds((4, t,...  106 us
    pallas_call x1, Pallas kernels, feed(): pl.pallas_call(functools.partial(feed_kernel, n), out_shape=[sds((t, d),...  91.5 us

profile of v2, /device:TPU:15, one launch (start us, length us, event | category | flops | bytes accessed | tf_op | source)
XLA Modules:
  0.0 390.8 jit_solution(9314007626522736974)
XLA Ops:
  0.7 1.0 copy-done
  1.8 0.8 reshape.200
  2.7 0.8 reshape.202
  4.8 1.5 concatenate.23
  7.0 0.8 reshape.189
  8.4 0.8 constant_dynamic-slice_fusion.7
  10.2 0.8 constant_dynamic-slice_fusion.2
  13.5 0.9 pad.37
  15.1 1.5 dynamic-slice_reduce_fusion
  16.7 0.8 copy.112
  17.4 105.8 %attend.1 = (bf16[4,256,1152]{2,1,0:T(8,128)(2,1)}, bf16[8,128,1024]{2,1,0:T(8,128)(2,1)}, f32[8,16,128]{2,1,0:T(8,128)}, bf16[2,320,1024]{2,1,0:T(8,128)(2,1)},...) custom-call(bf16[256,1024]{1,0:T(8,128)(2,1)} %x_ref.5, ...), custom_call_target="tpu_custom_call" | custom-call | tf_op jit(solution)/shard_map/attend/pallas_call | solution.py:543
  123.2 91.5 %feed.1 = (bf16[256,1024]{1,0:T(8,128)(2,1)}, f32[256,1024]{1,0:T(8,128)}, bf16[640,1024]{1,0:T(8,128)(2,1)}, bf16[4,128,1024]{2,1,0:T(8,128)(2,1)}, bf16[2,128,...) custom-call(bf16[256,1024]{1,0:T(8,128)(2,1)} %x_ref.5, ...), custom_call_target="tpu_custom_call" | custom-call | tf_op jit(solution)/shard_map/feed/pallas_call | solution.py:955
  214.7 154.3 %back.1 = (f32[256,1024]{1,0:T(8,128)}, bf16[4,128,512]{2,1,0:T(8,128)(2,1)}, bf16[4,128,512]{2,1,0:T(8,128)(2,1)}, bf16[4,128,1024]{2,1,0:T(8,128)(2,1)}, bf16[...) custom-call(bf16[4,256,128]{2,1,0:T(8,128)(2,1)} %get-tuple-element., ...), custom_call_target="tpu_custom_call" | custom-call | tf_op jit(solution)/shard_map/back/pallas_call | solution.py:1414
  369.0 0.8 slice_reduce_fusion
  371.4 0.9 slice.82
  372.3 0.9 reduce_sum.29
  374.4 1.1 slice.79
  375.4 1.2 bitcast_convert_fusion.1
  381.2 1.1 bitcast_convert_fusion.2
  382.7 1.4 copy.105
  384.1 1.9 reshape.221
  385.9 2.9 bitcast_convert_fusion
  388.9 0.8 copy.115
  389.6 1.0 copy.116
  (77 shorter events, 14.6 us)
Async XLA Ops:
  0.7 1.1 copy-start
  7.0 6.5 %copy-start.4 = (bf16[280,1024]{1,0:T(8,128)(2,1)S(1)}, bf16[280,1024]{1,0:T(8,128)(2,1)}, u32[]{:S(2)}) copy-start(bf16[280,1024]{1,0:T(8,128)(2,1)} %param.37) | copy-start | bytes 1720324
  12.1 2.3 copy-start.2
  369.0 7.6 %copy-start.6 = (bf16[4,128,512]{2,1,0:T(8,128)(2,1)S(1)}, bf16[4,128,512]{2,1,0:T(8,128)(2,1)}, u32[]{:S(2)}) copy-start(bf16[4,128,512]{2,1,0:T(8,128)(2,1)} %get-tuple-element.72) | copy-start | bytes 1572868
  369.0 7.6 %copy-start.7 = (bf16[4,128,512]{2,1,0:T(8,128)(2,1)S(1)}, bf16[4,128,512]{2,1,0:T(8,128)(2,1)}, u32[]{:S(2)}) copy-start(bf16[4,128,512]{2,1,0:T(8,128)(2,1)} %get-tuple-element.73) | copy-start | bytes 1572868
  379.5 2.8 copy-start.1
  385.9 2.9 copy-start.5
  385.9 3.7 copy-start.3

commit v3 on v2

--- a/solution.py
+++ b/solution.py
@@ -242,10 +242,10 @@
 
 def attend_kernel(
     n,
-    x_ref, aux_ref, cot_ref, p1_ref, small_ref, wout_ref, w1_ref, bias_ref, table_ref,
-    tok_ref, p1g_ref, smallg_ref, woutg_ref, w1g_ref, cotg_ref, ev_ref, gates_ref, o_ref,
+    x_ref, aux_ref, cot_ref, p1_ref, small_ref, wout_ref, w2_ref, bias_ref, table_ref,
+    tok_ref, p1g_ref, smallg_ref, woutg_ref, w2e_ref, cotg_ref, ev_ref, gates_ref, o_ref,
     qcat_ref, qpos_ref, kv_ref, lse_ref, of_ref,
-    qs_ref, kvs_ref, qr_ref, os_ref, kcat_ref, m_ref, l_ref,
+    qs_ref, kvs_ref, qr_ref, os_ref, kcat_ref, vt_ref, m_ref, l_ref,
     sm_s, sm_r, p_r, p_a, p_b, p_c, w_r, w_a, w_b, w_c, h_r, h_a, h_b, h_c,
     t_s, t_r, c_s, c_r, q_s, q_r, kv_s, kv_r, kv_p, o_s, o_r, loc,
 ):
@@ -278,8 +278,10 @@
         lambda k, sub: woutg_ref.at[k, pl.ds(pl.multiple_of(sub * piece, piece), piece), :],
         w_r, w_a, w_b, w_c, subs=subs, lone=True,
     )
-    w1_copy = pltpu.make_async_copy(w1_ref, w1g_ref.at[c], loc.at[2])
-    gather_h = LineGather(f, c, n, lambda sub: w1_ref, lambda k, sub: w1g_ref.at[k], h_r, h_a, h_b, h_c)
+    early = w2e_ref.shape[1]
+    own2 = w2_ref.at[pl.ds(pl.multiple_of(f * (w2_ref.shape[0] // 4), 16), early), :]
+    w2_copy = pltpu.make_async_copy(own2, w2e_ref.at[c], loc.at[2])
+    gather_h = LineGather(f, c, n, lambda sub: own2, lambda k, sub: w2e_ref.at[k], h_r, h_a, h_b, h_c)
     cot_copy = pltpu.make_async_copy(cot_ref, cotg_ref.at[f], loc.at[1])
     cot_copy.start()
 
@@ -376,9 +378,9 @@
         lax.fori_loop(0, groups // 2, kv_send, 0)
         return 0
 
+    gather_h.begin(w2_copy.start)
     lax.fori_loop(0, 4, project, 0)
     gather_w.begin(wout_copy.start)
-    gather_h.begin(w1_copy.start)
 
     def kv_wait(block):
         copy_to(kvs_ref.at[0], kv_ref.at[block], kv_s.at[0], kv_r.at[block], f, c).wait_recv()
@@ -413,9 +415,9 @@
         first, second = rel_query[:, : width // 2], rel_query[:, width // 2 :]
         qcat_ref[i, :, 0 : width // 2] = ((first * sine + second * cosine) * scale).astype(BF16)
         qcat_ref[i, :, width // 2 : width] = ((second * sine - first * cosine) * scale).astype(BF16)
-        m_ref[i] = jnp.full((tokens, 1), MASKED, F32)
-        l_ref[i] = jnp.zeros((tokens, 1), F32)
-        of_ref[i] = jnp.zeros((tokens, LANES), F32)
+        m_ref[i] = jnp.full((1, tokens), MASKED, F32)
+        l_ref[i] = jnp.zeros((1, tokens), F32)
+        of_ref[i] = jnp.zeros((LANES, tokens), F32)
         return 0
 
     lax.fori_loop(0, 4, prepare, 0)
@@ -428,7 +430,7 @@
         result = of_ref[i] / total
         of_ref[i] = result
         lse_ref[i] = m_ref[i] + jnp.log(total)
-        os_ref[i] = result.astype(BF16)
+        os_ref[i] = result.T.astype(BF16)
         block = block_of(turn, i, groups)
 
         @pl.when(block != c)
@@ -456,18 +458,19 @@
         kcat_ref[:, 0 : width // 2] = cosine.astype(BF16)
         kcat_ref[:, width // 2 : width] = sine.astype(BF16)
         kcat_ref[:, width:] = kv_ref[kb, :, 0:128]
+        vt_ref[...] = kv_ref[kb, :, 128:256].astype(F32).T.astype(BF16)
 
         def query_block(i, _):
             gap = (block_of(turn, i, groups) - kb) * tokens
-            scores = mm_t(qcat_ref[i], kcat_ref[...])
-            scores = jnp.where(col_in <= row_in + gap, scores, MASKED)
+            scores = mm_t(kcat_ref[...], qcat_ref[i])
+            scores = jnp.where(row_in <= col_in + gap, scores, MASKED)
             before = m_ref[i]
-            best = jnp.maximum(before, jnp.max(scores, axis=1, keepdims=True))
+            best = jnp.maximum(before, jnp.max(scores, axis=0, keepdims=True))
             shrink = jnp.exp(before - best)
             probs = jnp.exp(scores - best)
             m_ref[i] = best
-            l_ref[i] = l_ref[i] * shrink + jnp.sum(probs, axis=1, keepdims=True)
-            of_ref[i] = of_ref[i] * shrink + mm(probs.astype(BF16), kv_ref[kb, :, 128:256])
+            l_ref[i] = l_ref[i] * shrink + jnp.sum(probs, axis=0, keepdims=True)
+            of_ref[i] = of_ref[i] * shrink + mm(vt_ref[...], probs.astype(BF16))
             return 0
 
         lax.fori_loop(first, 4, query_block, 0)
@@ -480,10 +483,13 @@
         def _():
             cot_gather.relay()
 
-        @pl.when(jnp.logical_and(kb >= n // 2, kb < n - 1))
-        def _():
-            gather_w.step(kb - n // 2 + 1)
-            gather_h.step(kb - n // 2 + 1)
+        @pl.when(jnp.logical_and(kb > 0, kb < n // 2))
+        def _():
+            gather_w.step(kb)
+
+        @pl.when(kb < n // 2 - 1)
+        def _():
+            gather_h.step(kb + 1)
 
         return 0
 
@@ -493,7 +499,7 @@
     cot_gather.sent()
     gather_w.finish()
     gather_h.finish()
-    w1_copy.wait()
+    w2_copy.wait()
 
     @pl.when(gather_w.valid(c // 2))
     def _():
@@ -534,7 +540,7 @@
     return jax.ShapeDtypeStruct(shape, dtype)
 
 
-def attend(n, x, aux, cot, p1, small, wout, w1, bias, table):
+def attend(n, x, aux, cot, p1, small, wout, w2, bias, table):
     t, d = x.shape
     rows = p1.shape[0]
     out_rows = wout.shape[0]
@@ -544,16 +550,16 @@
         functools.partial(attend_kernel, n),
         out_shape=[
             sds((4, t, d + LANES), BF16), sds((n, rows, d), BF16), sds((n, 16, LANES), F32),
-            sds((g, out_rows, d), BF16), sds((n,) + w1.shape, BF16), sds((4, t, d), BF16), sds((4, t, 640), BF16),
+            sds((g, out_rows, d), BF16), sds((n, early_rows(w2.shape[0] // 4), d), BF16), sds((4, t, d), BF16), sds((4, t, 640), BF16),
             sds((4, t, LANES), F32), sds((4, t, LANES), BF16), sds((4, t, d + LANES), BF16),
-            sds((4, t, LANES), BF16), sds((n, t, 256), BF16), sds((4, t, 1), F32), sds((4, t, LANES), F32),
+            sds((4, t, LANES), BF16), sds((n, t, 256), BF16), sds((4, 1, t), F32), sds((4, LANES, t), F32),
         ],
         in_specs=[VMEM, VMEM, ANY, VMEM, VMEM, ANY, ANY, VMEM, VMEM],
         out_specs=[VMEM, VMEM, VMEM, ANY, ANY, ANY] + [VMEM] * 8,
         scratch_shapes=[
             pltpu.VMEM((4, t, LANES), BF16), pltpu.VMEM((4, t, 256), BF16), pltpu.VMEM((4, t, LANES), BF16),
             pltpu.VMEM((4, t, LANES), BF16), pltpu.VMEM((t, d + LANES), BF16),
-            pltpu.VMEM((4, t, 1), F32), pltpu.VMEM((4, t, 1), F32),
+            pltpu.VMEM((LANES, t), BF16), pltpu.VMEM((4, 1, t), F32), pltpu.VMEM((4, 1, t), F32),
             DMA((n,)), DMA((n,)), DMA((n,)), DMA((n,)), DMA((n,)), DMA((n,)),
             DMA((g * subs,)), DMA((g * subs,)), DMA((g * subs,)), DMA((g * subs,)),
             DMA((n,)), DMA((n,)), DMA((n,)), DMA((n,)),
@@ -564,7 +570,7 @@
             collective_id=0, has_side_effects=True, vmem_limit_bytes=56 << 20
         ),
         name="attend",
-    )(x, aux, cot, p1, small, wout, w1, bias, table)
+    )(x, aux, cot, p1, small, wout, w2, bias, table)
 
 
 class QuadSum:
@@ -795,26 +801,36 @@
 
 def feed_kernel(
     n,
-    x_ref, cot_ref, gates_ref, o_ref, wout_ref, small_ref, w1g, w2_ref,
-    out_ref, dmid_ref, gwout_ref, s1_ref, s2_ref, da_ref, gsel_ref, vec_ref,
-    w2g, n2_ref, act_ref, slope_ref, dpre_ref, mixed_ref, dml_ref, mid_ref, gw1_ref, gw2_ref, got1, in2, stage2,
+    x_ref, cot_ref, gates_ref, o_ref, wout_ref, small_ref, w1_ref, w2_ref, w2e_ref,
+    out_ref, dmid_ref, gwout_ref, s1_ref, s2_ref, do_ref, gsel_ref, vec_ref,
+    w1g, w2g, n2_ref, act_ref, slope_ref, dpre_ref, mixed_ref, dml_ref, mid_ref, gw1_ref, gw2_ref, got1, in2, stage2,
     a0, a1, a2, a3, a4, a5, a6, b0, b1, b2, b3, b4, b5, b6, e0, e1, e2, e3, e4, e5, e6,
-    w2_r, w2_a, w2_b, w2_c, h1_s, h1_r, h2_s, h2_r, n_s, n_r, d_s, d_r, loc,
+    w1_r, w1_a, w1_b, w1_c, w2_r, w2_a, w2_b, w2_c, h1_s, h1_r, h2_s, h2_r, n_s, n_r, d_s, d_r, loc, da_ref, da_s, da_r,
 ):
     f, c = lax.axis_index("fsdp"), lax.axis_index("ctx")
     tokens, width = x_ref.shape
     quarter = w1g.shape[1]
+    groups = n // 4
+    own_turn, own_slot = holder_of(c, groups)
     greet(f, c, 4, n)
     rows1, rows2 = width // n, quarter // n
 
     def rows_of(ref, count):
         return lambda k: ref.at[pl.ds(pl.multiple_of(k * count, count), count), :]
 
-    own2 = w2_ref.at[pl.ds(pl.multiple_of(f * rows2, rows2), rows2), :]
-    at2 = rows_of(w2g, rows2)
-    gather2 = LineGather(f, c, n, lambda sub: own2, lambda k, sub: at2(k), w2_r, w2_a, w2_b, w2_c)
-    local2 = pltpu.make_async_copy(own2, at2(c), loc.at[0])
-    gather2.begin(local2.start)
+    early = w2e_ref.shape[1]
+    at1 = rows_of(w1g, rows1)
+    gather1 = LineGather(f, c, n, lambda sub: w1_ref, lambda k, sub: at1(k), w1_r, w1_a, w1_b, w1_c)
+    local1 = pltpu.make_async_copy(w1_ref, at1(c), loc.at[0])
+    bring2 = pltpu.make_async_copy(w2e_ref, w2g.at[:, 0:early, :], loc.at[1])
+    gather1.begin(local1.start)
+    bring2.start()
+    gather2 = None
+    if early < rows2:
+        own2 = w2_ref.at[pl.ds(pl.multiple_of(f * rows2 + early, 16), rows2 - early), :]
+        at2 = lambda k: w2g.at[k, early:rows2, :]
+        gather2 = LineGather(f, c, n, lambda sub: own2, lambda k, sub: at2(k), w2_r, w2_a, w2_b, w2_c)
+        local2 = pltpu.make_async_copy(own2, at2(c), loc.at[2])
     pair1 = PairSum(f, c, n, rows_of(gw1_ref, rows1), got1, s1_ref, h1_s, h1_r)
     line2 = LineSum(f, c, n, lambda o, sub: rows_of(gw2_ref, rows2)(2 * o + sub), in2, stage2, h2_s, h2_r, subs=2)
     attn_sum = QuadSum(f, c, a0, a1, a2, a3, a4, a5, a6)
@@ -830,7 +846,7 @@
         attn_sum.put(k, mm(mixed_ref[r], wout_ref[...]))
         if k == 2:
             attn_sum.cross()
-    gather2.step(1)
+    gather1.step(1)
     middle = x_ref[...].astype(F32) + attn_sum.total()
     mid_ref[...] = middle
     xhat, scale = layer_stats(middle)
@@ -839,6 +855,11 @@
     n2_ref[f] = (xhat * gain + shift).astype(BF16)
     n2_gather = QuadGather(f, c, n2_ref, n_s, n_r)
     n2_gather.begin()
+    gather1.steps(2)
+    if gather2 is not None:
+        gather2.begin(local2.start)
+    gather1.finish()
+    local1.wait()
     first_bias = spread_vector(small_ref[:, pl.ds(5 + f, 1), :].reshape(n, LANES), rows2)
 
     def enter(k):
@@ -847,27 +868,34 @@
         act_ref[r] = act.astype(BF16)
         slope_ref[r] = slope
 
-    gather2.step(2)
     enter(0)
     n2_gather.got(f ^ 1)
-    gather2.steps(3)
+    if gather2 is not None:
+        gather2.step(1)
     enter(1)
     n2_gather.relay()
+    if gather2 is not None:
+        gather2.step(2)
     enter(2)
+    if gather2 is not None:
+        gather2.steps(3)
     n2_gather.got(f ^ 3)
     enter(3)
-    gather2.finish()
-    local2.wait()
+    if gather2 is not None:
+        gather2.finish()
+        local2.wait()
+    bring2.wait()
+    second = w2g[...].reshape(quarter, width)
 
     for k in (3, 2, 1, 0):
         r = f ^ k
-        d_act = mm_t(cot_ref[r], w2g[...])
+        d_act = mm_t(cot_ref[r], second)
         dpre_ref[r] = (d_act * slope_ref[r]).astype(BF16)
         back_sum.put(k, mm_t(dpre_ref[r], w1g[...]))
         if k == 2:
             back_sum.cross()
     for k in (3, 2, 1, 0):
-        out_sum.put(k, mm(act_ref[f ^ k], w2g[...]))
+        out_sum.put(k, mm(act_ref[f ^ k], second))
     tile = 256
     all_tokens = 4 * tokens
 
@@ -916,6 +944,15 @@
             select = jnp.where(lane == e, column, select)
         da_ref[r] = d_attn.astype(BF16)
         gsel_ref[r] = select
+        to = r * groups + own_turn
+
+        @pl.when(to != c)
+        def _():
+            copy_to(da_ref.at[r], do_ref.at[own_slot], da_s.at[r], da_r.at[own_slot], f, to).start()
+
+        @pl.when(to == c)
+        def _():
+            do_ref[own_slot] = da_ref[r]
 
     line2.turn(1)
     leave(0)
@@ -947,8 +984,21 @@
     for one in (attn_sum, back_sum, out_sum, n2_gather, dml_gather):
         one.sent()
 
-
-def feed(n, x, cot, gates, o, wout, small, w1, w2):
+    def drain(i, _):
+        @pl.when(i * groups + own_turn != c)
+        def _():
+            copy_to(da_ref.at[i], do_ref.at[0], da_s.at[i], da_r.at[0], f, c).wait_send()
+
+        @pl.when(block_of(lax.rem(c, groups), i, groups) != c)
+        def _():
+            copy_to(da_ref.at[0], do_ref.at[i], da_s.at[0], da_r.at[i], f, c).wait_recv()
+
+        return 0
+
+    lax.fori_loop(0, 4, drain, 0)
+
+
+def feed(n, x, cot, gates, o, wout, small, w1, w2, w2e):
     t, d = x.shape
     quarter = w1.shape[1]
     line = n // 2
@@ -958,10 +1008,10 @@
             sds((t, d), BF16), sds((t, d), F32), sds((640, d), BF16), sds((line, d // n, quarter), BF16),
             sds((2, quarter // n, d), BF16), sds((4, t, LANES), BF16), sds((4, t, LANES), F32), sds((8, d), F32),
         ],
-        in_specs=[VMEM] * 7 + [ANY],
+        in_specs=[VMEM] * 6 + [ANY] * 3,
         out_specs=[VMEM] * 8,
         scratch_shapes=[
-            pltpu.VMEM((quarter, d), BF16), pltpu.VMEM((4, t, d), BF16),
+            pltpu.VMEM((d, quarter), BF16), pltpu.VMEM((n, quarter // n, d), BF16), pltpu.VMEM((4, t, d), BF16),
             pltpu.VMEM((4, t, quarter), BF16), pltpu.VMEM((4, t, quarter), F32), pltpu.VMEM((4, t, quarter), BF16),
             pltpu.VMEM((4, t, 640), BF16), pltpu.VMEM((4, t, d), BF16), pltpu.VMEM((t, d), F32),
             pltpu.VMEM((d, quarter), BF16), pltpu.VMEM((quarter, d), BF16),
@@ -969,13 +1019,13 @@
         ]
         + line_scratch(line, 2, 2 * quarter // n, d)
         + quad_sum_scratch(t, d) * 3
-        + [DMA((n,))] * 4 + [DMA((line,))] * 2 + line_sems(line, 2)
-        + [DMA((3,)), DMA((4,)), DMA((3,)), DMA((4,)), DMA((1,))],
+        + [DMA((n,))] * 8 + [DMA((line,))] * 2 + line_sems(line, 2)
+        + [DMA((3,)), DMA((4,)), DMA((3,)), DMA((4,)), DMA((3,)), pltpu.VMEM((4, t, LANES), BF16), DMA((4,)), DMA((4,))],
         compiler_params=pltpu.CompilerParams(
             collective_id=1, has_side_effects=True, vmem_limit_bytes=62 << 20
         ),
         name="feed",
-    )(x, cot, gates, o, wout, small, w1, w2)
+    )(x, cot, gates, o, wout, small, w1, w2, w2e)
 
 
 class LoneShare:
@@ -1022,15 +1072,15 @@
 
 def back_kernel(
     n, far_kv,
-    da_ref, gwout_ref, s1_ref, s2_ref, qcat_ref, qpos_ref, kv_ref, lse_ref, of_ref,
+    do_ref, gwout_ref, s1_ref, s2_ref, qcat_ref, qpos_ref, kv_ref, lse_ref, of_ref,
     tok_ref, p1_ref, ev_ref, gates_ref, gsel_ref, x_ref, small_ref, dmid_ref, vec_ref, table_ref,
     din_ref, gp_ref, gq_ref, g1_ref, g2_ref, go_ref, vq_ref, dkv_ref,
-    do_ref, delta_ref, grad_ref, kcat_ref, acc_ref, ring_ref, pin_ref, drel_ref, dqs_ref, dq_ref, part_ref, dp_ref,
+    delta_ref, grad_ref, kcat_ref, acc_ref, ring_ref, pin_ref, drel_ref, dqs_ref, dq_ref, part_ref, dp_ref,
     gpa_ref, gpb_ref, mine_ref, vin_ref,
     s0, s1, s2, s3, s4, s5, s6,
     p0, p1, p2, p3, p4, p5, p6, u1, u2, u5, u6,
     fin2, got2, two_s, two_r, w0, w1, w2, w3, w4, w5, w6, y1, y2, y5, y6, goty, swap_s, swap_r,
-    da_s, da_r, kv_s, kv_r, pin_r, dq_s, dq_r, gp_s, gp_r, gq_s, gq_r, g1_s, g1_r, g2_s, g2_r, go_s, go_r,
+    kv_s, kv_r, pin_r, dq_s, dq_r, gp_s, gp_r, gq_s, gq_r, g1_s, g1_r, g2_s, g2_r, go_s, go_r,
     vc_s, vc_r, vf_s, vf_r, loc,
 ):
     f, c = lax.axis_index("fsdp"), lax.axis_index("ctx")
@@ -1042,20 +1092,6 @@
     rows = width // n
     greet(f, c, 4, n)
 
-    def send_da(s, _):
-        to = s * groups + own_turn
-
-        @pl.when(to != c)
-        def _():
-            copy_to(da_ref.at[s], do_ref.at[own_slot], da_s.at[s], da_r.at[own_slot], f, to).start()
-
-        @pl.when(to == c)
-        def _():
-            do_ref[own_slot] = da_ref[s]
-
-        return 0
-
-    lax.fori_loop(0, 4, send_da, 0)
     sub_out = p0.shape[0] // max(1, groups // 2)
     cut = gwout_ref.shape[1] // sub_out
     sum_out = LineSum(
@@ -1076,18 +1112,15 @@
     swap_two = copy_to(s2_ref.at[1], got2, two_s, two_r, f, pair_to)
     swap_late = copy_to(y2.at[pair_to], goty, swap_s, swap_r, f, pair_to)
 
-    def prepare(i, _):
-        @pl.when(block_of(turn, i, groups) != c)
-        def _():
-            copy_to(da_ref.at[0], do_ref.at[i], da_s.at[0], da_r.at[i], f, c).wait_recv()
-
-        delta_ref[i] = jnp.sum(do_ref[i].astype(F32) * of_ref[i], axis=1, keepdims=True)
-        grad_ref[i] = jnp.zeros((tokens, width + LANES), F32)
-        return 0
-
-    lax.fori_loop(0, 4, prepare, 0)
     sum_out.begin()
     swap_two.start()
+
+    def prepare(i, _):
+        delta_ref[i] = jnp.sum(do_ref[i].astype(F32).T * of_ref[i], axis=0, keepdims=True)
+        grad_ref[i] = jnp.zeros((tokens, width + LANES), F32)
+        return 0
+
+    lax.fori_loop(0, 4, prepare, 0)
     row_in = lax.broadcasted_iota(jnp.int32, (tokens, tokens), 0)
     col_in = lax.broadcasted_iota(jnp.int32, (tokens, tokens), 1)
     lane = lax.broadcasted_iota(jnp.int32, (tokens, LANES), 1)
@@ -1185,13 +1218,13 @@
 
         def query_block(i, _):
             gap = (block_of(turn, i, groups) - kb) * tokens
-            scores = mm_t(qcat_ref[i], kcat_ref[...])
-            probs = jnp.where(col_in <= row_in + gap, jnp.exp(scores - lse_ref[i]), 0.0)
-            d_probs = mm_t(do_ref[i], kv_ref[kb, :, 128:256])
+            scores = mm_t(kcat_ref[...], qcat_ref[i])
+            probs = jnp.where(row_in <= col_in + gap, jnp.exp(scores - lse_ref[i]), 0.0)
+            d_probs = mm_t(kv_ref[kb, :, 128:256], do_ref[i])
             d_scores = (probs * (d_probs - delta_ref[i])).astype(BF16)
-            acc_ref[now, :, 0:128] += mm_left_t(d_scores, qcat_ref[i, :, width:])
-            acc_ref[now, :, 128:256] += mm_left_t(probs.astype(BF16), do_ref[i])
-            grad_ref[i] += mm(d_scores, kcat_ref[...])
+            acc_ref[now, :, 0:128] += mm(d_scores, qcat_ref[i, :, width:])
+            acc_ref[now, :, 128:256] += mm(probs.astype(BF16), do_ref[i])
+            grad_ref[i] += mm_left_t(d_scores, kcat_ref[...])
             return 0
 
         lax.fori_loop(first, 4, query_block, 0)
@@ -1213,23 +1246,16 @@
         def _():
             pass_on(kb - 1)
 
-        @pl.when(jnp.logical_and(now == 1, kb < n - 1))
-        def _():
-            sum_one.turn(kb // 2)
-
-        @pl.when(jnp.logical_and(now == 0, kb >= 4))
-        def _():
-            sum_out.turn(kb // 2 - 2)
+        @pl.when(jnp.logical_and(now == 0, kb >= 2))
+        def _():
+            sum_one.turn(kb // 2 - 1)
+
 
         return 0
 
     lax.fori_loop(0, n, key_block, 0)
     pass_on(n - 1)
-    sum_out.turn(n // 2 - 2)
-    swap_two.wait()
-    fin2[...] = (s2_ref[0].astype(F32) + got2[...].astype(F32)).astype(BF16)
-    sum_one.finish()
-    sum_out.finish()
+    sum_out.turn(0)
     share_out = LoneShare(sum_out, go_ref, go_s, go_r)
     gathers = []
     def hand_out(held, out, send, recv):
@@ -1238,10 +1264,6 @@
         gather = QuadGather(f, c, out, send, recv)
         gather.begin(held)
         gathers.append((gather, local))
-
-    hand_out(fin2, g2_ref, g2_s, g2_r)
-    hand_out(u2.at[c // 2], g1_ref, g1_s, g1_r)
-    share_out.begin()
 
     all_tokens = 4 * tokens
     d_rel = drel_ref[...].reshape(all_tokens, width)
@@ -1296,6 +1318,7 @@
 
     lax.fori_loop(0, 4, ring_drain, 0)
     lax.fori_loop(0, 4, collect, 0)
+    sum_out.turn(1)
     tile = 256
 
     def weight_tile(i, _):
@@ -1310,20 +1333,29 @@
     lax.fori_loop(0, width // tile, weight_tile, 0)
     sum_in.begin()
     sum_late.turn(0)
-    for gather, _ in gathers:
-        gather.relay()
-    share_out.relay()
+    lax.fori_loop(2, n // 2 - 1, lambda k, u: (sum_out.turn(k), u)[1], 0)
     in_sum = QuadSum(f, c, s0, s1, s2, s3, s4, s5, s6)
     for k in (3, 2, 1, 0):
         weights = p1_ref[:, :, 0:896].reshape(width, 896)
         in_sum.put(k, mm_t(dp_ref[f ^ k], weights))
         if k == 2:
             in_sum.cross()
-    lax.fori_loop(1, n // 2 - 1, lambda k, u: (sum_late.turn(k), u)[1], 0)
+    swap_two.wait()
+    fin2[...] = (s2_ref[0].astype(F32) + got2[...].astype(F32)).astype(BF16)
+    sum_one.finish()
+    sum_late.turn(1)
+    sum_out.finish()
+    hand_out(fin2, g2_ref, g2_s, g2_r)
+    hand_out(u2.at[c // 2], g1_ref, g1_s, g1_r)
+    share_out.begin()
+    lax.fori_loop(2, n // 2 - 1, lambda k, u: (sum_late.turn(k), u)[1], 0)
     sum_in.turn(0)
     sum_late.finish()
     swap_late.start()
     lax.fori_loop(1, n // 2 - 1, lambda k, u: (sum_in.turn(k), u)[1], 0)
+    for gather, _ in gathers:
+        gather.relay()
+    share_out.relay()
     d_norm = in_sum.total()
     xhat, spread = layer_stats(x_ref[...].astype(F32))
     gain = spread_vector(small_ref[:, 0, :], width // n)
@@ -1369,10 +1401,6 @@
     in_sum.sent()
 
     def drain(i, _):
-        @pl.when(i * groups + own_turn != c)
-        def _():
-            copy_to(da_ref.at[i], do_ref.at[0], da_s.at[i], da_r.at[0], f, c).wait_send()
-
         @pl.when(block_of(turn, i, groups) != c)
         def _():
             copy_to(dqs_ref.at[i], dq_ref.at[0], dq_s.at[i], dq_r.at[0], f, c).wait_send()
@@ -1380,6 +1408,10 @@
         return 0
 
     lax.fori_loop(0, 4, drain, 0)
+
+
+def early_rows(count):
+    return count // 2 if count % 32 == 0 else count
 
 
 def cuts(count):
@@ -1421,7 +1453,7 @@
         in_specs=[VMEM] * 19,
         out_specs=[VMEM, ANY, ANY, ANY, ANY, ANY, VMEM, ANY if far_kv else VMEM],
         scratch_shapes=[
-            pltpu.VMEM((4, t, LANES), BF16), pltpu.VMEM((4, t, 1), F32), pltpu.VMEM((4, t, d + LANES), F32),
+            pltpu.VMEM((4, 1, t), F32), pltpu.VMEM((4, t, d + LANES), F32),
             pltpu.VMEM((t, d + LANES), BF16), pltpu.VMEM((2, t, 256), F32), pltpu.VMEM((4, t, 256), BF16),
             pltpu.VMEM((line, t, 256), BF16),
             pltpu.VMEM((4, t, d), BF16), pltpu.VMEM((4, t, LANES), BF16), pltpu.VMEM((4, t, LANES), BF16),
@@ -1438,7 +1470,7 @@
         + line_scratch(line, 2, 2 * rows, half) + line_sems(line, 2)
         + [pltpu.VMEM((rows, half), BF16), DMA, DMA]
         + [
-            DMA((4,)), DMA((4,)), DMA((4,)), DMA((line,)), DMA((line,)), DMA((4,)), DMA((4,)), DMA((3,)), DMA((4,)),
+            DMA((4,)), DMA((line,)), DMA((line,)), DMA((4,)), DMA((4,)), DMA((3,)), DMA((4,)),
             DMA((3,)), DMA((4,)), DMA((3,)), DMA((4,)), DMA((3,)), DMA((4,)), DMA((2,)), DMA, DMA((n,)), DMA((n,)), DMA((4,)), DMA((4,)), DMA((5,)),
         ],
         compiler_params=pltpu.CompilerParams(
@@ -1499,6 +1531,73 @@
     return aux, p1, small, pieces, bias
 
 
+def unpack_kernel(
+    gp_ref, gq_ref, g1_ref, g2_ref, go_ref, vq_ref, y_ref, din_ref,
+    query_ref, key_ref, rel_ref, value_ref, vsel_ref, osel_ref, one_ref, two_ref, out_ref,
+    gain1_ref, shift1_ref, gain2_ref, shift2_ref, b2_ref, b1_ref, u_ref, v_ref, y_out, din_out,
+    heads_ref,
+):
+    c = lax.axis_index("ctx")
+    rows, half = gp_ref.shape[1], gp_ref.shape[2]
+    y_out[...] = y_ref[...]
+    din_out[...] = din_ref[...]
+
+    def block(h, k):
+        ref, spot = (gp_ref, k * LANES) if k * LANES < half else (gq_ref, k * LANES - half)
+        return ref[h, :, spot : spot + LANES].astype(F32).T
+
+    def place(ref, start, piece):
+        ref[start : start + 56, :] = piece[0:56]
+        ref[start + 56 : start + 112, :] = piece[64:120]
+
+    for h in range(4):
+        for ref, k in ((query_ref, 0), (key_ref, 1), (rel_ref, 7)):
+            place(ref, 112 * h, block(h, k))
+        for e in range(5):
+            piece = block(h, 2 + e)
+            place(value_ref, 560 * h + 112 * e, piece)
+            vsel_ref[5 * h + e : 5 * h + e + 1, :] = piece[SPOT_A : SPOT_A + 1]
+            osel_ref[5 * h + e : 5 * h + e + 1, :] = piece[SPOT_B : SPOT_B + 1]
+    part = g2_ref.shape[1]
+    for h in range(4):
+        two_ref[h * part : (h + 1) * part, :] = g2_ref[h].astype(F32)
+        for k in range(g1_ref.shape[2] // part):
+            spot = (4 * k + h) * part
+            one_ref[:, spot : spot + part] = g1_ref[h, :, k * part : (k + 1) * part].astype(F32)
+    for k in range(go_ref.shape[0]):
+        out_ref[56 * k : 56 * k + 56, :] = go_ref[k, 0:56, :].astype(F32)
+    own = pl.ds(pl.multiple_of(c * rows, rows), rows)
+    for ref, k in ((gain2_ref, 0), (shift2_ref, 1), (b2_ref, 2), (gain1_ref, 4), (shift1_ref, 5)):
+        ref[...] = sum(vq_ref[h, k : k + 1, own] for h in range(4))
+    for h in range(4):
+        b1_ref[:, h * part : (h + 1) * part] = vq_ref[h, 3:4, own]
+    lane = lax.broadcasted_iota(jnp.int32, (8, LANES), 1)
+    for ref, k in ((u_ref, 6), (v_ref, 7)):
+        for h in range(4):
+            heads_ref[h : h + 1, :] = vq_ref[h, k : k + 1, 0:LANES]
+        value = heads_ref[...]
+        moved = jnp.where(lane < 56, value, pltpu.roll(value, LANES - 8, 1))
+        ref[...] = moved[0:4, 0:112]
+
+
+def unpack(gp, gq, g1, g2, go, vq, y, d_in):
+    rows, part, d = gp.shape[1], g2.shape[1], g2.shape[2]
+    shapes = [
+        (448, rows), (448, rows), (448, rows), (2240, rows), (20, rows), (20, rows), (rows, 4 * g1.shape[2]),
+        (4 * part, d), (go.shape[0] * 56, d), (1, rows), (1, rows), (1, rows), (1, rows), (1, rows),
+        (1, 4 * part), (4, 112), (4, 112),
+    ]
+    return pl.pallas_call(
+        unpack_kernel,
+        out_shape=[sds(shape, F32) for shape in shapes] + [sds(y.shape, BF16), sds(d_in.shape, F32)],
+        in_specs=[VMEM] * 8,
+        out_specs=[VMEM] * (len(shapes) + 2),
+        scratch_shapes=[pltpu.VMEM((8, LANES), F32)],
+        compiler_params=pltpu.CompilerParams(vmem_limit_bytes=62 << 20),
+        name="unpack",
+    )(gp, gq, g1, g2, go, vq, y, d_in)
+
+
 def drop_pads(v, group):
     lead = v.shape[:-1]
     wide = group * 8 // 7
@@ -1522,18 +1621,27 @@
     rows, hidden = w1.shape
     part = hidden // n // 4
     w1_own = lax.dynamic_index_in_dim(w1.reshape(rows, n, 4, part), f, 2, keepdims=False).reshape(rows, n * part)
-    tok, p1g, smallg, woutg, w1g, cotg, ev, gates, o, qcat, qpos, kv, lse, of = attend(
-        n, x, aux, cot, p1, small, pieces, w1_own, bias, table
+    tok, p1g, smallg, woutg, w2e, cotg, ev, gates, o, qcat, qpos, kv, lse, of = attend(
+        n, x, aux, cot, p1, small, pieces, w2, bias, table
     )
     block = 640 // g
-    out, dmid, gwout, s1, s2, da, gsel, vec = feed(
-        n, x, cotg, gates, o, woutg[:, :block].reshape(640, d), smallg, w1g.reshape(d, n * part), w2
+    out, dmid, gwout, s1, s2, d_o, gsel, vec = feed(
+        n, x, cotg, gates, o, woutg[:, :block].reshape(640, d), smallg, w1_own, w2, w2e
     )
     gwout = gwout.reshape(g, block, d)
     gwout = jnp.pad(gwout, ((0, 0), (0, pieces.shape[0] - block), (0, 0)))
     d_in, gp, gq, g1, g2, go, vq, _ = back(
-        n, da, gwout, s1, s2, qcat, qpos, kv, lse, of, tok, p1g, ev, gates, gsel, x, smallg, dmid, vec, table
+        n, d_o, gwout, s1, s2, qcat, qpos, kv, lse, of, tok, p1g, ev, gates, gsel, x, smallg, dmid, vec, table
     )
+    if group == 56 and part == LANES and rows == LANES:
+        (
+            g_query, g_key, g_rel, g_value, g_vsel, g_osel, g_one, g_two, g_out,
+            gain1, shift1, gain2, shift2, g_b2, g_b1, g_u, g_v, out, d_in,
+        ) = unpack(gp, gq, g1, g2, go.reshape(-1, 64, d), vq, out, d_in)
+        return (
+            out, d_in, gain1[0], shift1[0], g_query.T, g_key.T, g_rel.T, g_u, g_v, g_vsel.T, g_value.T, g_osel.T, g_out,
+            gain2[0], shift2[0], g_one, g_b1[0], g_two, g_b2[0],
+        )
     gp = jnp.transpose(jnp.concatenate([gp, gq], axis=-1), (1, 0, 2))
     g_query = drop_pads(gp[..., 0:128], group).reshape(rows, 448).astype(F32)
     g_key = drop_pads(gp[..., 128:256], group).reshape(rows, 448).astype(F32)

time: 396 us -> 373 us (0.942)
  local copies, waits for them, and re-layouts: 25.5 us -> 12.5 us
  other arithmetic: 12.6 us -> 4.16 us
  Pallas kernels: 352 us -> 348 us
    pallas_call x1, Pallas kernels: 91.5 us -> 106 us  [feed(): pl.pallas_call(functools.partial(feed_kernel, n), out_shape=[sds((t, d),...]
    pallas_call x1, Pallas kernels: 154 us -> 140 us  [back(): pl.pallas_call(functools.partial(back_kernel, n, far_kv), out_shape=[sds(...]
    pallas_call x1, Pallas kernels: 106 us -> 96.1 us  [attend(): pl.pallas_call(functools.partial(attend_kernel, n), out_shape=[sds((4, t,...]
    convert_element_type x7 -> x0, other arithmetic: 7.39 us -> none  [the longest x1 2.91 us: on_device(): g_two = g2.reshape(-1, d).astype(F32)]
    pallas_call x0 -> x1, Pallas kernels: none -> 6.29 us  [unpack(): pl.pallas_call(unpack_kernel, out_shape=[sds(shape, F32) for shape in sha...]
    convert_element_type x5 -> x0, local copies, waits for them, and re-layouts: 4.54 us -> none  [the longest x3 3.34 us: on_device(): jnp.transpose(g1.reshape(4, rows, n, part), (1, 2, 0, 3))]
where the time goes in v3:
time: 373 us; the launch traced here: 366 us
  Pallas kernels  348 us (93%)
  local copies, waits for them, and re-layouts  12.5 us (3%)
  other arithmetic  4.16 us (1%)
    pallas_call x1, Pallas kernels, back(): pl.pallas_call(functools.partial(back_kernel, n, far_kv), out_shape=[sds(...  140 us
    pallas_call x1, Pallas kernels, feed(): pl.pallas_call(functools.partial(feed_kernel, n), out_shape=[sds((t, d),...  106 us
    pallas_call x1, Pallas kernels, attend(): pl.pallas_call(functools.partial(attend_kernel, n), out_shape=[sds((4, t,...  96.1 us

profile of v3, /device:TPU:15, one launch (start us, length us, event | category | flops | bytes accessed | tf_op | source)
XLA Modules:
  0.0 366.5 jit_solution(4437045446900292043)
XLA Ops:
  0.7 1.0 copy-done
  1.8 0.8 reshape.148
  2.7 0.8 reshape.150
  3.5 0.6 maximum_convert_fusion.bias_ref
  4.1 0.7 and_select_fusion.1
  4.8 1.5 concatenate.20
  6.4 0.6 pad_convert_fusion.small_ref
  7.0 0.8 reshape.139
  7.7 0.7 reshape.138
  8.4 0.8 constant_dynamic-slice_fusion.3
  9.3 0.7 convert_reduce_fusion
  10.2 0.8 constant_dynamic-slice_fusion
  11.4 0.7 maximum_maximum_fusion.aux_ref
  12.2 0.2 copy.75
  12.4 0.2 copy.74
  12.7 0.7 pad_maximum_fusion.p1_ref
  13.5 0.9 pad.37
  14.4 0.8 reshape.153
  15.2 1.5 dynamic-slice_reduce_fusion
  16.7 0.8 copy.84
  17.4 96.1 %attend.1 = (bf16[4,256,1152]{2,1,0:T(8,128)(2,1)}, bf16[8,128,1024]{2,1,0:T(8,128)(2,1)}, f32[8,16,128]{2,1,0:T(8,128)}, bf16[2,320,1024]{2,1,0:T(8,128)(2,1)},...) custom-call(bf16[256,1024]{1,0:T(8,128)(2,1)} %x_ref.5, ...), custom_call_target="tpu_custom_call" | custom-call | tf_op jit(solution)/shard_map/attend/pallas_call | solution.py:549
  113.6 106.1 %feed.1 = (bf16[256,1024]{1,0:T(8,128)(2,1)}, f32[256,1024]{1,0:T(8,128)}, bf16[640,1024]{1,0:T(8,128)(2,1)}, bf16[4,128,1024]{2,1,0:T(8,128)(2,1)}, bf16[2,128,...) custom-call(bf16[256,1024]{1,0:T(8,128)(2,1)} %x_ref.5, ...), custom_call_target="tpu_custom_call" | custom-call | tf_op jit(solution)/shard_map/feed/pallas_call | solution.py:1005
  219.7 139.9 %back.1 = (f32[256,1024]{1,0:T(8,128)}, bf16[4,128,512]{2,1,0:T(8,128)(2,1)}, bf16[4,128,512]{2,1,0:T(8,128)(2,1)}, bf16[4,128,1024]{2,1,0:T(8,128)(2,1)}, bf16[...) custom-call(bf16[4,256,128]{2,1,0:T(8,128)(2,1)} %get-tuple-element., ...), custom_call_target="tpu_custom_call" | custom-call | tf_op jit(solution)/shard_map/back/pallas_call | solution.py:1446
  359.6 6.3 %unpack.1 = (f32[448,128]{1,0:T(8,128)}, f32[448,128]{1,0:T(8,128)}, f32[448,128]{1,0:T(8,128)}, f32[2240,128]{1,0:T(8,128)}, f32[20,128]{1,0:T(8,128)}, /*index...) custom-call(bf16[4,128,512]{2,1,0:T(8,128)(2,1)} %get-tuple-element., ...), custom_call_target="tpu_custom_call" | custom-call | tf_op jit(solution)/shard_map/unpack/pallas_call | solution.py:1590
  (31 shorter events, 1.2 us)
Async XLA Ops:
  0.7 1.1 copy-start
  7.0 6.5 %copy-start.2 = (bf16[280,1024]{1,0:T(8,128)(2,1)S(1)}, bf16[280,1024]{1,0:T(8,128)(2,1)}, u32[]{:S(2)}) copy-start(bf16[280,1024]{1,0:T(8,128)(2,1)} %param.37) | copy-start | bytes 1720324
  12.1 2.3 copy-start.1

commit v4 on v3

--- a/solution.py
+++ b/solution.py
@@ -192,12 +192,16 @@
 
 
 class QuadGather:
-    def __init__(self, f, c, out, send, recv):
+    def __init__(self, f, c, out, send, recv, part=None):
         self.f, self.c, self.out, self.send, self.recv = f, c, out, send, recv
+        self.part = part
+
+    def at(self, slot):
+        return self.out.at[slot] if self.part is None else self.out.at[slot, self.part, :]
 
     def copy(self, slot, k, to, src=None):
-        src = self.out.at[slot] if src is None else src
-        return copy_to(src, self.out.at[slot], self.send.at[k], self.recv.at[slot], to, self.c)
+        src = self.at(slot) if src is None else src
+        return copy_to(src, self.at(slot), self.send.at[k], self.recv.at[slot], to, self.c)
 
     def begin(self, src=None):
         self.copy(self.f, 1, self.f ^ 2, src).start()
@@ -804,8 +808,9 @@
     x_ref, cot_ref, gates_ref, o_ref, wout_ref, small_ref, w1_ref, w2_ref, w2e_ref,
     out_ref, dmid_ref, gwout_ref, s1_ref, s2_ref, do_ref, gsel_ref, vec_ref,
     w1g, w2g, n2_ref, act_ref, slope_ref, dpre_ref, mixed_ref, dml_ref, mid_ref, gw1_ref, gw2_ref, got1, in2, stage2,
-    a0, a1, a2, a3, a4, a5, a6, b0, b1, b2, b3, b4, b5, b6, e0, e1, e2, e3, e4, e5, e6,
-    w1_r, w1_a, w1_b, w1_c, w2_r, w2_a, w2_b, w2_c, h1_s, h1_r, h2_s, h2_r, n_s, n_r, d_s, d_r, loc, da_ref, da_s, da_r,
+    a0, a1, a2, a3, a4, a5, a6, i0, i1, i2, i3, i4, i5, i6, b0, b1, b2, b3, b4, b5, b6, j0, j1, j2, j3, j4, j5, j6,
+    e0, e1, e2, e3, e4, e5, e6,
+    w1_r, w1_a, w1_b, w1_c, w2_r, w2_a, w2_b, w2_c, h1_s, h1_r, h2_s, h2_r, n_s, n_r, d_s, d_r, m_s, m_r, k_s, k_r, loc, da_ref, da_s, da_r,
 ):
     f, c = lax.axis_index("fsdp"), lax.axis_index("ctx")
     tokens, width = x_ref.shape
@@ -833,28 +838,32 @@
         local2 = pltpu.make_async_copy(own2, at2(c), loc.at[2])
     pair1 = PairSum(f, c, n, rows_of(gw1_ref, rows1), got1, s1_ref, h1_s, h1_r)
     line2 = LineSum(f, c, n, lambda o, sub: rows_of(gw2_ref, rows2)(2 * o + sub), in2, stage2, h2_s, h2_r, subs=2)
-    attn_sum = QuadSum(f, c, a0, a1, a2, a3, a4, a5, a6)
-    back_sum = QuadSum(f, c, b0, b1, b2, b3, b4, b5, b6)
+    attn_sum = (QuadSum(f, c, a0, a1, a2, a3, a4, a5, a6), QuadSum(f, c, i0, i1, i2, i3, i4, i5, i6))
+    back_sum = (QuadSum(f, c, b0, b1, b2, b3, b4, b5, b6), QuadSum(f, c, j0, j1, j2, j3, j4, j5, j6))
+    span = tokens // 2
+    halves = (slice(0, span), slice(span, tokens))
     out_sum = QuadSum(f, c, e0, e1, e2, e3, e4, e5, e6)
 
-    for k in (3, 2, 1, 0):
-        r = f ^ k
-        for e in range(5):
-            mixed_ref[r, :, e * LANES : (e + 1) * LANES] = (
-                gates_ref[r, :, e : e + 1] * o_ref[r].astype(F32)
-            ).astype(BF16)
-        attn_sum.put(k, mm(mixed_ref[r], wout_ref[...]))
-        if k == 2:
-            attn_sum.cross()
+    for half, one in zip(halves, attn_sum):
+        for k in (3, 2, 1, 0):
+            r = f ^ k
+            for e in range(5):
+                mixed_ref[r, half, e * LANES : (e + 1) * LANES] = (
+                    gates_ref[r, half, e : e + 1] * o_ref[r, half, :].astype(F32)
+                ).astype(BF16)
+            one.put(k, mm(mixed_ref[r, half, :], wout_ref[...]))
+            if k == 2:
+                one.cross()
     gather1.step(1)
-    middle = x_ref[...].astype(F32) + attn_sum.total()
-    mid_ref[...] = middle
-    xhat, scale = layer_stats(middle)
     gain = spread_vector(small_ref[:, 2, :], width // n)
     shift = spread_vector(small_ref[:, 3, :], width // n)
-    n2_ref[f] = (xhat * gain + shift).astype(BF16)
-    n2_gather = QuadGather(f, c, n2_ref, n_s, n_r)
-    n2_gather.begin()
+    n2_gather = (QuadGather(f, c, n2_ref, n_s, n_r, halves[0]), QuadGather(f, c, n2_ref, m_s, m_r, halves[1]))
+    for half, one, gather in zip(halves, attn_sum, n2_gather):
+        middle = x_ref[half, :].astype(F32) + one.total()
+        mid_ref[half, :] = middle
+        xhat, _ = layer_stats(middle)
+        n2_ref[f, half, :] = (xhat * gain + shift).astype(BF16)
+        gather.begin()
     gather1.steps(2)
     if gather2 is not None:
         gather2.begin(local2.start)
@@ -868,34 +877,24 @@
         act_ref[r] = act.astype(BF16)
         slope_ref[r] = slope
 
+    def got(pair, slot):
+        for gather in pair:
+            gather.got(slot)
+
     enter(0)
-    n2_gather.got(f ^ 1)
+    got(n2_gather, f ^ 1)
+    n2_gather[0].relay()
     if gather2 is not None:
         gather2.step(1)
     enter(1)
-    n2_gather.relay()
+    n2_gather[1].relay()
     if gather2 is not None:
         gather2.step(2)
     enter(2)
     if gather2 is not None:
         gather2.steps(3)
-    n2_gather.got(f ^ 3)
+    got(n2_gather, f ^ 3)
     enter(3)
-    if gather2 is not None:
-        gather2.finish()
-        local2.wait()
-    bring2.wait()
-    second = w2g[...].reshape(quarter, width)
-
-    for k in (3, 2, 1, 0):
-        r = f ^ k
-        d_act = mm_t(cot_ref[r], second)
-        dpre_ref[r] = (d_act * slope_ref[r]).astype(BF16)
-        back_sum.put(k, mm_t(dpre_ref[r], w1g[...]))
-        if k == 2:
-            back_sum.cross()
-    for k in (3, 2, 1, 0):
-        out_sum.put(k, mm(act_ref[f ^ k], second))
     tile = 256
     all_tokens = 4 * tokens
 
@@ -911,19 +910,39 @@
 
     weight_tile(act_ref, cot_ref, gw2_ref)
     line2.turn(0)
+    if gather2 is not None:
+        gather2.finish()
+        local2.wait()
+    bring2.wait()
+    second = w2g[...].reshape(quarter, width)
+
+    for k in (3, 2, 1, 0):
+        r = f ^ k
+        d_act = mm_t(cot_ref[r], second)
+        dpre_ref[r] = (d_act * slope_ref[r]).astype(BF16)
+        term = mm_t(dpre_ref[r], w1g[...])
+        for half, one in zip(halves, back_sum):
+            one.put(k, term[half])
+        if k == 2:
+            for one in back_sum:
+                one.cross()
     weight_tile(n2_ref, dpre_ref, gw1_ref)
     pair1.begin()
-    d_norm = back_sum.total()
-    xhat, scale = layer_stats(mid_ref[...])
-    d_middle = cot_ref[f].astype(F32) + layer_back(d_norm, gain, xhat, scale)
-    dmid_ref[...] = d_middle
-    dml_ref[f] = d_middle.astype(BF16)
-    dml_gather = QuadGather(f, c, dml_ref, d_s, d_r)
-    dml_gather.begin()
+    line2.turn(1)
+    for k in (3, 2, 1, 0):
+        out_sum.put(k, mm(act_ref[f ^ k], second))
+    vec_ref[...] = jnp.zeros_like(vec_ref)
+    dml_gather = (QuadGather(f, c, dml_ref, d_s, d_r, halves[0]), QuadGather(f, c, dml_ref, k_s, k_r, halves[1]))
+    for half, one, gather in zip(halves, back_sum, dml_gather):
+        d_norm = one.total()
+        xhat, scale = layer_stats(mid_ref[half, :])
+        d_middle = cot_ref[f, half, :].astype(F32) + layer_back(d_norm, gain, xhat, scale)
+        dmid_ref[half, :] = d_middle
+        dml_ref[f, half, :] = d_middle.astype(BF16)
+        gather.begin()
+        vec_ref[0:1, :] += jnp.sum(d_norm * xhat, axis=0, keepdims=True)
+        vec_ref[1:2, :] += jnp.sum(d_norm, axis=0, keepdims=True)
     out_sum.cross()
-    vec_ref[...] = jnp.zeros_like(vec_ref)
-    vec_ref[0:1, :] = jnp.sum(d_norm * xhat, axis=0, keepdims=True)
-    vec_ref[1:2, :] = jnp.sum(d_norm, axis=0, keepdims=True)
     vec_ref[2:3, :] = jnp.sum(cot_ref[f].astype(F32), axis=0, keepdims=True)
     total = jnp.zeros((1, quarter), F32)
     for r in range(4):
@@ -954,14 +973,14 @@
         def _():
             do_ref[own_slot] = da_ref[r]
 
-    line2.turn(1)
+    line2.turn(2)
     leave(0)
-    dml_gather.got(f ^ 1)
+    got(dml_gather, f ^ 1)
     leave(1)
-    dml_gather.relay()
-    line2.turn(2)
+    dml_gather[0].relay()
+    dml_gather[1].relay()
     leave(2)
-    dml_gather.got(f ^ 3)
+    got(dml_gather, f ^ 3)
     leave(3)
 
     def out_tile(i, _):
@@ -981,7 +1000,7 @@
     s2_ref[1] = stage2[own + 1 - 2 * lax.rem(c, 2)]
     line2.sent()
     pair1.finish()
-    for one in (attn_sum, back_sum, out_sum, n2_gather, dml_gather):
+    for one in attn_sum + back_sum + n2_gather + dml_gather + (out_sum,):
         one.sent()
 
     def drain(i, _):
@@ -1018,9 +1037,10 @@
             pltpu.VMEM((line, d // n, quarter), BF16),
         ]
         + line_scratch(line, 2, 2 * quarter // n, d)
-        + quad_sum_scratch(t, d) * 3
+        + quad_sum_scratch(t // 2, d) * 4
+        + quad_sum_scratch(t, d)
         + [DMA((n,))] * 8 + [DMA((line,))] * 2 + line_sems(line, 2)
-        + [DMA((3,)), DMA((4,)), DMA((3,)), DMA((4,)), DMA((3,)), pltpu.VMEM((4, t, LANES), BF16), DMA((4,)), DMA((4,))],
+        + [DMA((3,)), DMA((4,))] * 4 + [DMA((3,)), pltpu.VMEM((4, t, LANES), BF16), DMA((4,)), DMA((4,))],
         compiler_params=pltpu.CompilerParams(
             collective_id=1, has_side_effects=True, vmem_limit_bytes=62 << 20
         ),
@@ -1349,6 +1369,20 @@
     hand_out(u2.at[c // 2], g1_ref, g1_s, g1_r)
     share_out.begin()
     lax.fori_loop(2, n // 2 - 1, lambda k, u: (sum_late.turn(k), u)[1], 0)
+    d_norm = in_sum.total()
+    xhat, spread = layer_stats(x_ref[...].astype(F32))
+    gain = spread_vector(small_ref[:, 0, :], width // n)
+    din_ref[...] = dmid_ref[...] + layer_back(d_norm, gain, xhat, spread)
+    mine_ref[4:5, :] = jnp.sum(d_norm * xhat, axis=0, keepdims=True)
+    mine_ref[5:6, :] = jnp.sum(d_norm, axis=0, keepdims=True)
+
+    def vec_send(k, _):
+        to = lax.rem(c + k, n)
+        copy_to(mine_ref, vin_ref.at[c], vc_s.at[to], vc_r.at[c], f, to).start()
+        return 0
+
+    lax.fori_loop(1, n, vec_send, 0)
+    vin_ref[c] = mine_ref[...]
     sum_in.turn(0)
     sum_late.finish()
     swap_late.start()
@@ -1356,20 +1390,6 @@
     for gather, _ in gathers:
         gather.relay()
     share_out.relay()
-    d_norm = in_sum.total()
-    xhat, spread = layer_stats(x_ref[...].astype(F32))
-    gain = spread_vector(small_ref[:, 0, :], width // n)
-    din_ref[...] = dmid_ref[...] + layer_back(d_norm, gain, xhat, spread)
-    mine_ref[4:5, :] = jnp.sum(d_norm * xhat, axis=0, keepdims=True)
-    mine_ref[5:6, :] = jnp.sum(d_norm, axis=0, keepdims=True)
-
-    def vec_send(k, _):
-        to = lax.rem(c + k, n)
-        copy_to(mine_ref, vin_ref.at[c], vc_s.at[to], vc_r.at[c], f, to).start()
-        return 0
-
-    lax.fori_loop(1, n, vec_send, 0)
-    vin_ref[c] = mine_ref[...]
     swap_late.wait()
     y2[c] = (y2[c].astype(F32) + goty[...].astype(F32)).astype(BF16)
     hand_out(y2.at[c], gq_ref, gq_s, gq_r)

time: 373 us -> 358 us (0.960)
  the two profiles are of different devices: /device:TPU:15 before, /device:TPU:5 now
where the time goes in v4:
time: 358 us; the launch traced here: 354 us
  Pallas kernels  336 us (94%)
  local copies, waits for them, and re-layouts  12.5 us (3%)
  other arithmetic  4.16 us (1%)
    pallas_call x1, Pallas kernels, back(): pl.pallas_call(functools.partial(back_kernel, n, far_kv), out_shape=[sds(...  138 us
    pallas_call x1, Pallas kernels, feed(): pl.pallas_call(functools.partial(feed_kernel, n), out_shape=[sds((t, d),...  107 us
    pallas_call x1, Pallas kernels, attend(): pl.pallas_call(functools.partial(attend_kernel, n), out_shape=[sds((4, t,...  85 us

profile of v4, /device:TPU:5, one launch (start us, length us, event | category | flops | bytes accessed | tf_op | source)
XLA Modules:
  0.0 353.7 jit_solution(13482569267512477221)
XLA Ops:
  0.7 1.0 copy-done
  1.8 0.8 reshape.148
  2.7 0.8 reshape.150
  3.5 0.6 maximum_convert_fusion.bias_ref
  4.1 0.7 and_select_fusion.1
  4.8 1.5 concatenate.20
  6.4 0.6 pad_convert_fusion.small_ref
  7.0 0.8 reshape.139
  7.7 0.7 reshape.138
  8.4 0.8 constant_dynamic-slice_fusion.3
  9.3 0.7 convert_reduce_fusion
  10.2 0.8 constant_dynamic-slice_fusion
  11.4 0.7 maximum_maximum_fusion.aux_ref
  12.2 0.2 copy.75
  12.4 0.2 copy.74
  12.7 0.7 pad_maximum_fusion.p1_ref
  13.5 0.9 pad.37
  14.4 0.8 reshape.153
  15.2 1.5 dynamic-slice_reduce_fusion
  16.7 0.8 copy.84
  17.4 85.0 %attend.1 = (bf16[4,256,1152]{2,1,0:T(8,128)(2,1)}, bf16[8,128,1024]{2,1,0:T(8,128)(2,1)}, f32[8,16,128]{2,1,0:T(8,128)}, bf16[2,320,1024]{2,1,0:T(8,128)(2,1)},...) custom-call(bf16[256,1024]{1,0:T(8,128)(2,1)} %x_ref.5, ...), custom_call_target="tpu_custom_call" | custom-call | tf_op jit(solution)/shard_map/attend/pallas_call | solution.py:553
  102.4 106.9 %feed.1 = (bf16[256,1024]{1,0:T(8,128)(2,1)}, f32[256,1024]{1,0:T(8,128)}, bf16[640,1024]{1,0:T(8,128)(2,1)}, bf16[4,128,1024]{2,1,0:T(8,128)(2,1)}, bf16[2,128,...) custom-call(bf16[256,1024]{1,0:T(8,128)(2,1)} %x_ref.5, ...), custom_call_target="tpu_custom_call" | custom-call | tf_op jit(solution)/shard_map/feed/pallas_call | solution.py:1024
  209.3 137.9 %back.1 = (f32[256,1024]{1,0:T(8,128)}, bf16[4,128,512]{2,1,0:T(8,128)(2,1)}, bf16[4,128,512]{2,1,0:T(8,128)(2,1)}, bf16[4,128,1024]{2,1,0:T(8,128)(2,1)}, bf16[...) custom-call(bf16[4,256,128]{2,1,0:T(8,128)(2,1)} %get-tuple-element., ...), custom_call_target="tpu_custom_call" | custom-call | tf_op jit(solution)/shard_map/back/pallas_call | solution.py:1466
  347.2 6.3 %unpack.1 = (f32[448,128]{1,0:T(8,128)}, f32[448,128]{1,0:T(8,128)}, f32[448,128]{1,0:T(8,128)}, f32[2240,128]{1,0:T(8,128)}, f32[20,128]{1,0:T(8,128)}, /*index...) custom-call(bf16[4,128,512]{2,1,0:T(8,128)(2,1)} %get-tuple-element., ...), custom_call_target="tpu_custom_call" | custom-call | tf_op jit(solution)/shard_map/unpack/pallas_call | solution.py:1610
  (31 shorter events, 1.2 us)
Async XLA Ops:
  0.7 1.1 copy-start
  7.0 6.5 %copy-start.2 = (bf16[280,1024]{1,0:T(8,128)(2,1)S(1)}, bf16[280,1024]{1,0:T(8,128)(2,1)}, u32[]{:S(2)}) copy-start(bf16[280,1024]{1,0:T(8,128)(2,1)} %param.37) | copy-start | bytes 1720324
  12.1 2.3 copy-start.1

commit v5 on v4

--- a/solution.py
+++ b/solution.py
@@ -855,6 +855,8 @@
             if k == 2:
                 one.cross()
     gather1.step(1)
+    if gather2 is not None:
+        gather2.begin(local2.start)
     gain = spread_vector(small_ref[:, 2, :], width // n)
     shift = spread_vector(small_ref[:, 3, :], width // n)
     n2_gather = (QuadGather(f, c, n2_ref, n_s, n_r, halves[0]), QuadGather(f, c, n2_ref, m_s, m_r, halves[1]))
@@ -865,8 +867,6 @@
         n2_ref[f, half, :] = (xhat * gain + shift).astype(BF16)
         gather.begin()
     gather1.steps(2)
-    if gather2 is not None:
-        gather2.begin(local2.start)
     gather1.finish()
     local1.wait()
     first_bias = spread_vector(small_ref[:, pl.ds(5 + f, 1), :].reshape(n, LANES), rows2)
@@ -1266,9 +1266,9 @@
         def _():
             pass_on(kb - 1)
 
-        @pl.when(jnp.logical_and(now == 0, kb >= 2))
-        def _():
-            sum_one.turn(kb // 2 - 1)
+        @pl.when(jnp.logical_and(now == 1, kb < n - 1))
+        def _():
+            sum_one.turn(kb // 2)
 
 
         return 0

time: 358 us -> 356 us (level)
  the two profiles are of different devices: /device:TPU:5 before, /device:TPU:15 now
where the time goes in v5:
time: 356 us; the launch traced here: 349 us
  Pallas kernels  331 us (93%)
  local copies, waits for them, and re-layouts  12.5 us (4%)
  other arithmetic  4.16 us (1%)
    pallas_call x1, Pallas kernels, back(): pl.pallas_call(functools.partial(back_kernel, n, far_kv), out_shape=[sds(...  135 us
    pallas_call x1, Pallas kernels, attend(): pl.pallas_call(functools.partial(attend_kernel, n), out_shape=[sds((4, t,...  96.1 us
    pallas_call x1, Pallas kernels, feed(): pl.pallas_call(functools.partial(feed_kernel, n), out_shape=[sds((t, d),...  93.4 us

profile of v5, /device:TPU:15, one launch (start us, length us, event | category | flops | bytes accessed | tf_op | source)
XLA Modules:
  0.0 348.6 jit_solution(10316470495731955876)
XLA Ops:
  0.7 1.0 copy-done
  1.8 0.8 reshape.148
  2.7 0.8 reshape.150
  3.5 0.6 maximum_convert_fusion.bias_ref
  4.1 0.7 and_select_fusion.1
  4.8 1.5 concatenate.20
  6.4 0.6 pad_convert_fusion.small_ref
  7.0 0.8 reshape.139
  7.7 0.7 reshape.138
  8.4 0.8 constant_dynamic-slice_fusion.3
  9.3 0.7 convert_reduce_fusion
  10.2 0.8 constant_dynamic-slice_fusion
  11.4 0.7 maximum_maximum_fusion.aux_ref
  12.2 0.2 copy.75
  12.4 0.2 copy.74
  12.7 0.7 pad_maximum_fusion.p1_ref
  13.5 0.9 pad.37
  14.4 0.8 reshape.153
  15.2 1.5 dynamic-slice_reduce_fusion
  16.7 0.8 copy.84
  17.4 96.1 %attend.1 = (bf16[4,256,1152]{2,1,0:T(8,128)(2,1)}, bf16[8,128,1024]{2,1,0:T(8,128)(2,1)}, f32[8,16,128]{2,1,0:T(8,128)}, bf16[2,320,1024]{2,1,0:T(8,128)(2,1)},...) custom-call(bf16[256,1024]{1,0:T(8,128)(2,1)} %x_ref.5, ...), custom_call_target="tpu_custom_call" | custom-call | tf_op jit(solution)/shard_map/attend/pallas_call | solution.py:553
  113.6 93.4 %feed.1 = (bf16[256,1024]{1,0:T(8,128)(2,1)}, f32[256,1024]{1,0:T(8,128)}, bf16[640,1024]{1,0:T(8,128)(2,1)}, bf16[4,128,1024]{2,1,0:T(8,128)(2,1)}, bf16[2,128,...) custom-call(bf16[256,1024]{1,0:T(8,128)(2,1)} %x_ref.5, ...), custom_call_target="tpu_custom_call" | custom-call | tf_op jit(solution)/shard_map/feed/pallas_call | solution.py:1024
  207.0 135.1 %back.1 = (f32[256,1024]{1,0:T(8,128)}, bf16[4,128,512]{2,1,0:T(8,128)(2,1)}, bf16[4,128,512]{2,1,0:T(8,128)(2,1)}, bf16[4,128,1024]{2,1,0:T(8,128)(2,1)}, bf16[...) custom-call(bf16[4,256,128]{2,1,0:T(8,128)(2,1)} %get-tuple-element., ...), custom_call_target="tpu_custom_call" | custom-call | tf_op jit(solution)/shard_map/back/pallas_call | solution.py:1466
  342.1 6.3 %unpack.1 = (f32[448,128]{1,0:T(8,128)}, f32[448,128]{1,0:T(8,128)}, f32[448,128]{1,0:T(8,128)}, f32[2240,128]{1,0:T(8,128)}, f32[20,128]{1,0:T(8,128)}, /*index...) custom-call(bf16[4,128,512]{2,1,0:T(8,128)(2,1)} %get-tuple-element., ...), custom_call_target="tpu_custom_call" | custom-call | tf_op jit(solution)/shard_map/unpack/pallas_call | solution.py:1610
  (31 shorter events, 1.2 us)
Async XLA Ops:
  0.7 1.1 copy-start
  7.0 6.5 %copy-start.2 = (bf16[280,1024]{1,0:T(8,128)(2,1)S(1)}, bf16[280,1024]{1,0:T(8,128)(2,1)}, u32[]{:S(2)}) copy-start(bf16[280,1024]{1,0:T(8,128)(2,1)} %param.37) | copy-start | bytes 1720324
  12.1 2.3 copy-start.1

commit v6 on v5

--- a/solution.py
+++ b/solution.py
@@ -866,7 +866,9 @@
         xhat, _ = layer_stats(middle)
         n2_ref[f, half, :] = (xhat * gain + shift).astype(BF16)
         gather.begin()
-    gather1.steps(2)
+        if gather is n2_gather[0]:
+            gather1.step(2)
+    gather1.steps(3)
     gather1.finish()
     local1.wait()
     first_bias = spread_vector(small_ref[:, pl.ds(5 + f, 1), :].reshape(n, LANES), rows2)

time: 356 us -> 356 us (level)
  no operation moved by 1% of the time
where the time goes in v6:
time: 356 us; the launch traced here: 349 us
  Pallas kernels  331 us (93%)
  local copies, waits for them, and re-layouts  12.5 us (4%)
  other arithmetic  4.16 us (1%)
    pallas_call x1, Pallas kernels, back(): pl.pallas_call(functools.partial(back_kernel, n, far_kv), out_shape=[sds(...  135 us
    pallas_call x1, Pallas kernels, attend(): pl.pallas_call(functools.partial(attend_kernel, n), out_shape=[sds((4, t,...  96.1 us
    pallas_call x1, Pallas kernels, feed(): pl.pallas_call(functools.partial(feed_kernel, n), out_shape=[sds((t, d),...  93.2 us

profile of v6, /device:TPU:15, one launch (start us, length us, event | category | flops | bytes accessed | tf_op | source)
XLA Modules:
  0.0 348.5 jit_solution(15057650634782741369)
XLA Ops:
  0.7 1.0 copy-done
  1.8 0.8 reshape.148
  2.7 0.8 reshape.150
  3.5 0.6 maximum_convert_fusion.bias_ref
  4.1 0.7 and_select_fusion.1
  4.8 1.5 concatenate.20
  6.4 0.6 pad_convert_fusion.small_ref
  7.0 0.8 reshape.139
  7.7 0.7 reshape.138
  8.4 0.8 constant_dynamic-slice_fusion.3
  9.3 0.7 convert_reduce_fusion
  10.2 0.8 constant_dynamic-slice_fusion
  11.4 0.7 maximum_maximum_fusion.aux_ref
  12.2 0.2 copy.75
  12.4 0.2 copy.74
  12.7 0.7 pad_maximum_fusion.p1_ref
  13.5 0.9 pad.37
  14.4 0.8 reshape.153
  15.2 1.5 dynamic-slice_reduce_fusion
  16.7 0.8 copy.84
  17.4 96.1 %attend.1 = (bf16[4,256,1152]{2,1,0:T(8,128)(2,1)}, bf16[8,128,1024]{2,1,0:T(8,128)(2,1)}, f32[8,16,128]{2,1,0:T(8,128)}, bf16[2,320,1024]{2,1,0:T(8,128)(2,1)},...) custom-call(bf16[256,1024]{1,0:T(8,128)(2,1)} %x_ref.5, ...), custom_call_target="tpu_custom_call" | custom-call | tf_op jit(solution)/shard_map/attend/pallas_call | solution.py:553
  113.6 93.2 %feed.1 = (bf16[256,1024]{1,0:T(8,128)(2,1)}, f32[256,1024]{1,0:T(8,128)}, bf16[640,1024]{1,0:T(8,128)(2,1)}, bf16[4,128,1024]{2,1,0:T(8,128)(2,1)}, bf16[2,128,...) custom-call(bf16[256,1024]{1,0:T(8,128)(2,1)} %x_ref.5, ...), custom_call_target="tpu_custom_call" | custom-call | tf_op jit(solution)/shard_map/feed/pallas_call | solution.py:1026
  206.8 135.3 %back.1 = (f32[256,1024]{1,0:T(8,128)}, bf16[4,128,512]{2,1,0:T(8,128)(2,1)}, bf16[4,128,512]{2,1,0:T(8,128)(2,1)}, bf16[4,128,1024]{2,1,0:T(8,128)(2,1)}, bf16[...) custom-call(bf16[4,256,128]{2,1,0:T(8,128)(2,1)} %get-tuple-element., ...), custom_call_target="tpu_custom_call" | custom-call | tf_op jit(solution)/shard_map/back/pallas_call | solution.py:1468
  342.1 6.3 %unpack.1 = (f32[448,128]{1,0:T(8,128)}, f32[448,128]{1,0:T(8,128)}, f32[448,128]{1,0:T(8,128)}, f32[2240,128]{1,0:T(8,128)}, f32[20,128]{1,0:T(8,128)}, /*index...) custom-call(bf16[4,128,512]{2,1,0:T(8,128)(2,1)} %get-tuple-element., ...), custom_call_target="tpu_custom_call" | custom-call | tf_op jit(solution)/shard_map/unpack/pallas_call | solution.py:1612
  (31 shorter events, 1.2 us)
Async XLA Ops:
  0.7 1.1 copy-start
  7.0 6.5 %copy-start.2 = (bf16[280,1024]{1,0:T(8,128)(2,1)S(1)}, bf16[280,1024]{1,0:T(8,128)(2,1)}, u32[]{:S(2)}) copy-start(bf16[280,1024]{1,0:T(8,128)(2,1)} %param.37) | copy-start | bytes 1720324
  12.1 2.3 copy-start.1
